TPU v7x, 256 devices: a whole 4x4x8 slice. The times are simulated.
256 devices in a mesh: section: 16 (over z, core), dp: 16 (over x, y).
Axes of the slice: x: 4, y: 4, z: 8, core: 2. Of those that a mesh axis runs over, the one named last changes fastest.
Arguments:
- layer_input: bfloat16 [16, 4096, 8192], P('section', 'dp'), may hold values from -6 to 6
- key_cotangent: bfloat16 [16, 4096, 1024], P('section', 'dp'), may hold values from -6 to 6
- key_weight: bfloat16 [16, 8192, 1024], P('section', 'dp'), may hold values from -0.09375 to 0.09375
- block_mask: int32 [16, 128, 16], P('section'), may hold values from 0 to 1, as said below
Outputs:
- key_grad: float32 [16, 8192, 1024], P('section', 'dp')
- input_grad: bfloat16 [16, 4096, 8192], P('section', 'dp')
Inputs may be any that keep to these rules, and one draw needn't show every extreme that they name: `block_mask`: in each layer every aligned group of 8 block rows holds 2, 4 or 6 times 1024 / 64 kept blocks, and some group holds exactly 96.
All inputs are finite; a program needn't handle non-finite values.
Results may differ from a plain program's by a relative error of at most 0.001.
Values may be sent and summed in bfloat16 or wider, within the bound.
No kernel may reach another device: no remote copies, remote signals or barrier semaphores. Data moves between devices by JAX's collectives and lax.ppermute only.
A program may use at most 320 MiB of HBM per device.

v0:
```python
import math

import jax
import jax.numpy as jnp
from jax import lax
from jax.sharding import PartitionSpec as P

BLOCK = 64


def from_behind(value, axis, steps):
    count = lax.axis_size(axis)
    first, last = (max(0, -steps), min(count, count - steps))
    return lax.ppermute(value, axis, [(source, source + steps) for source in range(first, last)])


def expand(flags):
    return jnp.repeat(jnp.repeat(flags, BLOCK, 0), BLOCK, 1)


def shards(layer_input, key_cotangent, key_weight, block_mask):
    inputs = layer_input[0]
    cotangent = key_cotangent[0]
    weight = key_weight[0]
    flags_layer = block_mask[0]
    replicas = lax.axis_size("dp")
    own_index = lax.axis_index("dp")
    row_count = weight.shape[0]
    block_rows = row_count // BLOCK
    own_flags = lax.dynamic_slice_in_dim(flags_layer, own_index * block_rows, block_rows, 0)
    masked = weight * expand(own_flags).astype(weight.dtype)
    layer_grad = lax.dot_general(
        cotangent,
        lax.all_gather(masked, "dp", axis=0, tiled=True),
        (((1,), (1,)), ((), ())),
        preferred_element_type=jnp.float32,
    ).astype(jnp.bfloat16)
    incoming = from_behind(layer_grad, "section", -1)
    grad_scale = 1.0 / math.sqrt(inputs.shape[0] * replicas)
    product = lax.dot_general(
        inputs, cotangent, (((0,), (0,)), ((), ())), preferred_element_type=jnp.float32
    )
    weight_grad = lax.psum_scatter(
        product * expand(flags_layer).astype(jnp.float32) * grad_scale,
        "dp",
        scatter_dimension=0,
        tiled=True,
    )
    return (weight_grad[None], incoming[None])


def solution(mesh):
    placed = (
        P("section", "dp", None),
        P("section", "dp", None),
        P("section", "dp", None),
        P("section", None, None),
    )
    return jax.shard_map(
        shards,
        mesh=mesh,
        in_specs=placed,
        out_specs=(P("section", "dp", None), P("section", "dp", None)),
        check_vma=False,
    )
```

profile of v0, /device:TPU:1, one launch (start us, length us, event | category | flops | bytes accessed | tf_op | source)
XLA Modules:
  0.0 351.5 jit_solution(14776006265439015469)
XLA Ops:
  7.2 0.0 copy-start
  7.2 0.0 all-gather.2.cloned.1.call-start
  7.2 1.5 copy.15
  8.8 0.8 constant_dynamic-slice_fusion
  9.6 0.1 copy.19
  9.6 0.1 copy.17
  9.7 0.1 broadcast_in_dim.21
  9.8 0.1 convert_element_type.40
  9.9 1.1 bitcast_multiply_fusion
  11.0 0.0 all-gather.2.cloned.1.call-update
  11.0 0.0 reduce-scatter.2.cloned.1.call-start
  11.0 0.7 convert_bitcast_fusion
  11.7 0.3 broadcast_in_dim.18
  12.1 0.4 convert_element_type.36
  12.4 11.2 %broadcast_in_dim.19 = f32[8192,16,64]{0,2,1:T(8,128)} broadcast(f32[8192,16]{0,1:T(8,128)S(1)} %convert_element_type.36), dimensions={0,1} | broadcast | bytes 34078720 | tf_op jit(solution)/shard_map/broadcast_in_dim | solution.py:18
  23.7 33.7 %copy.14 = f32[8192,1024]{1,0:T(8,128)} copy(f32[8192,1024]{0,1:T(8,128)} %bitcast.26) | data formatting | bytes 67108864 | tf_op jit(solution)/shard_map/convert_element_type | solution.py:44
  57.4 0.0 copy-done
  57.4 23.1 %multiply_multiply_fusion = f32[8192,1024]{1,0:T(8,128)} fusion(f32[8192,1024]{1,0:T(8,128)} %copy.14, bf16[1,256,8192]{2,1,0:T(8,128)(2,1)} %param.4, bf16[1,256,1024]{2,1,0:T(8,128)(2,1)S(1)} %copy-done), kind=kOutput, calls=%fused_computation | convolution fusion | flops 4311744512 | bytes 71827456 | tf_op jit(solution)/shard_map/dot_general | solution.py:40
  80.5 0.0 reduce-scatter.2.cloned.1.call-update
  80.5 59.6 %all-gather.2.cloned.1.call-done = bf16[8192,1024]{0,1:T(8,128)(2,1)} async-done(((bf16[512,1024]{0,1:T(8,128)(2,1)}), bf16[8192,1024]{0,1:T(8,128)(2,1)}) %all-gather.2.cloned.1.call-update) | async-done | bytes 16777232 | tf_op jit(solution)/shard_map/all_gather | solution.py:34
  140.1 10.6 %fusion = bf16[256,8192]{0,1:T(8,128)(2,1)S(1)} fusion(bf16[8192,1024]{0,1:T(8,128)(2,1)} %all-gather.2.cloned.1.call-done, bf16[1,256,1024]{2,1,0:T(8,128)(2,1)S(1)} %copy-done), kind=kOutput, calls=%fused_computation.2 | convolution fusion | flops 4297064448 | bytes 21495808 | tf_op jit(solution)/shard_map/dot_general | solution.py:32
  150.7 3.5 collective-permute-start
  154.2 47.7 %collective-permute-done = bf16[256,8192]{0,1:T(8,128)(2,1)} collective-permute-done((bf16[256,8192]{0,1:T(8,128)(2,1)S(1)}, bf16[256,8192]{0,1:T(8,128)(2,1)}, u32[]{:S(2)}, u32[]{:S(2)}) %collective-permute-start) | collective-permute-done | bytes 4194336 | tf_op jit(solution)/shard_map/ppermute | solution.py:14
  201.9 6.3 %copy.18 = bf16[1,256,8192]{2,1,0:T(8,128)(2,1)} copy(bf16[1,256,8192]{1,2,0:T(8,128)(2,1)} %bitcast.9) | data formatting | bytes 8388608
  208.2 136.4 %reduce-scatter.2.cloned.1.call-done = f32[512,1024]{1,0:T(8,128)} async-done(((f32[8192,1024]{1,0:T(8,128)}), f32[512,1024]{1,0:T(8,128)}) %reduce-scatter.2.cloned.1.call-update) | async-done | bytes 2097168 | tf_op jit(solution)/shard_map/reduce_scatter | solution.py:43
  (1 shorter events, 0.0 us)
Async XLA Ops:
  7.2 50.2 %copy-start = (bf16[1,256,1024]{2,1,0:T(8,128)(2,1)S(1)}, bf16[1,256,1024]{2,1,0:T(8,128)(2,1)}, u32[]{:S(2)}) copy-start(bf16[1,256,1024]{2,1,0:T(8,128)(2,1)} %param.5) | copy-start | bytes 1572868
  7.2 132.9 %all-gather.2.cloned.1.call-start = ((), (), s32[]{:S(2)}) async-start(), calls=%async_computation.2 | async-start | bytes 17825792 | tf_op jit(solution)/shard_map/all_gather | solution.py:34
  11.0 333.7 %reduce-scatter.2.cloned.1.call-start = ((), (), s32[]{:S(2)}) async-start(), calls=%async_computation.1 | async-start | bytes 35651584 | tf_op jit(solution)/shard_map/reduce_scatter | solution.py:43
  150.7 51.2 %collective-permute-start = (bf16[256,8192]{0,1:T(8,128)(2,1)S(1)}, bf16[256,8192]{0,1:T(8,128)(2,1)}, u32[]{:S(2)}, u32[]{:S(2)}) collective-permute-start(bf16[256,8192]{0,1:T(8,128)(2,1)S(1)} %fusion), channel_id=1, source_target_pairs={{16,0},{32,16},{48,32},{64,48},{80,64},{96,80},{112,96},{128,112},... | collective-permute-start | bytes 12582920 | tf_op jit(solution)/shard_map/ppermute | solution.py:14
Sparse Core Ops, SparseCore 0:
  11.1 128.9 all-gather.1
  144.5 200.0 reduce-scatter.1
where the time goes:
time: 352 us; the launch traced here: 351 us
  waiting for transfers between devices  244 us (69%)
  local copies, waits for them, and re-layouts  54.6 us (16%)
  matrix products  33.6 us (10%)
  between operations  14.1 us (4%)
  starting transfers between devices  3.53 us (1%)
    reduce_scatter x1, waiting for transfers between devices, shards(): lax.psum_scatter(product * expand(flags_layer).astype(jnp.float32) * grad...  136 us
    all_gather x1, waiting for transfers between devices, shards(): lax.all_gather(masked, 'dp', axis=0, tiled=True)  59.6 us
    ppermute x1, waiting for transfers between devices, from_behind(): lax.ppermute(value, axis, [(source, source + steps) for source in range(f...  47.7 us
    convert_element_type x2, local copies, waits for them, and re-layouts, shards(): expand(flags_layer).astype(jnp.float32)  34.1 us
    dot_general x1, matrix products, shards(): lax.dot_general(inputs, cotangent, (((0,), (0,)), ((), ())), preferred_el...  23.1 us
    broadcast_in_dim x3, local copies, waits for them, and re-layouts, expand(): return jnp.repeat(jnp.repeat(flags, BLOCK, 0), BLOCK, 1)  11.6 us
    dot_general x1, matrix products, shards(): lax.dot_general(cotangent, lax.all_gather(masked, 'dp', axis=0, tiled=Tru...  10.6 us
    unnamed x5, local copies, waits for them, and re-layouts  7.97 us
  transfers between devices with their start and end apart: 3, of which 3 were waited for; matrix products, arithmetic and copies ran while one was open for 25% of the time, Pallas kernels for 0%

commit v1 on v0

v1 whole, which is shorter than its diff:
```python
import math

import jax
import jax.numpy as jnp
from jax import lax
from jax.experimental import pallas as pl
from jax.experimental.pallas import tpu as pltpu
from jax.sharding import PartitionSpec as P

BLOCK = 64
SIDE = 4


def along_x(value, steps):
    return lax.ppermute(
        value,
        "dp",
        [
            (x * SIDE + y, (x + steps) % SIDE * SIDE + y)
            for x in range(SIDE)
            for y in range(SIDE)
        ],
    )


def along_y(value, steps):
    return lax.ppermute(
        value,
        "dp",
        [
            (x * SIDE + y, x * SIDE + (y + steps) % SIDE)
            for x in range(SIDE)
            for y in range(SIDE)
        ],
    )


def to_layer_below(value):
    count = lax.axis_size("section")
    return lax.ppermute(value, "section", [(s, s - 1) for s in range(1, count)])


def expand(flags):
    return jnp.repeat(jnp.repeat(flags, BLOCK, 0), BLOCK, 1)


def column_start(place_ref, k, m, half, width):
    x = lax.rem(place_ref[0] + k, SIDE)
    y = lax.rem(place_ref[1] + m, SIDE)
    return pl.multiple_of((x * SIDE + y) * (2 * width) + half * width, width)


def run_copies(copies):
    for copy in copies:
        copy.start()
    for copy in copies:
        copy.wait()


def split_kernel(place_ref, whole_ref, *refs):
    pieces, sems = refs[: 2 * SIDE], refs[2 * SIDE]
    width = pieces[0].shape[1] // SIDE
    copies = []
    for a in range(SIDE):
        for b in range(SIDE):
            for half in range(2):
                k, m = (a, b) if half == 0 else (b, a)
                copies.append(
                    pltpu.make_async_copy(
                        whole_ref.at[:, pl.ds(column_start(place_ref, k, m, half, width), width)],
                        pieces[half * SIDE + a].at[:, pl.ds(b * width, width)],
                        sems.at[len(copies)],
                    )
                )
    run_copies(copies)


def join_kernel(place_ref, *refs):
    pieces, whole_ref, sems = refs[: 2 * SIDE], refs[2 * SIDE], refs[2 * SIDE + 1]
    width = pieces[0].shape[1] // SIDE
    copies = []
    for a in range(SIDE):
        for b in range(SIDE):
            for half in range(2):
                k, m = (a, b) if half == 0 else (b, a)
                copies.append(
                    pltpu.make_async_copy(
                        pieces[half * SIDE + a].at[:, pl.ds(b * width, width)],
                        whole_ref.at[:, pl.ds(column_start(place_ref, k, m, half, width), width)],
                        sems.at[len(copies)],
                    )
                )
    run_copies(copies)


def split_columns(place, whole):
    rows, columns = whole.shape
    piece = jax.ShapeDtypeStruct((rows, columns // (2 * SIDE)), whole.dtype)
    return pl.pallas_call(
        split_kernel,
        out_shape=[piece] * (2 * SIDE),
        in_specs=[pl.BlockSpec(memory_space=pltpu.SMEM), pl.BlockSpec(memory_space=pl.ANY)],
        out_specs=[pl.BlockSpec(memory_space=pl.ANY)] * (2 * SIDE),
        scratch_shapes=[pltpu.SemaphoreType.DMA((2 * SIDE * SIDE,))],
        cost_estimate=pl.CostEstimate(flops=0, bytes_accessed=4 * rows * columns, transcendentals=0),
    )(place, whole)


def join_columns(place, pieces):
    rows, columns = pieces[0].shape
    return pl.pallas_call(
        join_kernel,
        out_shape=jax.ShapeDtypeStruct((rows, columns * 2 * SIDE), pieces[0].dtype),
        in_specs=[pl.BlockSpec(memory_space=pltpu.SMEM)]
        + [pl.BlockSpec(memory_space=pl.ANY)] * (2 * SIDE),
        out_specs=pl.BlockSpec(memory_space=pl.ANY),
        scratch_shapes=[pltpu.SemaphoreType.DMA((2 * SIDE * SIDE,))],
        cost_estimate=pl.CostEstimate(
            flops=0, bytes_accessed=4 * rows * columns * 2 * SIDE, transcendentals=0
        ),
    )(place, *pieces)


def gather_line(move, cotangent, rows):
    tokens = cotangent.shape[0]
    both = jnp.concatenate([cotangent, rows], 0)
    before = move(both, 1)
    after = move(both, -1)
    far_cotangent = move(before[:tokens], 1)
    far_rows = move(after[tokens:], -1)
    return (
        [cotangent, after[:tokens], far_cotangent, before[:tokens]],
        [rows, after[tokens:], far_rows, before[tokens:]],
        before,
    )


def shards(layer_input, key_cotangent, key_weight, block_mask):
    inputs = layer_input[0]
    cotangent = key_cotangent[0]
    weight = key_weight[0]
    flags_layer = block_mask[0]
    own_index = lax.axis_index("dp")
    row_count = weight.shape[0]
    half = row_count // 2
    block_rows = row_count // BLOCK
    place = jnp.stack([own_index // SIDE, own_index % SIDE]).astype(jnp.int32)

    own_flags = lax.dynamic_slice_in_dim(flags_layer, own_index * block_rows, block_rows, 0)
    masked = weight * expand(own_flags).astype(weight.dtype)

    cot_x, rows_x, seen_x = gather_line(along_x, cotangent, masked[half:])
    cot_y, rows_y, seen_y = gather_line(along_y, cotangent, masked[:half])

    inputs, _, _ = lax.optimization_barrier((inputs, seen_x, seen_y))
    pieces = split_columns(place, inputs)
    in_x = [pieces[0]] + [along_x(pieces[-j % SIDE], -j) for j in range(1, SIDE)]
    in_y = [pieces[SIDE]] + [along_y(pieces[SIDE + -j % SIDE], -j) for j in range(1, SIDE)]

    def layer_term(cot, rows):
        rows = jnp.concatenate(rows, 0)
        return [
            lax.dot_general(
                c, rows, (((1,), (1,)), ((), ())), preferred_element_type=jnp.float32
            ).astype(jnp.bfloat16)
            for c in cot
        ]

    out_x = layer_term(cot_x, rows_y)
    out_y = layer_term(cot_y, rows_x)
    grad_x = [out_x[0]] + [along_x(out_x[-j % SIDE], -j) for j in range(1, SIDE)]
    grad_y = [out_y[0]] + [along_y(out_y[-j % SIDE], -j) for j in range(1, SIDE)]
    incoming = [to_layer_below(piece) for piece in grad_x + grad_y]
    input_grad = join_columns(place, incoming)

    def weight_term(ins, cot):
        ins = jnp.concatenate(ins, 0)
        cot = jnp.concatenate(cot, 0)
        return [
            lax.dot_general(
                ins[:, half * m : half * (m + 1)],
                cot,
                (((0,), (0,)), ((), ())),
                preferred_element_type=jnp.float32,
            )
            for m in range(SIDE)
        ]

    part_x = weight_term(in_x, cot_x)
    part_y = weight_term(in_y, cot_y)
    top = part_x[0] + sum(along_y(part_x[-j % SIDE], -j) for j in range(1, SIDE))
    bottom = part_y[0] + sum(along_x(part_y[-j % SIDE], -j) for j in range(1, SIDE))
    grad_scale = 1.0 / math.sqrt(cotangent.shape[0] * lax.axis_size("dp"))
    weight_grad = jnp.concatenate([top, bottom], 0) * (
        expand(own_flags).astype(jnp.float32) * grad_scale
    )
    return (weight_grad[None], input_grad[None])


def solution(mesh):
    placed = (
        P("section", "dp", None),
        P("section", "dp", None),
        P("section", "dp", None),
        P("section", None, None),
    )
    return jax.shard_map(
        shards,
        mesh=mesh,
        in_specs=placed,
        out_specs=(P("section", "dp", None), P("section", "dp", None)),
        check_vma=False,
    )
```

time: 352 us -> 457 us (1.30)
  Pallas kernels: 0 us -> 258 us
  waiting for transfers between devices: 244 us -> 75 us
  starting transfers between devices: 3.53 us -> 60.3 us
  local copies, waits for them, and re-layouts: 54.6 us -> 18.8 us
  between operations: 14.1 us -> 1.53 us
  matrix products: 33.6 us -> 38.4 us
    pallas_call x0 -> x2, Pallas kernels: none -> 258 us  [the longest x1 129 us: join_columns(): pl.pallas_call(join_kernel, out_shape=jax.ShapeDtypeStruct((rows, columns...]
    reduce_scatter x1 -> x0, waiting for transfers between devices: 136 us -> none  [shards(): lax.psum_scatter(product * expand(flags_layer).astype(jnp.float32) * grad...]
    all_gather x1 -> x0, waiting for transfers between devices: 59.6 us -> none  [shards(): lax.all_gather(masked, 'dp', axis=0, tiled=True)]
    ppermute x1 -> x34, starting transfers between devices: 3.45 us -> 60.3 us  [the longest x8 26.5 us: to_layer_below(): return lax.ppermute(value, 'section', [(s, s - 1) for s in range(1, count)])]
    convert_element_type x2 -> x0, local copies, waits for them, and re-layouts: 34.1 us -> none  [shards(): expand(flags_layer).astype(jnp.float32)]
    ppermute x1 -> x34, waiting for transfers between devices: 47.7 us -> 75 us  [the longest x13 34.8 us: along_x(): lax.ppermute(value, 'dp', [(x * SIDE + y, (x + steps) % SIDE * SIDE + y)...]
    broadcast_in_dim x3, local copies, waits for them, and re-layouts: 11.6 us -> 1.75 us  [expand(): return jnp.repeat(jnp.repeat(flags, BLOCK, 0), BLOCK, 1)]
    slice x0 -> x5, local copies, waits for them, and re-layouts: none -> 8.92 us  [the longest x2 4.49 us: gather_line(): before[tokens:]]
  transfers between devices with their start and end apart: 3 -> 34, of which waited for: 3 -> 10; matrix products, arithmetic and copies ran while one was open for 25% -> 12% of each run, Pallas kernels for 0% -> 28%
where the time goes in v1:
time: 457 us; the launch traced here: 456 us
  Pallas kernels  258 us (56%)
  waiting for transfers between devices  75 us (16%)
  starting transfers between devices  60.3 us (13%)
  matrix products  38.4 us (8%)
  local copies, waits for them, and re-layouts  18.8 us (4%)
    pallas_call x1, Pallas kernels, join_columns(): pl.pallas_call(join_kernel, out_shape=jax.ShapeDtypeStruct((rows, columns...  129 us
    pallas_call x1, Pallas kernels, split_columns(): pl.pallas_call(split_kernel, out_shape=[piece] * (2 * SIDE), in_specs=[pl...  129 us
    ppermute x13, waiting for transfers between devices, along_x(): lax.ppermute(value, 'dp', [(x * SIDE + y, (x + steps) % SIDE * SIDE + y)...  34.8 us
    ppermute x13, waiting for transfers between devices, along_y(): lax.ppermute(value, 'dp', [(x * SIDE + y, x * SIDE + (y + steps) % SIDE)...  31.4 us
    ppermute x8, starting transfers between devices, to_layer_below(): return lax.ppermute(value, 'section', [(s, s - 1) for s in range(1, count)])  26.5 us
    dot_general x8, matrix products, weight_term(): lax.dot_general(ins[:, half * m:half * (m + 1)], cot, (((0,), (0,)), ((),...  23 us
    ppermute x13, starting transfers between devices, along_y(): lax.ppermute(value, 'dp', [(x * SIDE + y, x * SIDE + (y + steps) % SIDE)...  17.4 us
    ppermute x13, starting transfers between devices, along_x(): lax.ppermute(value, 'dp', [(x * SIDE + y, (x + steps) % SIDE * SIDE + y)...  16.4 us
  transfers between devices with their start and end apart: 34, of which 10 were waited for; matrix products, arithmetic and copies ran while one was open for 12% of the time, Pallas kernels for 28%

profile of v1, /device:TPU:1, one launch (start us, length us, event | category | flops | bytes accessed | tf_op | source)
XLA Modules:
  0.0 456.0 jit_solution(3794148015179252567)
XLA Ops:
  7.7 2.7 collective-permute-start.13
  12.5 17.1 %collective-permute-done = bf16[512,1024]{0,1:T(8,128)(2,1)} collective-permute-done((bf16[512,1024]{0,1:T(8,128)(2,1)S(1)}, bf16[512,1024]{0,1:T(8,128)(2,1)}, u32[]{:S(2)}, u32[]{:S(2)}) %collective-permute-start) | collective-permute-done | bytes 1048608 | tf_op jit(solution)/shard_map/ppermute | solution.py:15
  29.6 2.2 fusion.37
  33.8 2.3 fusion.38
  36.0 3.0 collective-permute-start.18
  39.1 2.3 fusion.39
  43.4 2.7 collective-permute-start.26
  46.1 129.1 %shard_map.59 = (bf16[256,1024]{1,0:T(8,128)(2,1)}, bf16[256,1024]{1,0:T(8,128)(2,1)}, bf16[256,1024]{1,0:T(8,128)(2,1)}, bf16[256,1024]{1,0:T(8,128)(2,1)}, bf1...) custom-call(s32[2]{0:T(128)} %pad_add_fusion.place_ref, ...), custom_call_target="tpu_custom_call" | custom-call | bytes 8388608 | tf_op jit(solution)/shard_map/pallas_call | solution.py:99
  180.4 2.2 convolution_convert_fusion.7
  182.6 2.8 collective-permute-start.10
  191.1 3.6 collective-permute-start.22
  196.5 9.9 %collective-permute-done.4 = bf16[256,1024]{1,0:T(8,128)(2,1)S(1)} collective-permute-done((bf16[256,1024]{1,0:T(8,128)(2,1)S(1)}, bf16[256,1024]{1,0:T(8,128)(2,1)S(1)}, u32[]{:S(2)}, u32[]{:S(2)}) %collective-permute-start.4) | collective-permute-done | bytes 524320 | tf_op jit(solution)/shard_map/ppermute | solution.py:15
  208.4 2.7 fusion.17
  219.8 3.7 fusion.10
  223.5 2.4 collective-permute-start.8
  227.9 9.4 %collective-permute-start.19 = (bf16[256,1024]{1,0:T(8,128)(2,1)S(1)}, bf16[256,1024]{1,0:T(8,128)(2,1)S(1)}, u32[]{:S(2)}, u32[]{:S(2)}) collective-permute-start(bf16[256,1024]{1,0:T(8,128)(2,1)S(1)} %fusion.6), channel_id=1, source_target_pairs={{16,0},{32,16},{48,32},{64,48},{80,64},{96,80},{112,96},{128,112},... | collective-permute-start | bytes 1572872 | tf_op jit(solution)/shard_map/ppermute | solution.py:40
  237.3 2.2 collective-permute-start.7
  240.1 3.0 fusion.12
  243.1 3.0 fusion.8
  246.2 15.1 %collective-permute-done.32 = bf16[256,1024]{1,0:T(8,128)(2,1)S(1)} collective-permute-done((bf16[256,1024]{1,0:T(8,128)(2,1)S(1)}, bf16[256,1024]{1,0:T(8,128)(2,1)S(1)}, u32[]{:S(2)}, u32[]{:S(2)}) %collective-permute-start.32) | collective-permute-done | bytes 524320 | tf_op jit(solution)/shard_map/ppermute | solution.py:27
  264.4 13.3 %collective-permute-done.7 = f32[256,1024]{1,0:T(8,128)S(1)} collective-permute-done((f32[256,1024]{1,0:T(8,128)S(1)}, f32[256,1024]{1,0:T(8,128)S(1)}, u32[]{:S(2)}, u32[]{:S(2)}) %collective-permute-start.7) | collective-permute-done | bytes 1048608 | tf_op jit(solution)/shard_map/ppermute | solution.py:27
  277.7 3.2 collective-permute-start.27
  280.9 2.9 collective-permute-done.9
  283.9 2.3 collective-permute-start.23
  290.0 3.4 fusion.5
  299.4 7.2 %collective-permute-done.15 = f32[256,1024]{1,0:T(8,128)} collective-permute-done((f32[256,1024]{1,0:T(8,128)}, f32[256,1024]{1,0:T(8,128)}, u32[]{:S(2)}, u32[]{:S(2)}) %collective-permute-start.15) | collective-permute-done | bytes 1048608 | tf_op jit(solution)/shard_map/ppermute | solution.py:15
  306.7 3.5 collective-permute-start.29
  310.7 2.4 collective-permute-start.33
  313.1 3.1 fusion.4
  318.0 2.9 collective-permute-done.29.refs_5_
  320.9 5.6 %collective-permute-done.33.refs_7_ = bf16[256,1024]{1,0:T(8,128)(2,1)} collective-permute-done((bf16[256,1024]{1,0:T(8,128)(2,1)S(1)}, bf16[256,1024]{1,0:T(8,128)(2,1)}, u32[]{:S(2)}, u32[]{:S(2)}) %collective-permute-start.33) | collective-permute-done | bytes 524320 | tf_op jit(solution)/shard_map/ppermute | solution.py:40
  326.5 129.2 %shard_map.60 = bf16[256,8192]{1,0:T(8,128)(2,1)} custom-call(s32[2]{0:T(128)} %pad_add_fusion.place_ref, bf16[256,1024]{1,0:T(8,128)(2,1)} %copy-done.2, bf16[256,1024]{1,0:T(8,128)(2,1)} %collective-permute-done.21.refs_1_, bf16[256,1024]{1,0:T(8,128)(2,1)} %collective-permute-done.23.refs_2_, bf16[256,1024]{1,0:T(8,128)(2,1)} %collective-permute-done.25.refs_3_, ...), custom_call_target="tpu_custom_call" | custom-call | bytes 8388608 | tf_op jit(solution)/shard_map/pallas_call | solution.py:111
  (146 shorter events, 53.8 us)
Async XLA Ops:
  5.6 24.0 %collective-permute-start = (bf16[512,1024]{0,1:T(8,128)(2,1)S(1)}, bf16[512,1024]{0,1:T(8,128)(2,1)}, u32[]{:S(2)}, u32[]{:S(2)}) collective-permute-start(bf16[512,1024]{0,1:T(8,128)(2,1)S(1)} %get-tuple-element.31), channel_id=1, source_target_pairs={{0,4},{1,5},{2,6},{3,7},{4,8},{5,9},{6,10},{7,11},{8,12},{9,13},{1... | collective-permute-start | bytes 3145736 | tf_op jit(solution)/shard_map/ppermute | solution.py:15
  7.7 26.1 %collective-permute-start.13 = (bf16[512,1024]{0,1:T(8,128)(2,1)}, bf16[512,1024]{0,1:T(8,128)(2,1)}, u32[]{:S(2)}, u32[]{:S(2)}) collective-permute-start(bf16[512,1024]{0,1:T(8,128)(2,1)} %get-tuple-element.30), channel_id=1, source_target_pairs={{0,3},{1,0},{2,1},{3,2},{4,7},{5,4},{6,5},{7,6},{8,11},{9,8},{10,9... | collective-permute-start | bytes 3145736 | tf_op jit(solution)/shard_map/ppermute | solution.py:27
  10.4 28.7 %collective-permute-start.1 = (bf16[512,1024]{0,1:T(8,128)(2,1)}, bf16[512,1024]{0,1:T(8,128)(2,1)}, u32[]{:S(2)}, u32[]{:S(2)}) collective-permute-start(bf16[512,1024]{0,1:T(8,128)(2,1)} %get-tuple-element.30), channel_id=1, source_target_pairs={{0,1},{1,2},{2,3},{3,0},{4,5},{5,6},{6,7},{7,4},{8,9},{9,10},{10,1... | collective-permute-start | bytes 3145736 | tf_op jit(solution)/shard_map/ppermute | solution.py:27
  10.4 30.9 %collective-permute-start.5 = (bf16[512,1024]{0,1:T(8,128)(2,1)S(1)}, bf16[512,1024]{0,1:T(8,128)(2,1)}, u32[]{:S(2)}, u32[]{:S(2)}) collective-permute-start(bf16[512,1024]{0,1:T(8,128)(2,1)S(1)} %get-tuple-element.31), channel_id=1, source_target_pairs={{0,12},{1,13},{2,14},{3,15},{4,0},{5,1},{6,2},{7,3},{8,4},{9,5},{1... | collective-permute-start | bytes 3145736 | tf_op jit(solution)/shard_map/ppermute | solution.py:15
  31.9 144.9 %collective-permute-start.6 = (bf16[256,1024]{0,1:T(8,128)(2,1)}, bf16[256,1024]{0,1:T(8,128)(2,1)}, u32[]{:S(2)}, u32[]{:S(2)}) collective-permute-start(bf16[256,1024]{0,1:T(8,128)(2,1)} %get-tuple-element.23), channel_id=1, source_target_pairs={{0,4},{1,5},{2,6},{3,7},{4,8},{5,9},{6,10},{7,11},{8,12},{9,13},{1... | collective-permute-start | bytes 1572872 | tf_op jit(solution)/shard_map/ppermute | solution.py:15
  36.0 141.4 %collective-permute-start.18 = (bf16[256,1024]{0,1:T(8,128)(2,1)}, bf16[256,1024]{0,1:T(8,128)(2,1)}, u32[]{:S(2)}, u32[]{:S(2)}) collective-permute-start(bf16[256,1024]{0,1:T(8,128)(2,1)} %get-tuple-element.24), channel_id=1, source_target_pairs={{0,3},{1,0},{2,1},{3,2},{4,7},{5,4},{6,5},{7,6},{8,11},{9,8},{10,9... | collective-permute-start | bytes 1572872 | tf_op jit(solution)/shard_map/ppermute | solution.py:27
  41.3 141.3 %collective-permute-start.14 = (bf16[256,1024]{0,1:T(8,128)(2,1)}, bf16[256,1024]{0,1:T(8,128)(2,1)}, u32[]{:S(2)}, u32[]{:S(2)}) collective-permute-start(bf16[256,1024]{0,1:T(8,128)(2,1)} %get-tuple-element.27), channel_id=1, source_target_pairs={{0,1},{1,2},{2,3},{3,0},{4,5},{5,6},{6,7},{7,4},{8,9},{9,10},{10,1... | collective-permute-start | bytes 1572872 | tf_op jit(solution)/shard_map/ppermute | solution.py:27
  43.4 142.0 %collective-permute-start.26 = (bf16[256,1024]{0,1:T(8,128)(2,1)S(1)}, bf16[256,1024]{0,1:T(8,128)(2,1)S(1)}, u32[]{:S(2)}, u32[]{:S(2)}) collective-permute-start(bf16[256,1024]{0,1:T(8,128)(2,1)S(1)} %get-tuple-element.20), channel_id=1, source_target_pairs={{0,12},{1,13},{2,14},{3,15},{4,0},{5,1},{6,2},{7,3},{8,4},{9,5},{1... | collective-permute-start | bytes 1572872 | tf_op jit(solution)/shard_map/ppermute | solution.py:15
  175.3 15.1 %collective-permute-start.2 = (bf16[256,1024]{1,0:T(8,128)(2,1)}, bf16[256,1024]{1,0:T(8,128)(2,1)S(1)}, u32[]{:S(2)}, u32[]{:S(2)}) collective-permute-start(bf16[256,1024]{1,0:T(8,128)(2,1)} %get-tuple-element.13), channel_id=1, source_target_pairs={{0,12},{1,13},{2,14},{3,15},{4,0},{5,1},{6,2},{7,3},{8,4},{9,5},{1... | collective-permute-start | bytes 1572872 | tf_op jit(solution)/shard_map/ppermute | solution.py:15
  176.8 14.3 %collective-permute-start.3 = (bf16[256,1024]{1,0:T(8,128)(2,1)S(1)}, bf16[256,1024]{1,0:T(8,128)(2,1)S(1)}, u32[]{:S(2)}, u32[]{:S(2)}) collective-permute-start(bf16[256,1024]{1,0:T(8,128)(2,1)S(1)} %copy-done.30), channel_id=1, source_target_pairs={{0,8},{1,9},{2,10},{3,11},{4,12},{5,13},{6,14},{7,15},{8,0},{9,1},... | collective-permute-start | bytes 1572872 | tf_op jit(solution)/shard_map/ppermute | solution.py:15
  177.4 29.0 %collective-permute-start.4 = (bf16[256,1024]{1,0:T(8,128)(2,1)S(1)}, bf16[256,1024]{1,0:T(8,128)(2,1)S(1)}, u32[]{:S(2)}, u32[]{:S(2)}) collective-permute-start(bf16[256,1024]{1,0:T(8,128)(2,1)S(1)} %copy-done.29), channel_id=1, source_target_pairs={{0,4},{1,5},{2,6},{3,7},{4,8},{5,9},{6,10},{7,11},{8,12},{9,13},{1... | collective-permute-start | bytes 1572872 | tf_op jit(solution)/shard_map/ppermute | solution.py:15
  182.6 32.4 %collective-permute-start.10 = (bf16[256,1024]{1,0:T(8,128)(2,1)S(1)}, bf16[256,1024]{1,0:T(8,128)(2,1)S(1)}, u32[]{:S(2)}, u32[]{:S(2)}) collective-permute-start(bf16[256,1024]{1,0:T(8,128)(2,1)S(1)} %copy-done.28), channel_id=1, source_target_pairs={{0,3},{1,0},{2,1},{3,2},{4,7},{5,4},{6,5},{7,6},{8,11},{9,8},{10,9... | collective-permute-start | bytes 1572872 | tf_op jit(solution)/shard_map/ppermute | solution.py:27
  186.2 30.8 %collective-permute-start.11 = (bf16[256,1024]{1,0:T(8,128)(2,1)S(1)}, bf16[256,1024]{1,0:T(8,128)(2,1)S(1)}, u32[]{:S(2)}, u32[]{:S(2)}) collective-permute-start(bf16[256,1024]{1,0:T(8,128)(2,1)S(1)} %copy-done.27), channel_id=1, source_target_pairs={{0,2},{1,3},{2,0},{3,1},{4,6},{5,7},{6,4},{7,5},{8,10},{9,11},{10,... | collective-permute-start | bytes 1572872 | tf_op jit(solution)/shard_map/ppermute | solution.py:27
  190.4 28.2 %collective-permute-start.12 = (bf16[256,1024]{1,0:T(8,128)(2,1)S(1)}, bf16[256,1024]{1,0:T(8,128)(2,1)S(1)}, u32[]{:S(2)}, u32[]{:S(2)}) collective-permute-start(bf16[256,1024]{1,0:T(8,128)(2,1)S(1)} %copy-done.26), channel_id=1, source_target_pairs={{0,1},{1,2},{2,3},{3,0},{4,5},{5,6},{6,7},{7,4},{8,9},{9,10},{10,1... | collective-permute-start | bytes 1572872 | tf_op jit(solution)/shard_map/ppermute | solution.py:27
  191.1 32.4 %collective-permute-start.22 = (bf16[256,1024]{1,0:T(8,128)(2,1)S(1)}, bf16[256,1024]{1,0:T(8,128)(2,1)}, u32[]{:S(2)}, u32[]{:S(2)}) collective-permute-start(bf16[256,1024]{1,0:T(8,128)(2,1)S(1)} %convolution_convert_fusion.6), channel_id=1, source_target_pairs={{0,8},{1,9},{2,10},{3,11},{4,12},{5,13},{6,14},{7,15},{8,0},{9,1},... | collective-permute-start | bytes 1572872 | tf_op jit(solution)/shard_map/ppermute | solution.py:15
  206.4 21.4 %collective-permute-start.30 = (bf16[256,1024]{1,0:T(8,128)(2,1)S(1)}, bf16[256,1024]{1,0:T(8,128)(2,1)S(1)}, u32[]{:S(2)}, u32[]{:S(2)}) collective-permute-start(bf16[256,1024]{1,0:T(8,128)(2,1)S(1)} %convolution_convert_fusion.3), channel_id=1, source_target_pairs={{0,2},{1,3},{2,0},{3,1},{4,6},{5,7},{6,4},{7,5},{8,10},{9,11},{10,... | collective-permute-start | bytes 1572872 | tf_op jit(solution)/shard_map/ppermute | solution.py:27
  217.0 20.3 %collective-permute-start.24 = (bf16[256,1024]{1,0:T(8,128)(2,1)S(1)}, bf16[256,1024]{1,0:T(8,128)(2,1)}, u32[]{:S(2)}, u32[]{:S(2)}) collective-permute-start(bf16[256,1024]{1,0:T(8,128)(2,1)S(1)} %convolution_convert_fusion.5), channel_id=1, source_target_pairs={{0,4},{1,5},{2,6},{3,7},{4,8},{5,9},{6,10},{7,11},{8,12},{9,13},{1... | collective-permute-start | bytes 1572872 | tf_op jit(solution)/shard_map/ppermute | solution.py:15
  218.6 20.9 %collective-permute-start.28 = (bf16[256,1024]{1,0:T(8,128)(2,1)S(1)}, bf16[256,1024]{1,0:T(8,128)(2,1)}, u32[]{:S(2)}, u32[]{:S(2)}) collective-permute-start(bf16[256,1024]{1,0:T(8,128)(2,1)S(1)} %convolution_convert_fusion.4), channel_id=1, source_target_pairs={{0,3},{1,0},{2,1},{3,2},{4,7},{5,4},{6,5},{7,6},{8,11},{9,8},{10,9... | collective-permute-start | bytes 1572872 | tf_op jit(solution)/shard_map/ppermute | solution.py:27
  223.5 39.0 %collective-permute-start.8 = (f32[256,1024]{1,0:T(8,128)S(1)}, f32[256,1024]{1,0:T(8,128)S(1)}, u32[]{:S(2)}, u32[]{:S(2)}) collective-permute-start(f32[256,1024]{1,0:T(8,128)S(1)} %fusion.17), channel_id=1, source_target_pairs={{0,2},{1,3},{2,0},{3,1},{4,6},{5,7},{6,4},{7,5},{8,10},{9,11},{10,... | collective-permute-start | bytes 3145736 | tf_op jit(solution)/shard_map/ppermute | solution.py:27
  227.8 33.5 %collective-permute-start.32 = (bf16[256,1024]{1,0:T(8,128)(2,1)S(1)}, bf16[256,1024]{1,0:T(8,128)(2,1)S(1)}, u32[]{:S(2)}, u32[]{:S(2)}) collective-permute-start(bf16[256,1024]{1,0:T(8,128)(2,1)S(1)} %convolution_convert_fusion.2), channel_id=1, source_target_pairs={{0,1},{1,2},{2,3},{3,0},{4,5},{5,6},{6,7},{7,4},{8,9},{9,10},{10,1... | collective-permute-start | bytes 1572872 | tf_op jit(solution)/shard_map/ppermute | solution.py:27
  227.9 33.4 %collective-permute-start.19 = (bf16[256,1024]{1,0:T(8,128)(2,1)S(1)}, bf16[256,1024]{1,0:T(8,128)(2,1)S(1)}, u32[]{:S(2)}, u32[]{:S(2)}) collective-permute-start(bf16[256,1024]{1,0:T(8,128)(2,1)S(1)} %fusion.6), channel_id=1, source_target_pairs={{16,0},{32,16},{48,32},{64,48},{80,64},{96,80},{112,96},{128,112},... | collective-permute-start | bytes 1572872 | tf_op jit(solution)/shard_map/ppermute | solution.py:40
  237.3 40.4 %collective-permute-start.7 = (f32[256,1024]{1,0:T(8,128)S(1)}, f32[256,1024]{1,0:T(8,128)S(1)}, u32[]{:S(2)}, u32[]{:S(2)}) collective-permute-start(f32[256,1024]{1,0:T(8,128)S(1)} %fusion.19), channel_id=1, source_target_pairs={{0,3},{1,0},{2,1},{3,2},{4,7},{5,4},{6,5},{7,6},{8,11},{9,8},{10,9... | collective-permute-start | bytes 3145736 | tf_op jit(solution)/shard_map/ppermute | solution.py:27
  239.5 44.4 %collective-permute-start.9 = (f32[256,1024]{1,0:T(8,128)S(1)}, f32[256,1024]{1,0:T(8,128)S(1)}, u32[]{:S(2)}, u32[]{:S(2)}) collective-permute-start(f32[256,1024]{1,0:T(8,128)S(1)} %fusion.15), channel_id=1, source_target_pairs={{0,1},{1,2},{2,3},{3,0},{4,5},{5,6},{6,7},{7,4},{8,9},{9,10},{10,1... | collective-permute-start | bytes 3145736 | tf_op jit(solution)/shard_map/ppermute | solution.py:27
  261.3 36.2 %collective-permute-start.16 = (f32[256,1024]{1,0:T(8,128)}, f32[256,1024]{1,0:T(8,128)}, u32[]{:S(2)}, u32[]{:S(2)}) collective-permute-start(f32[256,1024]{1,0:T(8,128)} %fusion.10), channel_id=1, source_target_pairs={{0,8},{1,9},{2,10},{3,11},{4,12},{5,13},{6,14},{7,15},{8,0},{9,1},... | collective-permute-start | bytes 3145736 | tf_op jit(solution)/shard_map/ppermute | solution.py:15
  261.3 45.3 %collective-permute-start.15 = (f32[256,1024]{1,0:T(8,128)}, f32[256,1024]{1,0:T(8,128)}, u32[]{:S(2)}, u32[]{:S(2)}) collective-permute-start(f32[256,1024]{1,0:T(8,128)} %fusion.12), channel_id=1, source_target_pairs={{0,12},{1,13},{2,14},{3,15},{4,0},{5,1},{6,2},{7,3},{8,4},{9,5},{1... | collective-permute-start | bytes 3145736 | tf_op jit(solution)/shard_map/ppermute | solution.py:15
  262.5 48.1 %collective-permute-start.17 = (f32[256,1024]{1,0:T(8,128)}, f32[256,1024]{1,0:T(8,128)}, u32[]{:S(2)}, u32[]{:S(2)}) collective-permute-start(f32[256,1024]{1,0:T(8,128)} %fusion.8), channel_id=1, source_target_pairs={{0,4},{1,5},{2,6},{3,7},{4,8},{5,9},{6,10},{7,11},{8,12},{9,13},{1... | collective-permute-start | bytes 3145736 | tf_op jit(solution)/shard_map/ppermute | solution.py:15
  277.7 15.7 %collective-permute-start.27 = (bf16[256,1024]{1,0:T(8,128)(2,1)}, bf16[256,1024]{1,0:T(8,128)(2,1)S(1)}, u32[]{:S(2)}, u32[]{:S(2)}) collective-permute-start(bf16[256,1024]{1,0:T(8,128)(2,1)} %fusion.7), channel_id=1, source_target_pairs={{16,0},{32,16},{48,32},{64,48},{80,64},{96,80},{112,96},{128,112},... | collective-permute-start | bytes 1572872 | tf_op jit(solution)/shard_map/ppermute | solution.py:40
  293.5 24.5 %collective-permute-start.31 = (bf16[256,1024]{1,0:T(8,128)(2,1)S(1)}, bf16[256,1024]{1,0:T(8,128)(2,1)}, u32[]{:S(2)}, u32[]{:S(2)}) collective-permute-start(bf16[256,1024]{1,0:T(8,128)(2,1)S(1)} %copy-done.19), channel_id=1, source_target_pairs={{16,0},{32,16},{48,32},{64,48},{80,64},{96,80},{112,96},{128,112},... | collective-permute-start | bytes 1572872 | tf_op jit(solution)/shard_map/ppermute | solution.py:40
  295.5 22.4 %collective-permute-start.21 = (bf16[256,1024]{1,0:T(8,128)(2,1)S(1)}, bf16[256,1024]{1,0:T(8,128)(2,1)}, u32[]{:S(2)}, u32[]{:S(2)}) collective-permute-start(bf16[256,1024]{1,0:T(8,128)(2,1)S(1)} %copy-done.23), channel_id=1, source_target_pairs={{16,0},{32,16},{48,32},{64,48},{80,64},{96,80},{112,96},{128,112},... | collective-permute-start | bytes 1572872 | tf_op jit(solution)/shard_map/ppermute | solution.py:40
  297.5 20.5 %collective-permute-start.25 = (bf16[256,1024]{1,0:T(8,128)(2,1)}, bf16[256,1024]{1,0:T(8,128)(2,1)}, u32[]{:S(2)}, u32[]{:S(2)}) collective-permute-start(bf16[256,1024]{1,0:T(8,128)(2,1)} %collective-permute-done.24), channel_id=1, source_target_pairs={{16,0},{32,16},{48,32},{64,48},{80,64},{96,80},{112,96},{128,112},... | collective-permute-start | bytes 1572872 | tf_op jit(solution)/shard_map/ppermute | solution.py:40
  306.7 14.3 %collective-permute-start.29 = (bf16[256,1024]{1,0:T(8,128)(2,1)}, bf16[256,1024]{1,0:T(8,128)(2,1)}, u32[]{:S(2)}, u32[]{:S(2)}) collective-permute-start(bf16[256,1024]{1,0:T(8,128)(2,1)} %collective-permute-done.28), channel_id=1, source_target_pairs={{16,0},{32,16},{48,32},{64,48},{80,64},{96,80},{112,96},{128,112},... | collective-permute-start | bytes 1572872 | tf_op jit(solution)/shard_map/ppermute | solution.py:40
  310.7 15.9 %collective-permute-start.33 = (bf16[256,1024]{1,0:T(8,128)(2,1)S(1)}, bf16[256,1024]{1,0:T(8,128)(2,1)}, u32[]{:S(2)}, u32[]{:S(2)}) collective-permute-start(bf16[256,1024]{1,0:T(8,128)(2,1)S(1)} %copy-done.25), channel_id=1, source_target_pairs={{16,0},{32,16},{48,32},{64,48},{80,64},{96,80},{112,96},{128,112},... | collective-permute-start | bytes 1572872 | tf_op jit(solution)/shard_map/ppermute | solution.py:40
  (33 other events, 543.5 us)

commit v2 on v0

v2 whole, which is shorter than its diff:
```python
import math

import jax
import jax.numpy as jnp
from jax import lax
from jax.experimental import pallas as pl
from jax.experimental.pallas import tpu as pltpu
from jax.sharding import PartitionSpec as P

BLOCK = 64
SIDE = 4
TAIL = 8


def on_axis(index, parity, first, steps):
    x, y = index // SIDE, index % SIDE
    if (parity == 0) == first:
        x = (x + steps) % SIDE
    else:
        y = (y + steps) % SIDE
    return x * SIDE + y


def move(value, first, steps):
    sections, replicas = lax.axis_size("section"), lax.axis_size("dp")
    pairs = [
        (s * replicas + i, s * replicas + on_axis(i, s % 2, first, steps))
        for s in range(sections)
        for i in range(replicas)
    ]
    return lax.ppermute(value, ("section", "dp"), pairs)


def to_layer_below(value):
    count = lax.axis_size("section")
    return lax.ppermute(value, "section", [(s, s - 1) for s in range(1, count)])


def expand(flags):
    return jnp.repeat(jnp.repeat(flags, BLOCK, 0), BLOCK, 1)


def column_start(place_ref, k, m, width):
    a = lax.rem(place_ref[1] + k, SIDE)
    b = lax.rem(place_ref[2] + m, SIDE)
    owner = jnp.where(place_ref[0] == 0, a * SIDE + b, b * SIDE + a)
    return pl.multiple_of(owner * width, width)


def split_kernel(place_ref, whole_ref, *pieces):
    width = pieces[0].shape[1] // SIDE
    for k in range(SIDE):
        for m in range(SIDE):
            start = column_start(place_ref, k, m, width)
            pieces[k][:, m * width : (m + 1) * width] = whole_ref[:, pl.ds(start, width)]


def join_kernel(place_ref, *refs):
    pieces, whole_ref = refs[:SIDE], refs[SIDE]
    width = pieces[0].shape[1] // SIDE
    for k in range(SIDE):
        for m in range(SIDE):
            start = column_start(place_ref, k, m, width)
            whole_ref[:, pl.ds(start, width)] = pieces[k][:, m * width : (m + 1) * width]


def layer_kernel(*refs):
    cots, rows, outs = refs[:SIDE], refs[SIDE : 2 * SIDE], refs[2 * SIDE :]
    width = rows[0].shape[0]
    for m in range(SIDE):
        for j in range(SIDE):
            outs[j][:, m * width : (m + 1) * width] = lax.dot_general(
                cots[j][...],
                rows[m][...],
                (((1,), (1,)), ((), ())),
                preferred_element_type=jnp.float32,
            ).astype(jnp.bfloat16)


def weight_kernel(*refs):
    ins, cots = refs[:SIDE], refs[SIDE : 2 * SIDE]
    outs, exponent_ref = refs[2 * SIDE : 3 * SIDE], refs[3 * SIDE]
    width = outs[0].shape[0]
    cot = jnp.concatenate([c[...] for c in cots], 0)
    for m in range(SIDE):
        part = lax.dot_general(
            jnp.concatenate([i[:, m * width : (m + 1) * width] for i in ins], 0),
            cot,
            (((0,), (0,)), ((), ())),
            preferred_element_type=jnp.float32,
        )
        outs[m][...] = part
        if m > 0:
            peak = jnp.max(jnp.abs(part), axis=0, keepdims=True)
            peak = jnp.max(peak, axis=1, keepdims=True)
            exponent = jnp.clip(jnp.floor(14.0 - jnp.log2(peak)), -100.0, 100.0)
            exponent_ref[m - 1 : m, :] = jnp.broadcast_to(exponent, (1, exponent_ref.shape[1]))


def local_call(kernel, out_shape, operands, scalars=0, flops=0):
    shapes = list(operands) + list(out_shape)
    moved = sum(math.prod(a.shape) * a.dtype.itemsize for a in shapes)
    vmem = pl.BlockSpec(memory_space=pltpu.VMEM)
    return pl.pallas_call(
        kernel,
        out_shape=out_shape,
        in_specs=[pl.BlockSpec(memory_space=pltpu.SMEM)] * scalars
        + [vmem] * (len(operands) - scalars),
        out_specs=[vmem] * len(out_shape),
        compiler_params=pltpu.CompilerParams(vmem_limit_bytes=40 * 1024 * 1024),
        cost_estimate=pl.CostEstimate(flops=flops, bytes_accessed=moved, transcendentals=0),
    )(*operands)


def split_columns(place, whole):
    rows, columns = whole.shape
    piece = jax.ShapeDtypeStruct((rows, columns // SIDE), whole.dtype)
    return local_call(split_kernel, [piece] * SIDE, [place, whole], 1)


def join_columns(place, pieces):
    rows, columns = pieces[0].shape
    whole = jax.ShapeDtypeStruct((rows, columns * SIDE), pieces[0].dtype)
    return local_call(join_kernel, [whole], [place, *pieces], 1)[0]


def layer_terms(cots, rows):
    tokens, features = cots[0].shape
    width = rows[0].shape[0]
    out = jax.ShapeDtypeStruct((tokens, SIDE * width), jnp.bfloat16)
    flops = 2 * tokens * features * width * SIDE * SIDE
    return local_call(layer_kernel, [out] * SIDE, [*cots, *rows], 0, flops)


def weight_terms(ins, cots):
    tokens, features = cots[0].shape
    width = ins[0].shape[1] // SIDE
    part = jax.ShapeDtypeStruct((width, features), jnp.float32)
    exponents = jax.ShapeDtypeStruct((SIDE - 1, 128), jnp.float32)
    flops = 2 * tokens * features * width * SIDE * SIDE
    *parts, exponents = local_call(
        weight_kernel, [part] * SIDE + [exponents], [*ins, *cots], 0, flops
    )
    return parts, exponents[:, 0]


def exchange(pieces, first):
    return [pieces[0]] + [move(pieces[-j % SIDE], first, -j) for j in range(1, SIDE)]


def gather(value, first):
    return exchange([value] * SIDE, first)


def coded(part, exponent):
    tail = jnp.full((TAIL, part.shape[1]), exponent)
    return jnp.concatenate([part * jnp.exp2(exponent), tail], 0).astype(jnp.float16)


def decoded(value):
    value = value.astype(jnp.float32)
    return value[:-TAIL] * jnp.exp2(-value[-1:, :1])


def shards(layer_input, key_cotangent, key_weight, block_mask):
    inputs = layer_input[0]
    cotangent = key_cotangent[0]
    weight = key_weight[0]
    flags_layer = block_mask[0]
    own_index = lax.axis_index("dp")
    parity = lax.axis_index("section") % 2
    x, y = own_index // SIDE, own_index % SIDE
    block_rows = weight.shape[0] // BLOCK
    even = jnp.stack([0, x, y]).astype(jnp.int32)
    odd = jnp.stack([1, y, x]).astype(jnp.int32)
    place = jnp.where(parity == 0, even, odd)
    place_above = jnp.where(parity == 0, odd, even)

    with jax.named_scope("cot"):
        cots = gather(cotangent, True)

    with jax.named_scope("rows"):
        own_flags = lax.dynamic_slice_in_dim(flags_layer, own_index * block_rows, block_rows, 0)
        masked = weight * expand(own_flags).astype(weight.dtype)
        rows = gather(masked, False)

    with jax.named_scope("ins"):
        inputs, _ = lax.optimization_barrier((inputs, rows[1]))
        ins = exchange(split_columns(place, inputs), True)

    with jax.named_scope("layer"):
        grads = exchange(layer_terms(cots, rows), True)
    with jax.named_scope("below"):
        incoming = [to_layer_below(piece) for piece in grads]
        input_grad = join_columns(place_above, incoming)

    with jax.named_scope("weight"):
        parts, exponents = weight_terms(ins, cots)
        sent = exchange(
            [parts[0]] + [coded(parts[m], exponents[m - 1]) for m in range(1, SIDE)], False
        )
        total = sent[0] + sum(decoded(value) for value in sent[1:])
        grad_scale = 1.0 / math.sqrt(cotangent.shape[0] * lax.axis_size("dp"))
        weight_grad = total * (expand(own_flags).astype(jnp.float32) * grad_scale)
    return (weight_grad[None], input_grad[None])


def solution(mesh):
    placed = (
        P("section", "dp", None),
        P("section", "dp", None),
        P("section", "dp", None),
        P("section", None, None),
    )
    return jax.shard_map(
        shards,
        mesh=mesh,
        in_specs=placed,
        out_specs=(P("section", "dp", None), P("section", "dp", None)),
        check_vma=False,
    )
```

time: 352 us -> 164 us (0.47)
  waiting for transfers between devices: 244 us -> 75.8 us
  local copies, waits for them, and re-layouts: 54.6 us -> 16.8 us
  matrix products: 33.6 us -> 0 us
  starting transfers between devices: 3.53 us -> 35.2 us
  Pallas kernels: 0 us -> 18.5 us
  between operations: 14.1 us -> 7.03 us
  other arithmetic: 1.76 us -> 7.91 us
    reduce_scatter x1 -> x0, waiting for transfers between devices: 136 us -> none  [shards(): lax.psum_scatter(product * expand(flags_layer).astype(jnp.float32) * grad...]
    all_gather x1 -> x0, waiting for transfers between devices: 59.6 us -> none  [shards(): lax.all_gather(masked, 'dp', axis=0, tiled=True)]
    convert_element_type x2 -> x0, local copies, waits for them, and re-layouts: 34.1 us -> none  [shards(): expand(flags_layer).astype(jnp.float32)]
    dot_general x2 -> x0, matrix products: 33.6 us -> none  [the longest x1 23.1 us: shards(): lax.dot_general(inputs, cotangent, (((0,), (0,)), ((), ())), preferred_el...]
    ppermute x1 -> x19, starting transfers between devices: 3.45 us -> 35.2 us  [the longest x15 22.4 us: move(): return lax.ppermute(value, ('section', 'dp'), pairs)]
    ppermute x1 -> x19, waiting for transfers between devices: 47.7 us -> 75.8 us  [the longest x15 57.1 us: move(): return lax.ppermute(value, ('section', 'dp'), pairs)]
    pallas_call x0 -> x4, Pallas kernels: none -> 18.5 us  [local_call(): pl.pallas_call(kernel, out_shape=out_shape, in_specs=[pl.BlockSpec(memory...]
    broadcast_in_dim x3 -> x4, local copies, waits for them, and re-layouts: 11.6 us -> 1.83 us  [expand(): return jnp.repeat(jnp.repeat(flags, BLOCK, 0), BLOCK, 1)]
  transfers between devices with their start and end apart: 3 -> 19, of which waited for: 3 -> 6; matrix products, arithmetic and copies ran while one was open for 25% -> 9% of each run, Pallas kernels for 0% -> 11%
where the time goes in v2:
time: 164 us; the launch traced here: 161 us
  waiting for transfers between devices  75.8 us (46%)
  starting transfers between devices  35.2 us (21%)
  Pallas kernels  18.5 us (11%)
  local copies, waits for them, and re-layouts  16.8 us (10%)
  other arithmetic  7.91 us (5%)
  between operations  7.03 us (4%)
    ppermute x15, waiting for transfers between devices, move(): return lax.ppermute(value, ('section', 'dp'), pairs)  57.1 us
    ppermute x15, starting transfers between devices, move(): return lax.ppermute(value, ('section', 'dp'), pairs)  22.4 us
    ppermute x4, waiting for transfers between devices, to_layer_below(): return lax.ppermute(value, 'section', [(s, s - 1) for s in range(1, count)])  18.7 us
    pallas_call x4, Pallas kernels, local_call(): pl.pallas_call(kernel, out_shape=out_shape, in_specs=[pl.BlockSpec(memory...  18.5 us
    ppermute x4, starting transfers between devices, to_layer_below(): return lax.ppermute(value, 'section', [(s, s - 1) for s in range(1, count)])  12.8 us
    unnamed x17, local copies, waits for them, and re-layouts  5.15 us
    convert_element_type x3, other arithmetic, decoded(): value = value.astype(jnp.float32)  4.27 us
    concatenate x3, local copies, waits for them, and re-layouts, coded(): jnp.concatenate([part * jnp.exp2(exponent), tail], 0).astype(jnp.float16)  3.83 us
  transfers between devices with their start and end apart: 19, of which 6 were waited for; matrix products, arithmetic and copies ran while one was open for 9% of the time, Pallas kernels for 11%

profile of v2, /device:TPU:1, one launch (start us, length us, event | category | flops | bytes accessed | tf_op | source)
XLA Modules:
  0.0 161.2 jit_solution(17979066163047730309)
XLA Ops:
  2.5 3.4 %collective-permute-start = (bf16[512,1024]{1,0:T(8,128)(2,1)S(1)}, bf16[512,1024]{1,0:T(8,128)(2,1)S(1)}, u32[]{:S(2)}, u32[]{:S(2)}) collective-permute-start(bf16[512,1024]{1,0:T(8,128)(2,1)S(1)} %bitcast_multiply_fusion.refs_4_), channel_id=1, source_target_pairs={{0,3},{1,0},{2,1},{3,2},{4,7},{5,4},{6,5},{7,6},{8,11},{9,8},{10,9... | collective-permute-start | bytes 3145736 | tf_op jit(solution)/shard_map/rows/ppermute | solution.py:31
  7.0 2.7 %collective-permute-start.4 = (bf16[256,1024]{1,0:T(8,128)(2,1)}, bf16[256,1024]{1,0:T(8,128)(2,1)}, u32[]{:S(2)}, u32[]{:S(2)}) collective-permute-start(bf16[256,1024]{1,0:T(8,128)(2,1)} %bitcast.6.refs_4_.refs_0_), channel_id=1, source_target_pairs={{0,12},{1,13},{2,14},{3,15},{4,0},{5,1},{6,2},{7,3},{8,4},{9,5},{1... | collective-permute-start | bytes 1572872 | tf_op jit(solution)/shard_map/cot/ppermute | solution.py:31
  10.1 29.4 %collective-permute-done.refs_5_ = bf16[512,1024]{1,0:T(8,128)(2,1)S(1)} collective-permute-done((bf16[512,1024]{1,0:T(8,128)(2,1)S(1)}, bf16[512,1024]{1,0:T(8,128)(2,1)S(1)}, u32[]{:S(2)}, u32[]{:S(2)}) %collective-permute-start) | collective-permute-done | bytes 1048608 | tf_op jit(solution)/shard_map/rows/ppermute | solution.py:31
  39.6 1.0 collective-permute-start.6
  40.6 2.2 %copy-done.2 = bf16[1,256,8192]{2,1,0:T(8,128)(2,1)S(1)} copy-done((bf16[1,256,8192]{2,1,0:T(8,128)(2,1)S(1)}, bf16[1,256,8192]{2,1,0:T(8,128)(2,1)}, u32[]{:S(2)}) %copy-start.2) | copy-done | bytes 4194328
  43.7 2.4 %collective-permute-start.1 = (bf16[256,2048]{1,0:T(8,128)(2,1)S(1)}, bf16[256,2048]{1,0:T(8,128)(2,1)S(1)}, u32[]{:S(2)}, u32[]{:S(2)}) collective-permute-start(bf16[256,2048]{1,0:T(8,128)(2,1)S(1)} %get-tuple-element.18), channel_id=1, source_target_pairs={{0,12},{1,13},{2,14},{3,15},{4,0},{5,1},{6,2},{7,3},{8,4},{9,5},{1... | collective-permute-start | bytes 3145736 | tf_op jit(solution)/shard_map/ins/ppermute | solution.py:31
  46.1 1.3 collective-permute-start.2
  47.4 2.6 %collective-permute-done.6.refs_7_.refs_3_ = bf16[256,1024]{1,0:T(8,128)(2,1)} collective-permute-done((bf16[256,1024]{1,0:T(8,128)(2,1)}, bf16[256,1024]{1,0:T(8,128)(2,1)}, u32[]{:S(2)}, u32[]{:S(2)}) %collective-permute-start.6) | collective-permute-done | bytes 524320 | tf_op jit(solution)/shard_map/cot/ppermute | solution.py:31
  50.1 6.4 %layer.1 = (bf16[256,2048]{1,0:T(8,128)(2,1)S(1)}, bf16[256,2048]{1,0:T(8,128)(2,1)S(1)}, bf16[256,2048]{1,0:T(8,128)(2,1)S(1)}, bf16[256,2048]{1,0:T(8,128)(2,1)S(1)}) custom-call(bf16[256,1024]{1,0:T(8,128)(2,1)} %bitcast.6.refs_4_.refs_0_, bf16[256,1024]{1,0:T(8,128)(2,1)} %collective-permute-done.4.refs_5_.refs_1_, ...), custom_call_target="tpu_custom_call" | custom-call | flops 4294967296 | bytes 10485760 | tf_op jit(solution)/shard_map/layer/pallas_call | solution.py:104
  56.5 1.5 collective-permute-start.13
  58.0 4.6 %collective-permute-start.12 = (bf16[256,2048]{1,0:T(8,128)(2,1)S(1)}, bf16[256,2048]{1,0:T(8,128)(2,1)S(1)}, u32[]{:S(2)}, u32[]{:S(2)}) collective-permute-start(bf16[256,2048]{1,0:T(8,128)(2,1)S(1)} %get-tuple-element.26), channel_id=1, source_target_pairs={{16,0},{32,16},{48,32},{64,48},{80,64},{96,80},{112,96},{128,112},... | collective-permute-start | bytes 3145736 | tf_op jit(solution)/shard_map/below/ppermute | solution.py:36
  62.6 6.5 %collective-permute-done.1.refs_1_ = bf16[256,2048]{1,0:T(8,128)(2,1)S(1)} collective-permute-done((bf16[256,2048]{1,0:T(8,128)(2,1)S(1)}, bf16[256,2048]{1,0:T(8,128)(2,1)S(1)}, u32[]{:S(2)}, u32[]{:S(2)}) %collective-permute-start.1) | collective-permute-done | bytes 1048608 | tf_op jit(solution)/shard_map/ins/ppermute | solution.py:31
  69.1 4.0 %collective-permute-start.17 = (bf16[256,2048]{1,0:T(8,128)(2,1)S(1)}, bf16[256,2048]{1,0:T(8,128)(2,1)}, u32[]{:S(2)}, u32[]{:S(2)}) collective-permute-start(bf16[256,2048]{1,0:T(8,128)(2,1)S(1)} %get-tuple-element.29), channel_id=1, source_target_pairs={{0,4},{1,5},{2,6},{3,7},{4,8},{5,9},{6,10},{7,11},{8,12},{9,13},{1... | collective-permute-start | bytes 3145736 | tf_op jit(solution)/shard_map/layer/ppermute | solution.py:31
  73.1 18.5 %collective-permute-done.13 = bf16[256,2048]{1,0:T(8,128)(2,1)S(1)} collective-permute-done((bf16[256,2048]{1,0:T(8,128)(2,1)S(1)}, bf16[256,2048]{1,0:T(8,128)(2,1)S(1)}, u32[]{:S(2)}, u32[]{:S(2)}) %collective-permute-start.13) | collective-permute-done | bytes 1048608 | tf_op jit(solution)/shard_map/layer/ppermute | solution.py:31
  91.6 4.4 %collective-permute-start.14 = (bf16[256,2048]{1,0:T(8,128)(2,1)S(1)}, bf16[256,2048]{1,0:T(8,128)(2,1)S(1)}, u32[]{:S(2)}, u32[]{:S(2)}) collective-permute-start(bf16[256,2048]{1,0:T(8,128)(2,1)S(1)} %collective-permute-done.13), channel_id=1, source_target_pairs={{16,0},{32,16},{48,32},{64,48},{80,64},{96,80},{112,96},{128,112},... | collective-permute-start | bytes 3145736 | tf_op jit(solution)/shard_map/below/ppermute | solution.py:36
  96.0 7.4 %weight.1 = (f32[512,1024]{1,0:T(8,128)S(1)}, f32[512,1024]{1,0:T(8,128)S(1)}, f32[512,1024]{1,0:T(8,128)S(1)}, f32[512,1024]{1,0:T(8,128)}, f32[3,128]{1,0:T(4,128)S(1)}) custom-call(bf16[256,2048]{1,0:T(8,128)(2,1)S(1)} %get-tuple-element.17.refs_0_, bf16[256,2048]{1,0:T(8,128)(2,1)S(1)} %collective-permute-done.1.refs_1_, ...), custom_call_target="tpu_custom_call" | custom-call | flops 4294967296 | bytes 14681600 | tf_op jit(solution)/shard_map/weight/pallas_call | solution.py:104
  106.7 1.3 concatenate.11
  109.0 1.3 concatenate.10
  110.3 4.6 %collective-permute-start.8 = (f16[520,1024]{1,0:T(8,128)(2,1)}, f16[520,1024]{1,0:T(8,128)(2,1)}, u32[]{:S(2)}, u32[]{:S(2)}) collective-permute-start(f16[520,1024]{1,0:T(8,128)(2,1)} %concatenate.10), channel_id=1, source_target_pairs={{0,2},{1,3},{2,0},{3,1},{4,6},{5,7},{6,4},{7,5},{8,10},{9,11},{10,... | collective-permute-start | bytes 3194888 | tf_op jit(solution)/shard_map/weight/ppermute | solution.py:31
  115.9 1.2 concatenate.9
  117.1 1.9 %collective-permute-start.16 = (bf16[256,2048]{1,0:T(8,128)(2,1)}, bf16[256,2048]{1,0:T(8,128)(2,1)}, u32[]{:S(2)}, u32[]{:S(2)}) collective-permute-start(bf16[256,2048]{1,0:T(8,128)(2,1)} %collective-permute-done.15), channel_id=1, source_target_pairs={{16,0},{32,16},{48,32},{64,48},{80,64},{96,80},{112,96},{128,112},... | collective-permute-start | bytes 3145736 | tf_op jit(solution)/shard_map/below/ppermute | solution.py:36
  120.0 1.9 %collective-permute-start.18 = (bf16[256,2048]{1,0:T(8,128)(2,1)}, bf16[256,2048]{1,0:T(8,128)(2,1)}, u32[]{:S(2)}, u32[]{:S(2)}) collective-permute-start(bf16[256,2048]{1,0:T(8,128)(2,1)} %collective-permute-done.17), channel_id=1, source_target_pairs={{16,0},{32,16},{48,32},{64,48},{80,64},{96,80},{112,96},{128,112},... | collective-permute-start | bytes 3145736 | tf_op jit(solution)/shard_map/below/ppermute | solution.py:36
  122.2 1.6 broadcast_in_dim.24
  123.8 2.9 %copy.11 = f32[512,1024]{1,0:T(8,128)} copy(f32[512,1024]{0,1:T(8,128)} %bitcast.29) | data formatting | bytes 4194304 | tf_op jit(solution)/shard_map/weight/mul | solution.py:204
  126.8 7.7 %collective-permute-done.16.refs_2_ = bf16[256,2048]{1,0:T(8,128)(2,1)} collective-permute-done((bf16[256,2048]{1,0:T(8,128)(2,1)}, bf16[256,2048]{1,0:T(8,128)(2,1)}, u32[]{:S(2)}, u32[]{:S(2)}) %collective-permute-start.16) | collective-permute-done | bytes 1048608 | tf_op jit(solution)/shard_map/below/ppermute | solution.py:36
  134.5 10.9 %collective-permute-done.18.refs_3_ = bf16[256,2048]{1,0:T(8,128)(2,1)} collective-permute-done((bf16[256,2048]{1,0:T(8,128)(2,1)}, bf16[256,2048]{1,0:T(8,128)(2,1)}, u32[]{:S(2)}, u32[]{:S(2)}) %collective-permute-start.18) | collective-permute-done | bytes 1048608 | tf_op jit(solution)/shard_map/below/ppermute | solution.py:36
  145.5 1.2 copy-done.4
  146.7 3.8 %below.1 = bf16[256,8192]{1,0:T(8,128)(2,1)} custom-call(s32[3]{0:T(128)S(1)} %broadcast_select_fusion.place_ref, bf16[256,2048]{1,0:T(8,128)(2,1)S(1)} %collective-permute-done.12.refs_0_, bf16[256,2048]{1,0:T(8,128)(2,1)S(1)} %copy-done.4, bf16[256,2048]{1,0:T(8,128)(2,1)} %collective-permute-done.16.refs_2_, bf16[256,2048]{1,0:T(8,128)(2,1)} %collective-permute-done.18.refs_3_), custom_call_target="tpu_custom_call" | custom-call | bytes 8388620 | tf_op jit(solution)/shard_map/below/pallas_call | solution.py:104
  150.6 1.4 convert_element_type.40
  153.2 1.4 convert_element_type.39
  156.0 1.4 convert_element_type.38
  158.6 2.6 %fusion.3 = f32[1,512,1024]{2,1,0:T(8,128)} fusion(f32[512,1024]{1,0:T(8,128)S(1)} %copy-done.5, f32[512,1024]{1,0:T(8,128)S(1)} %get-tuple-element.21, f32[520,1024]{1,0:T(8,128)S(1)} %convert_element_type.40, f32[520,1024]{1,0:T(8,128)S(1)} %convert_element_type.39, f32[520,1024]{1,0:T(8,128)S(1)} %convert_element_type.38, f32[]{:T(128)} %bitcast.15, ...), kind=kLoop, calls=%fused_computation.4 | loop fusion | flops 3670016 | bytes 12582924 | tf_op jit(solution)/shard_map/broadcast_in_dim | solution.py:205
  (57 shorter events, 8.5 us)
Async XLA Ops:
  0.6 0.7 copy-start
  0.6 1.8 %copy-start.7 = (bf16[1,512,1024]{2,1,0:T(8,128)(2,1)S(1)}, bf16[1,512,1024]{2,1,0:T(8,128)(2,1)}, u32[]{:S(2)}) copy-start(bf16[1,512,1024]{2,1,0:T(8,128)(2,1)} %param.6) | copy-start | bytes 3145732
  2.5 37.0 %collective-permute-start = (bf16[512,1024]{1,0:T(8,128)(2,1)S(1)}, bf16[512,1024]{1,0:T(8,128)(2,1)S(1)}, u32[]{:S(2)}, u32[]{:S(2)}) collective-permute-start(bf16[512,1024]{1,0:T(8,128)(2,1)S(1)} %bitcast_multiply_fusion.refs_4_), channel_id=1, source_target_pairs={{0,3},{1,0},{2,1},{3,2},{4,7},{5,4},{6,5},{7,6},{8,11},{9,8},{10,9... | collective-permute-start | bytes 3145736 | tf_op jit(solution)/shard_map/rows/ppermute | solution.py:31
  5.9 44.1 %collective-permute-start.10 = (bf16[512,1024]{1,0:T(8,128)(2,1)S(1)}, bf16[512,1024]{1,0:T(8,128)(2,1)S(1)}, u32[]{:S(2)}, u32[]{:S(2)}) collective-permute-start(bf16[512,1024]{1,0:T(8,128)(2,1)S(1)} %bitcast_multiply_fusion.refs_4_), channel_id=1, source_target_pairs={{0,2},{1,3},{2,0},{3,1},{4,6},{5,7},{6,4},{7,5},{8,10},{9,11},{10,... | collective-permute-start | bytes 3145736 | tf_op jit(solution)/shard_map/rows/ppermute | solution.py:31
  6.4 43.6 %collective-permute-start.11 = (bf16[512,1024]{1,0:T(8,128)(2,1)S(1)}, bf16[512,1024]{1,0:T(8,128)(2,1)}, u32[]{:S(2)}, u32[]{:S(2)}) collective-permute-start(bf16[512,1024]{1,0:T(8,128)(2,1)S(1)} %bitcast_multiply_fusion.refs_4_), channel_id=1, source_target_pairs={{0,1},{1,2},{2,3},{3,0},{4,5},{5,6},{6,7},{7,4},{8,9},{9,10},{10,1... | collective-permute-start | bytes 3145736 | tf_op jit(solution)/shard_map/rows/ppermute | solution.py:31
  7.0 36.7 %collective-permute-start.4 = (bf16[256,1024]{1,0:T(8,128)(2,1)}, bf16[256,1024]{1,0:T(8,128)(2,1)}, u32[]{:S(2)}, u32[]{:S(2)}) collective-permute-start(bf16[256,1024]{1,0:T(8,128)(2,1)} %bitcast.6.refs_4_.refs_0_), channel_id=1, source_target_pairs={{0,12},{1,13},{2,14},{3,15},{4,0},{5,1},{6,2},{7,3},{8,4},{9,5},{1... | collective-permute-start | bytes 1572872 | tf_op jit(solution)/shard_map/cot/ppermute | solution.py:31
  9.8 36.3 %collective-permute-start.5 = (bf16[256,1024]{1,0:T(8,128)(2,1)}, bf16[256,1024]{1,0:T(8,128)(2,1)}, u32[]{:S(2)}, u32[]{:S(2)}) collective-permute-start(bf16[256,1024]{1,0:T(8,128)(2,1)} %bitcast.6.refs_4_.refs_0_), channel_id=1, source_target_pairs={{0,8},{1,9},{2,10},{3,11},{4,12},{5,13},{6,14},{7,15},{8,0},{9,1},... | collective-permute-start | bytes 1572872 | tf_op jit(solution)/shard_map/cot/ppermute | solution.py:31
  39.6 10.5 %collective-permute-start.6 = (bf16[256,1024]{1,0:T(8,128)(2,1)}, bf16[256,1024]{1,0:T(8,128)(2,1)}, u32[]{:S(2)}, u32[]{:S(2)}) collective-permute-start(bf16[256,1024]{1,0:T(8,128)(2,1)} %bitcast.6.refs_4_.refs_0_), channel_id=1, source_target_pairs={{0,4},{1,5},{2,6},{3,7},{4,8},{5,9},{6,10},{7,11},{8,12},{9,13},{1... | collective-permute-start | bytes 1572872 | tf_op jit(solution)/shard_map/cot/ppermute | solution.py:31
  40.6 2.2 %copy-start.2 = (bf16[1,256,8192]{2,1,0:T(8,128)(2,1)S(1)}, bf16[1,256,8192]{2,1,0:T(8,128)(2,1)}, u32[]{:S(2)}) copy-start(bf16[1,256,8192]{2,1,0:T(8,128)(2,1)} %param.4) | copy-start | bytes 12582916
  43.7 25.4 %collective-permute-start.1 = (bf16[256,2048]{1,0:T(8,128)(2,1)S(1)}, bf16[256,2048]{1,0:T(8,128)(2,1)S(1)}, u32[]{:S(2)}, u32[]{:S(2)}) collective-permute-start(bf16[256,2048]{1,0:T(8,128)(2,1)S(1)} %get-tuple-element.18), channel_id=1, source_target_pairs={{0,12},{1,13},{2,14},{3,15},{4,0},{5,1},{6,2},{7,3},{8,4},{9,5},{1... | collective-permute-start | bytes 3145736 | tf_op jit(solution)/shard_map/ins/ppermute | solution.py:31
  46.1 23.0 %collective-permute-start.2 = (bf16[256,2048]{1,0:T(8,128)(2,1)S(1)}, bf16[256,2048]{1,0:T(8,128)(2,1)S(1)}, u32[]{:S(2)}, u32[]{:S(2)}) collective-permute-start(bf16[256,2048]{1,0:T(8,128)(2,1)S(1)} %get-tuple-element.19), channel_id=1, source_target_pairs={{0,8},{1,9},{2,10},{3,11},{4,12},{5,13},{6,14},{7,15},{8,0},{9,1},... | collective-permute-start | bytes 3145736 | tf_op jit(solution)/shard_map/ins/ppermute | solution.py:31
  56.5 35.1 %collective-permute-start.13 = (bf16[256,2048]{1,0:T(8,128)(2,1)S(1)}, bf16[256,2048]{1,0:T(8,128)(2,1)S(1)}, u32[]{:S(2)}, u32[]{:S(2)}) collective-permute-start(bf16[256,2048]{1,0:T(8,128)(2,1)S(1)} %get-tuple-element.27), channel_id=1, source_target_pairs={{0,12},{1,13},{2,14},{3,15},{4,0},{5,1},{6,2},{7,3},{8,4},{9,5},{1... | collective-permute-start | bytes 3145736 | tf_op jit(solution)/shard_map/layer/ppermute | solution.py:31
  58.0 37.9 %collective-permute-start.3 = (bf16[256,2048]{1,0:T(8,128)(2,1)S(1)}, bf16[256,2048]{1,0:T(8,128)(2,1)S(1)}, u32[]{:S(2)}, u32[]{:S(2)}) collective-permute-start(bf16[256,2048]{1,0:T(8,128)(2,1)S(1)} %get-tuple-element.20), channel_id=1, source_target_pairs={{0,4},{1,5},{2,6},{3,7},{4,8},{5,9},{6,10},{7,11},{8,12},{9,13},{1... | collective-permute-start | bytes 3145736 | tf_op jit(solution)/shard_map/ins/ppermute | solution.py:31
  58.0 52.3 %collective-permute-start.12 = (bf16[256,2048]{1,0:T(8,128)(2,1)S(1)}, bf16[256,2048]{1,0:T(8,128)(2,1)S(1)}, u32[]{:S(2)}, u32[]{:S(2)}) collective-permute-start(bf16[256,2048]{1,0:T(8,128)(2,1)S(1)} %get-tuple-element.26), channel_id=1, source_target_pairs={{16,0},{32,16},{48,32},{64,48},{80,64},{96,80},{112,96},{128,112},... | collective-permute-start | bytes 3145736 | tf_op jit(solution)/shard_map/below/ppermute | solution.py:36
  69.1 48.0 %collective-permute-start.15 = (bf16[256,2048]{1,0:T(8,128)(2,1)S(1)}, bf16[256,2048]{1,0:T(8,128)(2,1)}, u32[]{:S(2)}, u32[]{:S(2)}) collective-permute-start(bf16[256,2048]{1,0:T(8,128)(2,1)S(1)} %get-tuple-element.28), channel_id=1, source_target_pairs={{0,8},{1,9},{2,10},{3,11},{4,12},{5,13},{6,14},{7,15},{8,0},{9,1},... | collective-permute-start | bytes 3145736 | tf_op jit(solution)/shard_map/layer/ppermute | solution.py:31
  69.1 48.0 %collective-permute-start.17 = (bf16[256,2048]{1,0:T(8,128)(2,1)S(1)}, bf16[256,2048]{1,0:T(8,128)(2,1)}, u32[]{:S(2)}, u32[]{:S(2)}) collective-permute-start(bf16[256,2048]{1,0:T(8,128)(2,1)S(1)} %get-tuple-element.29), channel_id=1, source_target_pairs={{0,4},{1,5},{2,6},{3,7},{4,8},{5,9},{6,10},{7,11},{8,12},{9,13},{1... | collective-permute-start | bytes 3145736 | tf_op jit(solution)/shard_map/layer/ppermute | solution.py:31
  91.6 27.5 %collective-permute-start.14 = (bf16[256,2048]{1,0:T(8,128)(2,1)S(1)}, bf16[256,2048]{1,0:T(8,128)(2,1)S(1)}, u32[]{:S(2)}, u32[]{:S(2)}) collective-permute-start(bf16[256,2048]{1,0:T(8,128)(2,1)S(1)} %collective-permute-done.13), channel_id=1, source_target_pairs={{16,0},{32,16},{48,32},{64,48},{80,64},{96,80},{112,96},{128,112},... | collective-permute-start | bytes 3145736 | tf_op jit(solution)/shard_map/below/ppermute | solution.py:36
  108.0 42.5 %collective-permute-start.9 = (f16[520,1024]{1,0:T(8,128)(2,1)}, f16[520,1024]{1,0:T(8,128)(2,1)}, u32[]{:S(2)}, u32[]{:S(2)}) collective-permute-start(f16[520,1024]{1,0:T(8,128)(2,1)} %concatenate.11), channel_id=1, source_target_pairs={{0,1},{1,2},{2,3},{3,0},{4,5},{5,6},{6,7},{7,4},{8,9},{9,10},{10,1... | collective-permute-start | bytes 3194888 | tf_op jit(solution)/shard_map/weight/ppermute | solution.py:31
  108.7 6.2 %copy-start.6 = (f32[512,1024]{1,0:T(8,128)S(1)}, f32[512,1024]{1,0:T(8,128)}, u32[]{:S(2)}) copy-start(f32[512,1024]{1,0:T(8,128)} %get-tuple-element.22) | copy-start | bytes 6291460
  110.3 42.8 %collective-permute-start.8 = (f16[520,1024]{1,0:T(8,128)(2,1)}, f16[520,1024]{1,0:T(8,128)(2,1)}, u32[]{:S(2)}, u32[]{:S(2)}) collective-permute-start(f16[520,1024]{1,0:T(8,128)(2,1)} %concatenate.10), channel_id=1, source_target_pairs={{0,2},{1,3},{2,0},{3,1},{4,6},{5,7},{6,4},{7,5},{8,10},{9,11},{10,... | collective-permute-start | bytes 3194888 | tf_op jit(solution)/shard_map/weight/ppermute | solution.py:31
  117.1 38.8 %collective-permute-start.7 = (f16[520,1024]{1,0:T(8,128)(2,1)}, f16[520,1024]{1,0:T(8,128)(2,1)}, u32[]{:S(2)}, u32[]{:S(2)}) collective-permute-start(f16[520,1024]{1,0:T(8,128)(2,1)} %concatenate.9), channel_id=1, source_target_pairs={{0,3},{1,0},{2,1},{3,2},{4,7},{5,4},{6,5},{7,6},{8,11},{9,8},{10,9... | collective-permute-start | bytes 3194888 | tf_op jit(solution)/shard_map/weight/ppermute | solution.py:31
  117.1 17.4 %collective-permute-start.16 = (bf16[256,2048]{1,0:T(8,128)(2,1)}, bf16[256,2048]{1,0:T(8,128)(2,1)}, u32[]{:S(2)}, u32[]{:S(2)}) collective-permute-start(bf16[256,2048]{1,0:T(8,128)(2,1)} %collective-permute-done.15), channel_id=1, source_target_pairs={{16,0},{32,16},{48,32},{64,48},{80,64},{96,80},{112,96},{128,112},... | collective-permute-start | bytes 3145736 | tf_op jit(solution)/shard_map/below/ppermute | solution.py:36
  119.1 1.0 copy-start.3
  120.0 25.4 %collective-permute-start.18 = (bf16[256,2048]{1,0:T(8,128)(2,1)}, bf16[256,2048]{1,0:T(8,128)(2,1)}, u32[]{:S(2)}, u32[]{:S(2)}) collective-permute-start(bf16[256,2048]{1,0:T(8,128)(2,1)} %collective-permute-done.17), channel_id=1, source_target_pairs={{16,0},{32,16},{48,32},{64,48},{80,64},{96,80},{112,96},{128,112},... | collective-permute-start | bytes 3145736 | tf_op jit(solution)/shard_map/below/ppermute | solution.py:36
  145.5 1.2 copy-start.4
  154.6 4.0 %copy-start.5 = (f32[512,1024]{1,0:T(8,128)S(1)}, f32[512,1024]{1,0:T(8,128)}, u32[]{:S(2)}) copy-start(f32[512,1024]{1,0:T(8,128)} %copy.11) | copy-start | bytes 6291460
  158.6 2.6 %copy-start.1 = (s32[1,128,16]{1,2,0:T(8,128)S(1)}, s32[1,128,16]{1,2,0:T(8,128)}, u32[]{:S(2)}) copy-start(s32[1,128,16]{1,2,0:T(8,128)} %param.7) | copy-start | bytes 24580

commit v3 on v0

v3 whole, which is shorter than its diff:
```python
import functools
import math

import jax
import jax.numpy as jnp
from jax import lax
from jax.experimental import pallas as pl
from jax.experimental.pallas import tpu as pltpu
from jax.sharding import PartitionSpec as P

BLOCK = 64
SIDE = 4
TAIL = 8
VMEM = pl.BlockSpec(memory_space=pltpu.VMEM)
SMEM = pl.BlockSpec(memory_space=pltpu.SMEM)
HBM = pl.BlockSpec(memory_space=pltpu.HBM)


def on_axis(index, parity, first, steps):
    x, y = index // SIDE, index % SIDE
    if (parity == 0) == first:
        x = (x + steps) % SIDE
    else:
        y = (y + steps) % SIDE
    return x * SIDE + y


def move(value, first, steps):
    sections, replicas = lax.axis_size("section"), lax.axis_size("dp")
    pairs = [
        (s * replicas + i, s * replicas + on_axis(i, s % 2, first, steps))
        for s in range(sections)
        for i in range(replicas)
    ]
    return lax.ppermute(value, ("section", "dp"), pairs)


def to_layer_below(value):
    count = lax.axis_size("section")
    return lax.ppermute(value, "section", [(s, s - 1) for s in range(1, count)])


def column_start(place_ref, k, m, width):
    a = lax.rem(place_ref[1] + k, SIDE)
    b = lax.rem(place_ref[2] + m, SIDE)
    owner = jnp.where(place_ref[0] == 0, a * SIDE + b, b * SIDE + a)
    return pl.multiple_of(owner * width, width)


def mask_kernel(place_ref, flags_ref, weight_ref, masked_ref, mask_ref):
    rows, columns = weight_ref.shape
    block_columns, all_block_rows = flags_ref.shape
    first = place_ref[3] * (rows // BLOCK)

    def spread(short, long, offset):
        block = lax.broadcasted_iota(jnp.int32, (short, long), 1) // BLOCK + offset
        return (block == lax.broadcasted_iota(jnp.int32, (short, long), 0)).astype(jnp.float32)

    tall = jnp.dot(
        flags_ref[...].astype(jnp.float32),
        spread(all_block_rows, rows, first),
        preferred_element_type=jnp.float32,
    )
    mask = lax.dot_general(
        tall,
        spread(block_columns, columns, 0),
        (((0,), (0,)), ((), ())),
        preferred_element_type=jnp.float32,
    ).astype(jnp.bfloat16)
    mask_ref[...] = mask
    masked_ref[...] = weight_ref[...] * mask


def split_kernel(place_ref, cot_ref, whole_ref, *refs):
    pieces, sem = refs[:SIDE], refs[SIDE]
    features = cot_ref.shape[1]
    width = (pieces[0].shape[1] - features) // SIDE
    copies = []
    for k in (2, 1, 3, 0):
        for m in range(SIDE):
            start = column_start(place_ref, k, m, width)
            copies.append(
                pltpu.make_async_copy(
                    whole_ref.at[:, pl.ds(start, width)],
                    pieces[k].at[:, pl.ds(m * width, width)],
                    sem.at[k, m],
                )
            )
    for copy in copies:
        copy.start()
    for piece in pieces:
        piece[:, SIDE * width :] = cot_ref[...]
    for copy in copies:
        copy.wait()


def join_kernel(senders, place_ref, *refs):
    pieces, whole_ref, sem = refs[: len(senders)], refs[-2], refs[-1]
    width = pieces[0].shape[1] // SIDE
    copies = []
    for n, m in enumerate(senders):
        for k in range(SIDE):
            start = column_start(place_ref, k, m, width)
            copies.append(
                pltpu.make_async_copy(
                    pieces[n].at[:, pl.ds(k * width, width)],
                    whole_ref.at[:, pl.ds(start, width)],
                    sem.at[n, k],
                )
            )
    for copy in copies:
        copy.start()
    for copy in copies:
        copy.wait()


def layer_kernel(j, cots_ref, *refs):
    rows, out_ref = refs[:-1], refs[-1]
    tokens = out_ref.shape[0]
    start = 0
    for row_ref in rows:
        stop = start + row_ref.shape[0]
        out_ref[:, start:stop] = lax.dot_general(
            cots_ref[j * tokens : (j + 1) * tokens, :],
            row_ref[...],
            (((1,), (1,)), ((), ())),
            preferred_element_type=jnp.float32,
        ).astype(jnp.bfloat16)
        start = stop


def weight_kernel(m, coded, *refs):
    ins, cots_ref, out_ref = refs[:SIDE], refs[SIDE], refs[SIDE + 1]
    features = out_ref.shape[1]
    width = (ins[0].shape[1] - features) // SIDE
    part = lax.dot_general(
        jnp.concatenate([i[:, m * width : (m + 1) * width] for i in ins], 0),
        cots_ref[...],
        (((0,), (0,)), ((), ())),
        preferred_element_type=jnp.float32,
    )
    if coded:
        peak = jnp.max(jnp.abs(part), axis=0, keepdims=True)
        peak = jnp.max(peak, axis=1, keepdims=True)
        exponent = jnp.clip(jnp.floor(14.0 - jnp.log2(peak)), -100.0, 100.0)
        out_ref[:width, :] = part * jnp.exp2(exponent)
        out_ref[width:, :] = jnp.broadcast_to(exponent, (TAIL, features))
    else:
        out_ref[...] = part


def local_call(
    kernel, out_shape, operands, in_specs, out_specs, scratch=(), flops=0, aliases={}, mib=40
):
    shapes = list(operands) + list(out_shape)
    moved = sum(math.prod(a.shape) * a.dtype.itemsize for a in shapes)
    return pl.pallas_call(
        kernel,
        out_shape=out_shape,
        in_specs=in_specs,
        out_specs=out_specs,
        scratch_shapes=scratch,
        input_output_aliases=aliases,
        compiler_params=pltpu.CompilerParams(vmem_limit_bytes=mib * 1024 * 1024),
        cost_estimate=pl.CostEstimate(flops=0, bytes_accessed=0, transcendentals=0),
    )(*operands)


def mask_rows(place, flags, weight):
    masked = jax.ShapeDtypeStruct(weight.shape, weight.dtype)
    return local_call(
        mask_kernel, [masked] * 2, [place, flags, weight], [SMEM, VMEM, VMEM], [VMEM] * 2
    )


def split_columns(place, cot, whole):
    rows, columns = whole.shape
    piece = jax.ShapeDtypeStruct((rows, columns // SIDE + cot.shape[1]), whole.dtype)
    return local_call(
        split_kernel,
        [piece] * SIDE,
        [place, cot, whole],
        [SMEM, VMEM, HBM],
        [VMEM] * SIDE,
        [pltpu.SemaphoreType.DMA((SIDE, SIDE))],
    )


def join_columns(place, pieces, senders, whole=None):
    rows, columns = pieces[0].shape
    shape = jax.ShapeDtypeStruct((rows, columns * SIDE), pieces[0].dtype)
    chosen = [pieces[m] for m in senders]
    operands = [place, *chosen] + ([] if whole is None else [whole])
    specs = [SMEM] + [VMEM] * len(chosen) + ([] if whole is None else [HBM])
    return local_call(
        functools.partial(join_kernel, senders),
        [shape],
        operands,
        specs,
        [HBM],
        [pltpu.SemaphoreType.DMA((len(senders), SIDE))],
        aliases={} if whole is None else {len(operands) - 1: 0},
    )[0]


def layer_term(cots, rows, j):
    tokens, features = cots.shape[0] // SIDE, cots.shape[1]
    width = rows[0].shape[0]
    out = jax.ShapeDtypeStruct((tokens, SIDE * width), jnp.bfloat16)
    flops = 2 * tokens * features * width * SIDE
    return local_call(
        functools.partial(layer_kernel, j),
        [out],
        [cots, *rows],
        [VMEM] * (1 + len(rows)),
        [VMEM],
        (),
        flops,
    )[0]


def weight_term(ins, cots, m):
    tokens, features = cots.shape
    width = (ins[0].shape[1] - features) // SIDE
    coded = m != 0
    part = jax.ShapeDtypeStruct((width + (TAIL if coded else 0), features), jnp.float32)
    kernel = functools.partial(weight_kernel, m, coded)
    flops = 2 * tokens * features * width
    part = local_call(kernel, [part], [*ins, cots], [VMEM] * (SIDE + 1), [VMEM], (), flops)[0]
    return part.astype(jnp.float16) if coded else part


def exchange(pieces, first):
    received = [pieces[0]]
    for j in range(1, SIDE):
        with jax.named_scope(f"from{j}"):
            received.append(move(pieces[-j % SIDE], first, -j))
    return received


def after(value, *others):
    return lax.optimization_barrier((value, others))[0]


def decoded(value):
    return value[:-TAIL].astype(jnp.float32) * jnp.exp2(-value[-1:, :1].astype(jnp.float32))


def shards(layer_input, key_cotangent, key_weight, block_mask):
    inputs = layer_input[0]
    cotangent = key_cotangent[0]
    weight = key_weight[0]
    own_index = lax.axis_index("dp")
    parity = lax.axis_index("section") % 2
    x, y = own_index // SIDE, own_index % SIDE
    place = jnp.where(
        parity == 0, jnp.stack([0, x, y, own_index]), jnp.stack([1, y, x, own_index])
    ).astype(jnp.int32)
    features = cotangent.shape[1]

    pieces = list(split_columns(place, cotangent, inputs))
    masked, mask = mask_rows(place, block_mask[0].T, after(weight, pieces[0]))
    with jax.named_scope("rows_below"):
        rows_above = to_layer_below(masked)

    pieces[2], rows_above = lax.optimization_barrier((pieces[2], rows_above))
    with jax.named_scope("ins"):
        ins = exchange(pieces, True)
    cots = jnp.concatenate([piece[:, -features:] for piece in ins], 0)
    with jax.named_scope("cots_below"):
        cots_above = to_layer_below(cots)
    with jax.named_scope("rows"):
        far = after(rows_above, ins[1], ins[3])
        rows = exchange([rows_above, rows_above, far, rows_above], True)

    ins, cots, rows[1], rows[3] = lax.optimization_barrier((ins, cots, rows[1], rows[3]))
    parts = [None] * SIDE
    with jax.named_scope("weight"):
        parts[2] = weight_term(ins, cots, 2)
        parts[1] = weight_term(after(ins, parts[2]), cots, 1)
        parts[3] = weight_term(after(ins, parts[1]), cots, 3)

    parts[1], parts[2], parts[3], rows[2] = lax.optimization_barrier((*parts[1:], rows[2]))

    terms = [None] * SIDE
    with jax.named_scope("layer"):
        terms[1] = layer_term(cots_above, rows, 1)
        terms[3] = layer_term(after(cots_above, terms[1]), rows, 3)
        terms[2] = layer_term(after(cots_above, terms[3]), rows, 2)
        terms[0] = layer_term(after(cots_above, terms[2]), rows, 0)
        grads = exchange(terms, False)
    with jax.named_scope("join"):
        input_grad = join_columns(place, grads, (0, 1, 2, 3))

    with jax.named_scope("weight"):
        parts[0] = weight_term(after(ins, terms), cots, 0)
        sent = after(exchange(parts, False), terms)
        total = sent[0]
        for value in sent[1:]:
            total = lax.optimization_barrier(total + decoded(value))
        grad_scale = 1.0 / math.sqrt(cotangent.shape[0] * lax.axis_size("dp"))
        weight_grad = total * (mask.astype(jnp.float32) * grad_scale)
    return (weight_grad[None], input_grad[None])


def solution(mesh):
    placed = (
        P("section", "dp", None),
        P("section", "dp", None),
        P("section", "dp", None),
        P("section", None, None),
    )
    return jax.shard_map(
        shards,
        mesh=mesh,
        in_specs=placed,
        out_specs=(P("section", "dp", None), P("section", "dp", None)),
        check_vma=False,
    )
```

time: 352 us -> 135 us (0.38)
  waiting for transfers between devices: 244 us -> 77.2 us
  local copies, waits for them, and re-layouts: 54.6 us -> 6.95 us
  matrix products: 33.6 us -> 0 us
  starting transfers between devices: 3.53 us -> 21.4 us
  Pallas kernels: 0 us -> 16.1 us
  between operations: 14.1 us -> 3.11 us
  other arithmetic: 1.76 us -> 8.69 us
    reduce_scatter x1 -> x0, waiting for transfers between devices: 136 us -> none  [shards(): lax.psum_scatter(product * expand(flags_layer).astype(jnp.float32) * grad...]
    all_gather x1 -> x0, waiting for transfers between devices: 59.6 us -> none  [shards(): lax.all_gather(masked, 'dp', axis=0, tiled=True)]
    convert_element_type x4 -> x0, local copies, waits for them, and re-layouts: 34.3 us -> none  [the longest x2 34.1 us: shards(): expand(flags_layer).astype(jnp.float32)]
    dot_general x2 -> x0, matrix products: 33.6 us -> none  [the longest x1 23.1 us: shards(): lax.dot_general(inputs, cotangent, (((0,), (0,)), ((), ())), preferred_el...]
    ppermute x1 -> x14, waiting for transfers between devices: 47.7 us -> 77.2 us  [the longest x12 66.2 us: move(): return lax.ppermute(value, ('section', 'dp'), pairs)]
    ppermute x1 -> x14, starting transfers between devices: 3.45 us -> 21.4 us  [the longest x12 14.1 us: move(): return lax.ppermute(value, ('section', 'dp'), pairs)]
    pallas_call x0 -> x11, Pallas kernels: none -> 16.1 us  [local_call(): pl.pallas_call(kernel, out_shape=out_shape, in_specs=in_specs, out_specs=...]
    broadcast_in_dim x3 -> x0, local copies, waits for them, and re-layouts: 11.6 us -> none  [expand(): return jnp.repeat(jnp.repeat(flags, BLOCK, 0), BLOCK, 1)]
  transfers between devices with their start and end apart: 3 -> 14, of which waited for: 3 -> 8; matrix products, arithmetic and copies ran while one was open for 25% -> 9% of each run, Pallas kernels for 0% -> 8%
where the time goes in v3:
time: 135 us; the launch traced here: 133 us
  waiting for transfers between devices  77.2 us (57%)
  starting transfers between devices  21.4 us (16%)
  Pallas kernels  16.1 us (12%)
  other arithmetic  8.69 us (6%)
  local copies, waits for them, and re-layouts  6.95 us (5%)
  between operations  3.11 us (2%)
    ppermute x12, waiting for transfers between devices, move(): return lax.ppermute(value, ('section', 'dp'), pairs)  66.2 us
    pallas_call x11, Pallas kernels, local_call(): pl.pallas_call(kernel, out_shape=out_shape, in_specs=in_specs, out_specs=...  16.1 us
    ppermute x12, starting transfers between devices, move(): return lax.ppermute(value, ('section', 'dp'), pairs)  14.1 us
    ppermute x2, waiting for transfers between devices, to_layer_below(): return lax.ppermute(value, 'section', [(s, s - 1) for s in range(1, count)])  11 us
    ppermute x2, starting transfers between devices, to_layer_below(): return lax.ppermute(value, 'section', [(s, s - 1) for s in range(1, count)])  7.3 us
    add x3, other arithmetic, shards(): total = lax.optimization_barrier(total + decoded(value))  5.11 us
    slice x3, local copies, waits for them, and re-layouts, decoded(): value[-1:, :1].astype(jnp.float32)  3.57 us
    unnamed x8, local copies, waits for them, and re-layouts  3.24 us
  transfers between devices with their start and end apart: 14, of which 8 were waited for; matrix products, arithmetic and copies ran while one was open for 9% of the time, Pallas kernels for 8%

profile of v3, /device:TPU:1, one launch (start us, length us, event | category | flops | bytes accessed | tf_op | source)
XLA Modules:
  0.0 133.5 jit_solution(8882561899821621919)
XLA Ops:
  0.7 2.2 %copy-done = bf16[1,256,8192]{2,1,0:T(8,128)(2,1)S(1)} copy-done((bf16[1,256,8192]{2,1,0:T(8,128)(2,1)S(1)}, bf16[1,256,8192]{2,1,0:T(8,128)(2,1)}, u32[]{:S(2)}) %copy-start) | copy-done | bytes 4194328
  4.0 1.3 shard_map.59
  6.4 5.1 %collective-permute-start.1 = (bf16[512,1024]{1,0:T(8,128)(2,1)S(1)}, bf16[512,1024]{1,0:T(8,128)(2,1)S(1)}, u32[]{:S(2)}, u32[]{:S(2)}) collective-permute-start(bf16[512,1024]{1,0:T(8,128)(2,1)S(1)} %get-tuple-element.46), channel_id=1, source_target_pairs={{16,0},{32,16},{48,32},{64,48},{80,64},{96,80},{112,96},{128,112},... | collective-permute-start | bytes 3145736 | tf_op jit(solution)/shard_map/rows_below/ppermute | solution.py:40
  13.1 11.0 %collective-permute-done.1.refs_0_ = bf16[512,1024]{1,0:T(8,128)(2,1)S(1)} collective-permute-done((bf16[512,1024]{1,0:T(8,128)(2,1)S(1)}, bf16[512,1024]{1,0:T(8,128)(2,1)S(1)}, u32[]{:S(2)}, u32[]{:S(2)}) %collective-permute-start.1) | collective-permute-done | bytes 1048608 | tf_op jit(solution)/shard_map/rows_below/ppermute | solution.py:40
  24.1 2.9 %collective-permute-start.2 = (bf16[256,3072]{1,0:T(8,128)(2,1)S(1)}, bf16[256,3072]{1,0:T(8,128)(2,1)S(1)}, u32[]{:S(2)}, u32[]{:S(2)}) collective-permute-start(bf16[256,3072]{1,0:T(8,128)(2,1)S(1)} %get-tuple-element.47), channel_id=1, source_target_pairs={{0,8},{1,9},{2,10},{3,11},{4,12},{5,13},{6,14},{7,15},{8,0},{9,1},... | collective-permute-start | bytes 4718600 | tf_op jit(solution)/shard_map/ins/from2/ppermute | solution.py:35
  27.5 2.3 %collective-permute-start.4 = (bf16[512,1024]{1,0:T(8,128)(2,1)S(1)}, bf16[512,1024]{1,0:T(8,128)(2,1)S(1)}, u32[]{:S(2)}, u32[]{:S(2)}) collective-permute-start(bf16[512,1024]{1,0:T(8,128)(2,1)S(1)} %collective-permute-done.1.refs_0_), channel_id=1, source_target_pairs={{0,12},{1,13},{2,14},{3,15},{4,0},{5,1},{6,2},{7,3},{8,4},{9,5},{1... | collective-permute-start | bytes 3145736 | tf_op jit(solution)/shard_map/rows/from1/ppermute | solution.py:35
  29.8 1.4 %collective-permute-done.refs_1_ = bf16[256,3072]{1,0:T(8,128)(2,1)S(1)} collective-permute-done((bf16[256,3072]{1,0:T(8,128)(2,1)S(1)}, bf16[256,3072]{1,0:T(8,128)(2,1)S(1)}, u32[]{:S(2)}, u32[]{:S(2)}) %collective-permute-start) | collective-permute-done | bytes 1572896 | tf_op jit(solution)/shard_map/ins/from1/ppermute | solution.py:35
  31.2 19.1 %collective-permute-done.3.refs_3_ = bf16[256,3072]{1,0:T(8,128)(2,1)S(1)} collective-permute-done((bf16[256,3072]{1,0:T(8,128)(2,1)S(1)}, bf16[256,3072]{1,0:T(8,128)(2,1)S(1)}, u32[]{:S(2)}, u32[]{:S(2)}) %collective-permute-start.3) | collective-permute-done | bytes 1572896 | tf_op jit(solution)/shard_map/ins/from3/ppermute | solution.py:35
  50.6 2.2 %collective-permute-start.6 = (bf16[1024,1024]{1,0:T(8,128)(2,1)S(1)}, bf16[1024,1024]{1,0:T(8,128)(2,1)S(1)}, u32[]{:S(2)}, u32[]{:S(2)}) collective-permute-start(bf16[1024,1024]{1,0:T(8,128)(2,1)S(1)} %pad_maximum_fusion.refs_4_), channel_id=1, source_target_pairs={{16,0},{32,16},{48,32},{64,48},{80,64},{96,80},{112,96},{128,112},... | collective-permute-start | bytes 6291464 | tf_op jit(solution)/shard_map/cots_below/ppermute | solution.py:40
  52.8 19.8 %collective-permute-done.5.refs_3_ = bf16[512,1024]{1,0:T(8,128)(2,1)S(1)} collective-permute-done((bf16[512,1024]{1,0:T(8,128)(2,1)S(1)}, bf16[512,1024]{1,0:T(8,128)(2,1)S(1)}, u32[]{:S(2)}, u32[]{:S(2)}) %collective-permute-start.5) | collective-permute-done | bytes 1048608 | tf_op jit(solution)/shard_map/rows/from3/ppermute | solution.py:35
  72.6 1.5 %weight.4 = f32[520,1024]{1,0:T(8,128)S(1)} custom-call(bf16[256,3072]{1,0:T(8,128)(2,1)S(1)} %get-tuple-element.70.refs_0_, bf16[256,3072]{1,0:T(8,128)(2,1)S(1)} %collective-permute-done.refs_1_, bf16[256,3072]{1,0:T(8,128)(2,1)S(1)} %collective-permute-done.2.refs_2_, bf16[256,3072]{1,0:T(8,128)(2,1)S(1)} %collective-permute-done.3.refs_3_, ...), custom_call_target="tpu_custom_call" | custom-call | tf_op jit(solution)/shard_map/weight/pallas_call | solution.py:157
  74.3 1.5 %weight.5 = f32[520,1024]{1,0:T(8,128)S(1)} custom-call(bf16[256,3072]{1,0:T(8,128)(2,1)S(1)} %get-tuple-element.70.refs_0_, bf16[256,3072]{1,0:T(8,128)(2,1)S(1)} %collective-permute-done.refs_1_, bf16[256,3072]{1,0:T(8,128)(2,1)S(1)} %collective-permute-done.2.refs_2_, bf16[256,3072]{1,0:T(8,128)(2,1)S(1)} %collective-permute-done.3.refs_3_, ...), custom_call_target="tpu_custom_call" | custom-call | tf_op jit(solution)/shard_map/weight/pallas_call | solution.py:157
  76.1 1.5 %weight.6 = f32[520,1024]{1,0:T(8,128)S(1)} custom-call(bf16[256,3072]{1,0:T(8,128)(2,1)S(1)} %get-tuple-element.70.refs_0_, bf16[256,3072]{1,0:T(8,128)(2,1)S(1)} %collective-permute-done.refs_1_, bf16[256,3072]{1,0:T(8,128)(2,1)S(1)} %collective-permute-done.2.refs_2_, bf16[256,3072]{1,0:T(8,128)(2,1)S(1)} %collective-permute-done.3.refs_3_, ...), custom_call_target="tpu_custom_call" | custom-call | tf_op jit(solution)/shard_map/weight/pallas_call | solution.py:157
  78.7 2.3 %collective-permute-start.8 = (f16[520,1024]{1,0:T(8,128)(2,1)}, f16[520,1024]{1,0:T(8,128)(2,1)}, u32[]{:S(2)}, u32[]{:S(2)}) collective-permute-start(f16[520,1024]{1,0:T(8,128)(2,1)} %convert_element_type.32), channel_id=1, source_target_pairs={{0,3},{1,0},{2,1},{3,2},{4,7},{5,4},{6,5},{7,6},{8,11},{9,8},{10,9... | collective-permute-start | bytes 3194888 | tf_op jit(solution)/shard_map/weight/from1/ppermute | solution.py:35
  82.2 1.3 layer.4
  83.5 1.3 layer.5
  84.8 2.1 %collective-permute-start.11 = (bf16[256,2048]{1,0:T(8,128)(2,1)S(1)}, bf16[256,2048]{1,0:T(8,128)(2,1)S(1)}, u32[]{:S(2)}, u32[]{:S(2)}) collective-permute-start(bf16[256,2048]{1,0:T(8,128)(2,1)S(1)} %layer.5), channel_id=1, source_target_pairs={{0,3},{1,0},{2,1},{3,2},{4,7},{5,4},{6,5},{7,6},{8,11},{9,8},{10,9... | collective-permute-start | bytes 3145736 | tf_op jit(solution)/shard_map/layer/from1/ppermute | solution.py:35
  86.9 1.3 layer.6
  88.2 1.3 collective-permute-start.12
  89.5 1.3 layer.7.refs_0_
  90.8 1.3 weight.7
  92.1 12.6 %collective-permute-done.8 = f16[520,1024]{1,0:T(8,128)(2,1)} collective-permute-done((f16[520,1024]{1,0:T(8,128)(2,1)}, f16[520,1024]{1,0:T(8,128)(2,1)}, u32[]{:S(2)}, u32[]{:S(2)}) %collective-permute-start.8) | collective-permute-done | bytes 1064992 | tf_op jit(solution)/shard_map/weight/from1/ppermute | solution.py:35
  104.8 3.5 %collective-permute-done.10 = f16[520,1024]{1,0:T(8,128)(2,1)} collective-permute-done((f16[520,1024]{1,0:T(8,128)(2,1)S(1)}, f16[520,1024]{1,0:T(8,128)(2,1)}, u32[]{:S(2)}, u32[]{:S(2)}) %collective-permute-start.10) | collective-permute-done | bytes 1064992 | tf_op jit(solution)/shard_map/weight/from3/ppermute | solution.py:35
  108.2 1.2 slice.39
  110.1 1.2 slice.37
  113.9 1.7 %multiply_add_fusion.2 = f32[512,1024]{1,0:T(8,128)S(1)} fusion(f32[512,1024]{1,0:T(8,128)S(1)} %weight.7, f32[]{:T(128)} %bitcast.8, f16[520,1024]{1,0:T(8,128)(2,1)} %collective-permute-done.8), kind=kLoop, calls=%fused_computation.4 | loop fusion | flops 1572864 | bytes 5242884 | tf_op jit(solution)/shard_map/weight/add | solution.py:300
  115.6 1.7 %multiply_add_fusion.1 = f32[512,1024]{1,0:T(8,128)S(1)} fusion(f32[512,1024]{1,0:T(8,128)S(1)} %multiply_add_fusion.2, f32[]{:T(128)} %bitcast.9, f16[520,1024]{1,0:T(8,128)(2,1)} %collective-permute-done.9), kind=kLoop, calls=%fused_computation.3 | loop fusion | flops 1572864 | bytes 5242884 | tf_op jit(solution)/shard_map/weight/add | solution.py:300
  117.3 1.7 %multiply_add_fusion = f32[512,1024]{1,0:T(8,128)S(1)} fusion(f32[512,1024]{1,0:T(8,128)S(1)} %multiply_add_fusion.1, f32[]{:T(128)} %bitcast.10, f16[520,1024]{1,0:T(8,128)(2,1)} %collective-permute-done.10), kind=kLoop, calls=%fused_computation.2 | loop fusion | flops 1572864 | bytes 5242884 | tf_op jit(solution)/shard_map/weight/add | solution.py:300
  119.0 1.8 %multiply_bitcast_fusion = f32[1,512,1024]{2,1,0:T(8,128)} fusion(f32[512,1024]{1,0:T(8,128)S(1)} %multiply_add_fusion, bf16[512,1024]{1,0:T(8,128)(2,1)S(1)} %get-tuple-element.81), kind=kLoop, calls=%fused_computation.1 | loop fusion | flops 1572864 | bytes 5242880 | tf_op jit(solution)/shard_map/broadcast_in_dim | solution.py:303
  120.8 6.3 %collective-permute-done.11.refs_1_ = bf16[256,2048]{1,0:T(8,128)(2,1)S(1)} collective-permute-done((bf16[256,2048]{1,0:T(8,128)(2,1)S(1)}, bf16[256,2048]{1,0:T(8,128)(2,1)S(1)}, u32[]{:S(2)}, u32[]{:S(2)}) %collective-permute-start.11) | collective-permute-done | bytes 1048608 | tf_op jit(solution)/shard_map/layer/from1/ppermute | solution.py:35
  127.1 3.5 %collective-permute-done.13.refs_3_ = bf16[256,2048]{1,0:T(8,128)(2,1)S(1)} collective-permute-done((bf16[256,2048]{1,0:T(8,128)(2,1)S(1)}, bf16[256,2048]{1,0:T(8,128)(2,1)S(1)}, u32[]{:S(2)}, u32[]{:S(2)}) %collective-permute-start.13) | collective-permute-done | bytes 1048608 | tf_op jit(solution)/shard_map/layer/from3/ppermute | solution.py:35
  130.6 2.7 %join.1 = bf16[256,8192]{1,0:T(8,128)(2,1)} custom-call(s32[4]{0:T(128)S(1)} %broadcast_select_fusion.place_ref, bf16[256,2048]{1,0:T(8,128)(2,1)S(1)} %layer.7.refs_0_, bf16[256,2048]{1,0:T(8,128)(2,1)S(1)} %collective-permute-done.11.refs_1_, bf16[256,2048]{1,0:T(8,128)(2,1)S(1)} %collective-permute-done.12.refs_2_, ...), custom_call_target="tpu_custom_call" | custom-call | tf_op jit(solution)/shard_map/join/pallas_call | solution.py:157
  (31 shorter events, 8.5 us)
Async XLA Ops:
  0.7 2.2 %copy-start = (bf16[1,256,8192]{2,1,0:T(8,128)(2,1)S(1)}, bf16[1,256,8192]{2,1,0:T(8,128)(2,1)}, u32[]{:S(2)}) copy-start(bf16[1,256,8192]{2,1,0:T(8,128)(2,1)} %param.4) | copy-start | bytes 12582916
  2.9 1.0 copy-start.2
  4.0 1.3 copy-start.1
  4.0 1.3 copy-start.3
  6.4 17.7 %collective-permute-start.1 = (bf16[512,1024]{1,0:T(8,128)(2,1)S(1)}, bf16[512,1024]{1,0:T(8,128)(2,1)S(1)}, u32[]{:S(2)}, u32[]{:S(2)}) collective-permute-start(bf16[512,1024]{1,0:T(8,128)(2,1)S(1)} %get-tuple-element.46), channel_id=1, source_target_pairs={{16,0},{32,16},{48,32},{64,48},{80,64},{96,80},{112,96},{128,112},... | collective-permute-start | bytes 3145736 | tf_op jit(solution)/shard_map/rows_below/ppermute | solution.py:40
  11.6 19.6 %collective-permute-start = (bf16[256,3072]{1,0:T(8,128)(2,1)S(1)}, bf16[256,3072]{1,0:T(8,128)(2,1)S(1)}, u32[]{:S(2)}, u32[]{:S(2)}) collective-permute-start(bf16[256,3072]{1,0:T(8,128)(2,1)S(1)} %get-tuple-element.43), channel_id=1, source_target_pairs={{0,12},{1,13},{2,14},{3,15},{4,0},{5,1},{6,2},{7,3},{8,4},{9,5},{1... | collective-permute-start | bytes 4718600 | tf_op jit(solution)/shard_map/ins/from1/ppermute | solution.py:35
  12.6 37.6 %collective-permute-start.3 = (bf16[256,3072]{1,0:T(8,128)(2,1)S(1)}, bf16[256,3072]{1,0:T(8,128)(2,1)S(1)}, u32[]{:S(2)}, u32[]{:S(2)}) collective-permute-start(bf16[256,3072]{1,0:T(8,128)(2,1)S(1)} %get-tuple-element.48), channel_id=1, source_target_pairs={{0,4},{1,5},{2,6},{3,7},{4,8},{5,9},{6,10},{7,11},{8,12},{9,13},{1... | collective-permute-start | bytes 4718600 | tf_op jit(solution)/shard_map/ins/from3/ppermute | solution.py:35
  24.1 26.2 %collective-permute-start.2 = (bf16[256,3072]{1,0:T(8,128)(2,1)S(1)}, bf16[256,3072]{1,0:T(8,128)(2,1)S(1)}, u32[]{:S(2)}, u32[]{:S(2)}) collective-permute-start(bf16[256,3072]{1,0:T(8,128)(2,1)S(1)} %get-tuple-element.47), channel_id=1, source_target_pairs={{0,8},{1,9},{2,10},{3,11},{4,12},{5,13},{6,14},{7,15},{8,0},{9,1},... | collective-permute-start | bytes 4718600 | tf_op jit(solution)/shard_map/ins/from2/ppermute | solution.py:35
  27.1 45.5 %collective-permute-start.5 = (bf16[512,1024]{1,0:T(8,128)(2,1)S(1)}, bf16[512,1024]{1,0:T(8,128)(2,1)S(1)}, u32[]{:S(2)}, u32[]{:S(2)}) collective-permute-start(bf16[512,1024]{1,0:T(8,128)(2,1)S(1)} %collective-permute-done.1.refs_0_), channel_id=1, source_target_pairs={{0,4},{1,5},{2,6},{3,7},{4,8},{5,9},{6,10},{7,11},{8,12},{9,13},{1... | collective-permute-start | bytes 3145736 | tf_op jit(solution)/shard_map/rows/from3/ppermute | solution.py:35
  27.5 45.1 %collective-permute-start.4 = (bf16[512,1024]{1,0:T(8,128)(2,1)S(1)}, bf16[512,1024]{1,0:T(8,128)(2,1)S(1)}, u32[]{:S(2)}, u32[]{:S(2)}) collective-permute-start(bf16[512,1024]{1,0:T(8,128)(2,1)S(1)} %collective-permute-done.1.refs_0_), channel_id=1, source_target_pairs={{0,12},{1,13},{2,14},{3,15},{4,0},{5,1},{6,2},{7,3},{8,4},{9,5},{1... | collective-permute-start | bytes 3145736 | tf_op jit(solution)/shard_map/rows/from1/ppermute | solution.py:35
  50.3 28.5 %collective-permute-start.7 = (bf16[512,1024]{1,0:T(8,128)(2,1)S(1)}, bf16[512,1024]{1,0:T(8,128)(2,1)S(1)}, u32[]{:S(2)}, u32[]{:S(2)}) collective-permute-start(bf16[512,1024]{1,0:T(8,128)(2,1)S(1)} %collective-permute-done.1.refs_0_), channel_id=1, source_target_pairs={{0,8},{1,9},{2,10},{3,11},{4,12},{5,13},{6,14},{7,15},{8,0},{9,1},... | collective-permute-start | bytes 3145736 | tf_op jit(solution)/shard_map/rows/from2/ppermute | solution.py:35
  50.6 31.6 %collective-permute-start.6 = (bf16[1024,1024]{1,0:T(8,128)(2,1)S(1)}, bf16[1024,1024]{1,0:T(8,128)(2,1)S(1)}, u32[]{:S(2)}, u32[]{:S(2)}) collective-permute-start(bf16[1024,1024]{1,0:T(8,128)(2,1)S(1)} %pad_maximum_fusion.refs_4_), channel_id=1, source_target_pairs={{16,0},{32,16},{48,32},{64,48},{80,64},{96,80},{112,96},{128,112},... | collective-permute-start | bytes 6291464 | tf_op jit(solution)/shard_map/cots_below/ppermute | solution.py:40
  78.7 26.0 %collective-permute-start.8 = (f16[520,1024]{1,0:T(8,128)(2,1)}, f16[520,1024]{1,0:T(8,128)(2,1)}, u32[]{:S(2)}, u32[]{:S(2)}) collective-permute-start(f16[520,1024]{1,0:T(8,128)(2,1)} %convert_element_type.32), channel_id=1, source_target_pairs={{0,3},{1,0},{2,1},{3,2},{4,7},{5,4},{6,5},{7,6},{8,11},{9,8},{10,9... | collective-permute-start | bytes 3194888 | tf_op jit(solution)/shard_map/weight/from1/ppermute | solution.py:35
  81.1 23.7 %collective-permute-start.9 = (f16[520,1024]{1,0:T(8,128)(2,1)S(1)}, f16[520,1024]{1,0:T(8,128)(2,1)}, u32[]{:S(2)}, u32[]{:S(2)}) collective-permute-start(f16[520,1024]{1,0:T(8,128)(2,1)S(1)} %convert_element_type.30), channel_id=1, source_target_pairs={{0,2},{1,3},{2,0},{3,1},{4,6},{5,7},{6,4},{7,5},{8,10},{9,11},{10,... | collective-permute-start | bytes 3194888 | tf_op jit(solution)/shard_map/weight/from2/ppermute | solution.py:35
  81.6 26.6 %collective-permute-start.10 = (f16[520,1024]{1,0:T(8,128)(2,1)S(1)}, f16[520,1024]{1,0:T(8,128)(2,1)}, u32[]{:S(2)}, u32[]{:S(2)}) collective-permute-start(f16[520,1024]{1,0:T(8,128)(2,1)S(1)} %convert_element_type.31), channel_id=1, source_target_pairs={{0,1},{1,2},{2,3},{3,0},{4,5},{5,6},{6,7},{7,4},{8,9},{9,10},{10,1... | collective-permute-start | bytes 3194888 | tf_op jit(solution)/shard_map/weight/from3/ppermute | solution.py:35
  84.8 42.3 %collective-permute-start.11 = (bf16[256,2048]{1,0:T(8,128)(2,1)S(1)}, bf16[256,2048]{1,0:T(8,128)(2,1)S(1)}, u32[]{:S(2)}, u32[]{:S(2)}) collective-permute-start(bf16[256,2048]{1,0:T(8,128)(2,1)S(1)} %layer.5), channel_id=1, source_target_pairs={{0,3},{1,0},{2,1},{3,2},{4,7},{5,4},{6,5},{7,6},{8,11},{9,8},{10,9... | collective-permute-start | bytes 3145736 | tf_op jit(solution)/shard_map/layer/from1/ppermute | solution.py:35
  88.2 32.6 %collective-permute-start.12 = (bf16[256,2048]{1,0:T(8,128)(2,1)S(1)}, bf16[256,2048]{1,0:T(8,128)(2,1)S(1)}, u32[]{:S(2)}, u32[]{:S(2)}) collective-permute-start(bf16[256,2048]{1,0:T(8,128)(2,1)S(1)} %layer.6), channel_id=1, source_target_pairs={{0,2},{1,3},{2,0},{3,1},{4,6},{5,7},{6,4},{7,5},{8,10},{9,11},{10,... | collective-permute-start | bytes 3145736 | tf_op jit(solution)/shard_map/layer/from2/ppermute | solution.py:35
  104.8 25.9 %collective-permute-start.13 = (bf16[256,2048]{1,0:T(8,128)(2,1)S(1)}, bf16[256,2048]{1,0:T(8,128)(2,1)S(1)}, u32[]{:S(2)}, u32[]{:S(2)}) collective-permute-start(bf16[256,2048]{1,0:T(8,128)(2,1)S(1)} %layer.4), channel_id=1, source_target_pairs={{0,1},{1,2},{2,3},{3,0},{4,5},{5,6},{6,7},{7,4},{8,9},{9,10},{10,1... | collective-permute-start | bytes 3145736 | tf_op jit(solution)/shard_map/layer/from3/ppermute | solution.py:35

commit v4 on v3

--- a/solution.py
+++ b/solution.py
@@ -263,40 +263,36 @@
     with jax.named_scope("rows_below"):
         rows_above = to_layer_below(masked)
 
-    pieces[2], rows_above = lax.optimization_barrier((pieces[2], rows_above))
     with jax.named_scope("ins"):
         ins = exchange(pieces, True)
     cots = jnp.concatenate([piece[:, -features:] for piece in ins], 0)
     with jax.named_scope("cots_below"):
         cots_above = to_layer_below(cots)
     with jax.named_scope("rows"):
-        far = after(rows_above, ins[1], ins[3])
-        rows = exchange([rows_above, rows_above, far, rows_above], True)
-
-    ins, cots, rows[1], rows[3] = lax.optimization_barrier((ins, cots, rows[1], rows[3]))
+        rows = exchange([rows_above] * SIDE, True)
+
     parts = [None] * SIDE
     with jax.named_scope("weight"):
         parts[2] = weight_term(ins, cots, 2)
         parts[1] = weight_term(after(ins, parts[2]), cots, 1)
         parts[3] = weight_term(after(ins, parts[1]), cots, 3)
 
-    parts[1], parts[2], parts[3], rows[2] = lax.optimization_barrier((*parts[1:], rows[2]))
+    parts[1:], rows = lax.optimization_barrier((parts[1:], rows))
 
     terms = [None] * SIDE
     with jax.named_scope("layer"):
         terms[1] = layer_term(cots_above, rows, 1)
         terms[3] = layer_term(after(cots_above, terms[1]), rows, 3)
-        terms[2] = layer_term(after(cots_above, terms[3]), rows, 2)
+        sent = exchange(parts, False)
+        terms[2] = layer_term(after(cots_above, sent[1]), rows, 2)
         terms[0] = layer_term(after(cots_above, terms[2]), rows, 0)
         grads = exchange(terms, False)
     with jax.named_scope("join"):
         input_grad = join_columns(place, grads, (0, 1, 2, 3))
 
     with jax.named_scope("weight"):
-        parts[0] = weight_term(after(ins, terms), cots, 0)
-        sent = after(exchange(parts, False), terms)
-        total = sent[0]
-        for value in sent[1:]:
+        total = weight_term(after(ins, terms[3]), cots, 0)
+        for value in after(sent[1:], terms):
             total = lax.optimization_barrier(total + decoded(value))
         grad_scale = 1.0 / math.sqrt(cotangent.shape[0] * lax.axis_size("dp"))
         weight_grad = total * (mask.astype(jnp.float32) * grad_scale)

time: 135 us -> 128 us (0.948)
  the two profiles are of different devices: /device:TPU:1 before, /device:TPU:6 now
where the time goes in v4:
time: 128 us
  waiting for transfers between devices  68.1 us (53%)
  starting transfers between devices  22.9 us (18%)
  Pallas kernels  16 us (12%)
  other arithmetic  10.4 us (8%)
  local copies, waits for them, and re-layouts  6.95 us (5%)
  between operations  3.08 us (2%)
    ppermute x12, waiting for transfers between devices, move(): return lax.ppermute(value, ('section', 'dp'), pairs)  64.9 us
    ppermute x12, starting transfers between devices, move(): return lax.ppermute(value, ('section', 'dp'), pairs)  20.3 us
    pallas_call x11, Pallas kernels, local_call(): pl.pallas_call(kernel, out_shape=out_shape, in_specs=in_specs, out_specs=...  16 us
    add x3, other arithmetic, shards(): total = lax.optimization_barrier(total + decoded(value))  4.87 us
    slice x3, local copies, waits for them, and re-layouts, decoded(): value[-1:, :1].astype(jnp.float32)  3.57 us
    convert_element_type x3, other arithmetic, weight_term(): return part.astype(jnp.float16) if coded else part  3.48 us
    unnamed x8, local copies, waits for them, and re-layouts  3.24 us
    ppermute x2, waiting for transfers between devices, to_layer_below(): return lax.ppermute(value, 'section', [(s, s - 1) for s in range(1, count)])  3.21 us
  transfers between devices with their start and end apart: 14, of which 10 were waited for; matrix products, arithmetic and copies ran while one was open for 11% of the time, Pallas kernels for 9%

profile of v4, /device:TPU:6, one launch (start us, length us, event | category | flops | bytes accessed | tf_op | source)
XLA Modules:
  0.0 127.5 jit_solution(4889746348259515498)
XLA Ops:
  0.7 2.2 %copy-done = bf16[1,256,8192]{2,1,0:T(8,128)(2,1)S(1)} copy-done((bf16[1,256,8192]{2,1,0:T(8,128)(2,1)S(1)}, bf16[1,256,8192]{2,1,0:T(8,128)(2,1)}, u32[]{:S(2)}) %copy-start) | copy-done | bytes 4194328
  4.0 1.3 shard_map.59
  6.1 2.8 %collective-permute-start.1 = (bf16[256,3072]{1,0:T(8,128)(2,1)S(1)}, bf16[256,3072]{1,0:T(8,128)(2,1)S(1)}, u32[]{:S(2)}, u32[]{:S(2)}) collective-permute-start(bf16[256,3072]{1,0:T(8,128)(2,1)S(1)} %get-tuple-element.36), channel_id=1, source_target_pairs={{0,8},{1,9},{2,10},{3,11},{4,12},{5,13},{6,14},{7,15},{8,0},{9,1},... | collective-permute-start | bytes 4718600 | tf_op jit(solution)/shard_map/ins/from2/ppermute | solution.py:35
  10.5 1.3 %collective-permute-start.4 = (bf16[512,1024]{1,0:T(8,128)(2,1)S(1)}, bf16[512,1024]{1,0:T(8,128)(2,1)S(1)}, u32[]{:S(2)}, u32[]{:S(2)}) collective-permute-start(bf16[512,1024]{1,0:T(8,128)(2,1)S(1)} %get-tuple-element.47), channel_id=1, source_target_pairs={{16,0},{32,16},{48,32},{64,48},{80,64},{96,80},{112,96},{128,112},... | collective-permute-start | bytes 3145736 | tf_op jit(solution)/shard_map/rows_below/ppermute | solution.py:40
  11.9 3.2 %collective-permute-done.4.refs_0_ = bf16[512,1024]{1,0:T(8,128)(2,1)S(1)} collective-permute-done((bf16[512,1024]{1,0:T(8,128)(2,1)S(1)}, bf16[512,1024]{1,0:T(8,128)(2,1)S(1)}, u32[]{:S(2)}, u32[]{:S(2)}) %collective-permute-start.4) | collective-permute-done | bytes 1048608 | tf_op jit(solution)/shard_map/rows_below/ppermute | solution.py:40
  16.0 2.9 %collective-permute-start.6 = (bf16[512,1024]{1,0:T(8,128)(2,1)S(1)}, bf16[512,1024]{1,0:T(8,128)(2,1)S(1)}, u32[]{:S(2)}, u32[]{:S(2)}) collective-permute-start(bf16[512,1024]{1,0:T(8,128)(2,1)S(1)} %collective-permute-done.4.refs_0_), channel_id=1, source_target_pairs={{0,8},{1,9},{2,10},{3,11},{4,12},{5,13},{6,14},{7,15},{8,0},{9,1},... | collective-permute-start | bytes 3145736 | tf_op jit(solution)/shard_map/rows/from2/ppermute | solution.py:35
  18.8 8.1 %collective-permute-done.refs_1_ = bf16[256,3072]{1,0:T(8,128)(2,1)S(1)} collective-permute-done((bf16[256,3072]{1,0:T(8,128)(2,1)S(1)}, bf16[256,3072]{1,0:T(8,128)(2,1)S(1)}, u32[]{:S(2)}, u32[]{:S(2)}) %collective-permute-start) | collective-permute-done | bytes 1572896 | tf_op jit(solution)/shard_map/ins/from1/ppermute | solution.py:35
  27.0 17.3 %collective-permute-done.1.refs_2_ = bf16[256,3072]{1,0:T(8,128)(2,1)S(1)} collective-permute-done((bf16[256,3072]{1,0:T(8,128)(2,1)S(1)}, bf16[256,3072]{1,0:T(8,128)(2,1)S(1)}, u32[]{:S(2)}, u32[]{:S(2)}) %collective-permute-start.1) | collective-permute-done | bytes 1572896 | tf_op jit(solution)/shard_map/ins/from2/ppermute | solution.py:35
  45.0 1.3 %collective-permute-start.3 = (bf16[1024,1024]{1,0:T(8,128)(2,1)S(1)}, bf16[1024,1024]{1,0:T(8,128)(2,1)S(1)}, u32[]{:S(2)}, u32[]{:S(2)}) collective-permute-start(bf16[1024,1024]{1,0:T(8,128)(2,1)S(1)} %pad_maximum_fusion.refs_4_), channel_id=1, source_target_pairs={{16,0},{32,16},{48,32},{64,48},{80,64},{96,80},{112,96},{128,112},... | collective-permute-start | bytes 6291464 | tf_op jit(solution)/shard_map/cots_below/ppermute | solution.py:40
  46.3 1.5 %weight.4 = f32[520,1024]{1,0:T(8,128)S(1)} custom-call(bf16[256,3072]{1,0:T(8,128)(2,1)S(1)} %get-tuple-element.53.refs_0_, bf16[256,3072]{1,0:T(8,128)(2,1)S(1)} %collective-permute-done.refs_1_, bf16[256,3072]{1,0:T(8,128)(2,1)S(1)} %collective-permute-done.1.refs_2_, bf16[256,3072]{1,0:T(8,128)(2,1)S(1)} %collective-permute-done.2.refs_3_, ...), custom_call_target="tpu_custom_call" | custom-call | tf_op jit(solution)/shard_map/weight/pallas_call | solution.py:157
  49.0 1.5 %weight.5 = f32[520,1024]{1,0:T(8,128)S(1)} custom-call(bf16[256,3072]{1,0:T(8,128)(2,1)S(1)} %get-tuple-element.53.refs_0_, bf16[256,3072]{1,0:T(8,128)(2,1)S(1)} %collective-permute-done.refs_1_, bf16[256,3072]{1,0:T(8,128)(2,1)S(1)} %collective-permute-done.1.refs_2_, bf16[256,3072]{1,0:T(8,128)(2,1)S(1)} %collective-permute-done.2.refs_3_, ...), custom_call_target="tpu_custom_call" | custom-call | tf_op jit(solution)/shard_map/weight/pallas_call | solution.py:157
  51.6 1.5 %weight.6 = f32[520,1024]{1,0:T(8,128)S(1)} custom-call(bf16[256,3072]{1,0:T(8,128)(2,1)S(1)} %get-tuple-element.53.refs_0_, bf16[256,3072]{1,0:T(8,128)(2,1)S(1)} %collective-permute-done.refs_1_, bf16[256,3072]{1,0:T(8,128)(2,1)S(1)} %collective-permute-done.1.refs_2_, bf16[256,3072]{1,0:T(8,128)(2,1)S(1)} %collective-permute-done.2.refs_3_, ...), custom_call_target="tpu_custom_call" | custom-call | tf_op jit(solution)/shard_map/weight/pallas_call | solution.py:157
  54.3 1.6 %collective-permute-done.7.refs_3_ = bf16[512,1024]{1,0:T(8,128)(2,1)S(1)} collective-permute-done((bf16[512,1024]{1,0:T(8,128)(2,1)S(1)}, bf16[512,1024]{1,0:T(8,128)(2,1)S(1)}, u32[]{:S(2)}, u32[]{:S(2)}) %collective-permute-start.7) | collective-permute-done | bytes 1048608 | tf_op jit(solution)/shard_map/rows/from3/ppermute | solution.py:35
  55.9 10.8 %collective-permute-done.5.refs_1_ = bf16[512,1024]{1,0:T(8,128)(2,1)S(1)} collective-permute-done((bf16[512,1024]{1,0:T(8,128)(2,1)S(1)}, bf16[512,1024]{1,0:T(8,128)(2,1)S(1)}, u32[]{:S(2)}, u32[]{:S(2)}) %collective-permute-start.5) | collective-permute-done | bytes 1048608 | tf_op jit(solution)/shard_map/rows/from1/ppermute | solution.py:35
  66.7 7.3 %collective-permute-start.8 = (f16[520,1024]{1,0:T(8,128)(2,1)}, f16[520,1024]{1,0:T(8,128)(2,1)}, u32[]{:S(2)}, u32[]{:S(2)}) collective-permute-start(f16[520,1024]{1,0:T(8,128)(2,1)} %convert_element_type.32), channel_id=1, source_target_pairs={{0,3},{1,0},{2,1},{3,2},{4,7},{5,4},{6,5},{7,6},{8,11},{9,8},{10,9... | collective-permute-start | bytes 3194888 | tf_op jit(solution)/shard_map/layer/from1/ppermute | solution.py:35
  74.1 1.3 %collective-permute-start.9 = (f16[520,1024]{1,0:T(8,128)(2,1)}, f16[520,1024]{1,0:T(8,128)(2,1)}, u32[]{:S(2)}, u32[]{:S(2)}) collective-permute-start(f16[520,1024]{1,0:T(8,128)(2,1)} %convert_element_type.30), channel_id=1, source_target_pairs={{0,2},{1,3},{2,0},{3,1},{4,6},{5,7},{6,4},{7,5},{8,10},{9,11},{10,... | collective-permute-start | bytes 3194888 | tf_op jit(solution)/shard_map/layer/from2/ppermute | solution.py:35
  75.7 1.3 %layer.4 = bf16[256,2048]{1,0:T(8,128)(2,1)S(1)} custom-call(bf16[1024,1024]{1,0:T(8,128)(2,1)S(1)} %collective-permute-done.3.cots_ref, bf16[512,1024]{1,0:T(8,128)(2,1)S(1)} %collective-permute-done.4.refs_0_, bf16[512,1024]{1,0:T(8,128)(2,1)S(1)} %collective-permute-done.5.refs_1_, bf16[512,1024]{1,0:T(8,128)(2,1)S(1)} %collective-permute-done.6.refs_2_, ...), custom_call_target="tpu_custom_call" | custom-call | tf_op jit(solution)/shard_map/layer/pallas_call | solution.py:157
  77.0 2.0 %collective-permute-start.13 = (bf16[256,2048]{1,0:T(8,128)(2,1)S(1)}, bf16[256,2048]{1,0:T(8,128)(2,1)S(1)}, u32[]{:S(2)}, u32[]{:S(2)}) collective-permute-start(bf16[256,2048]{1,0:T(8,128)(2,1)S(1)} %layer.4), channel_id=1, source_target_pairs={{0,1},{1,2},{2,3},{3,0},{4,5},{5,6},{6,7},{7,4},{8,9},{9,10},{10,1... | collective-permute-start | bytes 3145736 | tf_op jit(solution)/shard_map/layer/from3/ppermute | solution.py:35
  78.9 1.3 %layer.5 = bf16[256,2048]{1,0:T(8,128)(2,1)S(1)} custom-call(bf16[1024,1024]{1,0:T(8,128)(2,1)S(1)} %collective-permute-done.3.cots_ref, bf16[512,1024]{1,0:T(8,128)(2,1)S(1)} %collective-permute-done.4.refs_0_, bf16[512,1024]{1,0:T(8,128)(2,1)S(1)} %collective-permute-done.5.refs_1_, bf16[512,1024]{1,0:T(8,128)(2,1)S(1)} %collective-permute-done.6.refs_2_, ...), custom_call_target="tpu_custom_call" | custom-call | tf_op jit(solution)/shard_map/layer/pallas_call | solution.py:157
  80.2 1.4 %collective-permute-start.11 = (bf16[256,2048]{1,0:T(8,128)(2,1)S(1)}, bf16[256,2048]{1,0:T(8,128)(2,1)S(1)}, u32[]{:S(2)}, u32[]{:S(2)}) collective-permute-start(bf16[256,2048]{1,0:T(8,128)(2,1)S(1)} %layer.5), channel_id=1, source_target_pairs={{0,3},{1,0},{2,1},{3,2},{4,7},{5,4},{6,5},{7,6},{8,11},{9,8},{10,9... | collective-permute-start | bytes 3145736 | tf_op jit(solution)/shard_map/layer/from1/ppermute | solution.py:35
  81.6 16.7 %collective-permute-done.8 = f16[520,1024]{1,0:T(8,128)(2,1)} collective-permute-done((f16[520,1024]{1,0:T(8,128)(2,1)}, f16[520,1024]{1,0:T(8,128)(2,1)}, u32[]{:S(2)}, u32[]{:S(2)}) %collective-permute-start.8) | collective-permute-done | bytes 1064992 | tf_op jit(solution)/shard_map/layer/from1/ppermute | solution.py:35
  98.3 1.3 %layer.6 = bf16[256,2048]{1,0:T(8,128)(2,1)S(1)} custom-call(bf16[1024,1024]{1,0:T(8,128)(2,1)S(1)} %collective-permute-done.3.cots_ref, bf16[512,1024]{1,0:T(8,128)(2,1)S(1)} %collective-permute-done.4.refs_0_, bf16[512,1024]{1,0:T(8,128)(2,1)S(1)} %collective-permute-done.5.refs_1_, bf16[512,1024]{1,0:T(8,128)(2,1)S(1)} %collective-permute-done.6.refs_2_, ...), custom_call_target="tpu_custom_call" | custom-call | tf_op jit(solution)/shard_map/layer/pallas_call | solution.py:157
  99.7 1.3 %layer.7.refs_0_ = bf16[256,2048]{1,0:T(8,128)(2,1)S(1)} custom-call(bf16[1024,1024]{1,0:T(8,128)(2,1)S(1)} %collective-permute-done.3.cots_ref, bf16[512,1024]{1,0:T(8,128)(2,1)S(1)} %collective-permute-done.4.refs_0_, bf16[512,1024]{1,0:T(8,128)(2,1)S(1)} %collective-permute-done.5.refs_1_, bf16[512,1024]{1,0:T(8,128)(2,1)S(1)} %collective-permute-done.6.refs_2_, ...), custom_call_target="tpu_custom_call" | custom-call | tf_op jit(solution)/shard_map/layer/pallas_call | solution.py:157
  101.0 1.3 collective-permute-done.10
  107.9 1.3 %weight.7 = f32[512,1024]{1,0:T(8,128)S(1)} custom-call(bf16[256,3072]{1,0:T(8,128)(2,1)S(1)} %get-tuple-element.53.refs_0_, bf16[256,3072]{1,0:T(8,128)(2,1)S(1)} %collective-permute-done.refs_1_, bf16[256,3072]{1,0:T(8,128)(2,1)S(1)} %collective-permute-done.1.refs_2_, bf16[256,3072]{1,0:T(8,128)(2,1)S(1)} %collective-permute-done.2.refs_3_, ...), custom_call_target="tpu_custom_call" | custom-call | tf_op jit(solution)/shard_map/weight/pallas_call | solution.py:157
  109.2 1.7 %multiply_add_fusion.2 = f32[512,1024]{1,0:T(8,128)S(1)} fusion(f32[512,1024]{1,0:T(8,128)S(1)} %weight.7, f32[]{:T(128)} %bitcast.8, f16[520,1024]{1,0:T(8,128)(2,1)} %collective-permute-done.8), kind=kLoop, calls=%fused_computation.4 | loop fusion | flops 1572864 | bytes 5242884 | tf_op jit(solution)/shard_map/weight/add | solution.py:296
  110.9 1.6 %multiply_add_fusion.1 = f32[512,1024]{1,0:T(8,128)S(1)} fusion(f32[512,1024]{1,0:T(8,128)S(1)} %multiply_add_fusion.2, f32[]{:T(128)} %bitcast.9, f16[520,1024]{1,0:T(8,128)(2,1)} %collective-permute-done.9), kind=kLoop, calls=%fused_computation.3 | loop fusion | flops 1572864 | bytes 5242884 | tf_op jit(solution)/shard_map/weight/add | solution.py:296
  112.5 1.6 %multiply_add_fusion = f32[512,1024]{1,0:T(8,128)S(1)} fusion(f32[512,1024]{1,0:T(8,128)S(1)} %multiply_add_fusion.1, f32[]{:T(128)} %bitcast.10, f16[520,1024]{1,0:T(8,128)(2,1)} %collective-permute-done.10), kind=kLoop, calls=%fused_computation.2 | loop fusion | flops 1572864 | bytes 5242884 | tf_op jit(solution)/shard_map/weight/add | solution.py:296
  114.1 1.8 %multiply_bitcast_fusion = f32[1,512,1024]{2,1,0:T(8,128)} fusion(f32[512,1024]{1,0:T(8,128)S(1)} %multiply_add_fusion, bf16[512,1024]{1,0:T(8,128)(2,1)S(1)} %get-tuple-element.65), kind=kLoop, calls=%fused_computation.1 | loop fusion | flops 1572864 | bytes 5242880 | tf_op jit(solution)/shard_map/broadcast_in_dim | solution.py:299
  115.9 4.8 %collective-permute-done.11.refs_1_ = bf16[256,2048]{1,0:T(8,128)(2,1)S(1)} collective-permute-done((bf16[256,2048]{1,0:T(8,128)(2,1)S(1)}, bf16[256,2048]{1,0:T(8,128)(2,1)S(1)}, u32[]{:S(2)}, u32[]{:S(2)}) %collective-permute-start.11) | collective-permute-done | bytes 1048608 | tf_op jit(solution)/shard_map/layer/from1/ppermute | solution.py:35
  120.7 4.0 %collective-permute-done.12.refs_2_ = bf16[256,2048]{1,0:T(8,128)(2,1)S(1)} collective-permute-done((bf16[256,2048]{1,0:T(8,128)(2,1)S(1)}, bf16[256,2048]{1,0:T(8,128)(2,1)S(1)}, u32[]{:S(2)}, u32[]{:S(2)}) %collective-permute-start.12) | collective-permute-done | bytes 1048608 | tf_op jit(solution)/shard_map/layer/from2/ppermute | solution.py:35
  124.7 2.7 %join.1 = bf16[256,8192]{1,0:T(8,128)(2,1)} custom-call(s32[4]{0:T(128)S(1)} %broadcast_select_fusion.place_ref, bf16[256,2048]{1,0:T(8,128)(2,1)S(1)} %layer.7.refs_0_, bf16[256,2048]{1,0:T(8,128)(2,1)S(1)} %collective-permute-done.11.refs_1_, bf16[256,2048]{1,0:T(8,128)(2,1)S(1)} %collective-permute-done.12.refs_2_, ...), custom_call_target="tpu_custom_call" | custom-call | tf_op jit(solution)/shard_map/join/pallas_call | solution.py:157
  (31 shorter events, 12.5 us)
Async XLA Ops:
  0.7 2.2 %copy-start = (bf16[1,256,8192]{2,1,0:T(8,128)(2,1)S(1)}, bf16[1,256,8192]{2,1,0:T(8,128)(2,1)}, u32[]{:S(2)}) copy-start(bf16[1,256,8192]{2,1,0:T(8,128)(2,1)} %param.4) | copy-start | bytes 12582916
  2.9 1.0 copy-start.2
  4.0 5.4 %copy-start.1 = (bf16[1,512,1024]{2,1,0:T(8,128)(2,1)S(1)}, bf16[1,512,1024]{2,1,0:T(8,128)(2,1)}, u32[]{:S(2)}) copy-start(bf16[1,512,1024]{2,1,0:T(8,128)(2,1)} %param.6) | copy-start | bytes 3145732
  4.0 5.4 %copy-start.3 = (s32[1,128,16]{1,2,0:T(8,128)S(1)}, s32[1,128,16]{1,2,0:T(8,128)}, u32[]{:S(2)}) copy-start(s32[1,128,16]{1,2,0:T(8,128)} %param.7) | copy-start | bytes 24580
  5.2 21.7 %collective-permute-start = (bf16[256,3072]{1,0:T(8,128)(2,1)S(1)}, bf16[256,3072]{1,0:T(8,128)(2,1)S(1)}, u32[]{:S(2)}, u32[]{:S(2)}) collective-permute-start(bf16[256,3072]{1,0:T(8,128)(2,1)S(1)} %get-tuple-element.35), channel_id=1, source_target_pairs={{0,12},{1,13},{2,14},{3,15},{4,0},{5,1},{6,2},{7,3},{8,4},{9,5},{1... | collective-permute-start | bytes 4718600 | tf_op jit(solution)/shard_map/ins/from1/ppermute | solution.py:35
  6.1 38.2 %collective-permute-start.1 = (bf16[256,3072]{1,0:T(8,128)(2,1)S(1)}, bf16[256,3072]{1,0:T(8,128)(2,1)S(1)}, u32[]{:S(2)}, u32[]{:S(2)}) collective-permute-start(bf16[256,3072]{1,0:T(8,128)(2,1)S(1)} %get-tuple-element.36), channel_id=1, source_target_pairs={{0,8},{1,9},{2,10},{3,11},{4,12},{5,13},{6,14},{7,15},{8,0},{9,1},... | collective-permute-start | bytes 4718600 | tf_op jit(solution)/shard_map/ins/from2/ppermute | solution.py:35
  9.0 35.7 %collective-permute-start.2 = (bf16[256,3072]{1,0:T(8,128)(2,1)S(1)}, bf16[256,3072]{1,0:T(8,128)(2,1)S(1)}, u32[]{:S(2)}, u32[]{:S(2)}) collective-permute-start(bf16[256,3072]{1,0:T(8,128)(2,1)S(1)} %get-tuple-element.37), channel_id=1, source_target_pairs={{0,4},{1,5},{2,6},{3,7},{4,8},{5,9},{6,10},{7,11},{8,12},{9,13},{1... | collective-permute-start | bytes 4718600 | tf_op jit(solution)/shard_map/ins/from3/ppermute | solution.py:35
  10.5 4.6 %collective-permute-start.4 = (bf16[512,1024]{1,0:T(8,128)(2,1)S(1)}, bf16[512,1024]{1,0:T(8,128)(2,1)S(1)}, u32[]{:S(2)}, u32[]{:S(2)}) collective-permute-start(bf16[512,1024]{1,0:T(8,128)(2,1)S(1)} %get-tuple-element.47), channel_id=1, source_target_pairs={{16,0},{32,16},{48,32},{64,48},{80,64},{96,80},{112,96},{128,112},... | collective-permute-start | bytes 3145736 | tf_op jit(solution)/shard_map/rows_below/ppermute | solution.py:40
  15.1 40.9 %collective-permute-start.7 = (bf16[512,1024]{1,0:T(8,128)(2,1)S(1)}, bf16[512,1024]{1,0:T(8,128)(2,1)S(1)}, u32[]{:S(2)}, u32[]{:S(2)}) collective-permute-start(bf16[512,1024]{1,0:T(8,128)(2,1)S(1)} %collective-permute-done.4.refs_0_), channel_id=1, source_target_pairs={{0,4},{1,5},{2,6},{3,7},{4,8},{5,9},{6,10},{7,11},{8,12},{9,13},{1... | collective-permute-start | bytes 3145736 | tf_op jit(solution)/shard_map/rows/from3/ppermute | solution.py:35
  16.0 40.0 %collective-permute-start.6 = (bf16[512,1024]{1,0:T(8,128)(2,1)S(1)}, bf16[512,1024]{1,0:T(8,128)(2,1)S(1)}, u32[]{:S(2)}, u32[]{:S(2)}) collective-permute-start(bf16[512,1024]{1,0:T(8,128)(2,1)S(1)} %collective-permute-done.4.refs_0_), channel_id=1, source_target_pairs={{0,8},{1,9},{2,10},{3,11},{4,12},{5,13},{6,14},{7,15},{8,0},{9,1},... | collective-permute-start | bytes 3145736 | tf_op jit(solution)/shard_map/rows/from2/ppermute | solution.py:35
  26.9 39.8 %collective-permute-start.5 = (bf16[512,1024]{1,0:T(8,128)(2,1)S(1)}, bf16[512,1024]{1,0:T(8,128)(2,1)S(1)}, u32[]{:S(2)}, u32[]{:S(2)}) collective-permute-start(bf16[512,1024]{1,0:T(8,128)(2,1)S(1)} %collective-permute-done.4.refs_0_), channel_id=1, source_target_pairs={{0,12},{1,13},{2,14},{3,15},{4,0},{5,1},{6,2},{7,3},{8,4},{9,5},{1... | collective-permute-start | bytes 3145736 | tf_op jit(solution)/shard_map/rows/from1/ppermute | solution.py:35
  45.0 30.7 %collective-permute-start.3 = (bf16[1024,1024]{1,0:T(8,128)(2,1)S(1)}, bf16[1024,1024]{1,0:T(8,128)(2,1)S(1)}, u32[]{:S(2)}, u32[]{:S(2)}) collective-permute-start(bf16[1024,1024]{1,0:T(8,128)(2,1)S(1)} %pad_maximum_fusion.refs_4_), channel_id=1, source_target_pairs={{16,0},{32,16},{48,32},{64,48},{80,64},{96,80},{112,96},{128,112},... | collective-permute-start | bytes 6291464 | tf_op jit(solution)/shard_map/cots_below/ppermute | solution.py:40
  66.7 31.6 %collective-permute-start.8 = (f16[520,1024]{1,0:T(8,128)(2,1)}, f16[520,1024]{1,0:T(8,128)(2,1)}, u32[]{:S(2)}, u32[]{:S(2)}) collective-permute-start(f16[520,1024]{1,0:T(8,128)(2,1)} %convert_element_type.32), channel_id=1, source_target_pairs={{0,3},{1,0},{2,1},{3,2},{4,7},{5,4},{6,5},{7,6},{8,11},{9,8},{10,9... | collective-permute-start | bytes 3194888 | tf_op jit(solution)/shard_map/layer/from1/ppermute | solution.py:35
  74.1 26.9 %collective-permute-start.9 = (f16[520,1024]{1,0:T(8,128)(2,1)}, f16[520,1024]{1,0:T(8,128)(2,1)}, u32[]{:S(2)}, u32[]{:S(2)}) collective-permute-start(f16[520,1024]{1,0:T(8,128)(2,1)} %convert_element_type.30), channel_id=1, source_target_pairs={{0,2},{1,3},{2,0},{3,1},{4,6},{5,7},{6,4},{7,5},{8,10},{9,11},{10,... | collective-permute-start | bytes 3194888 | tf_op jit(solution)/shard_map/layer/from2/ppermute | solution.py:35
  75.4 26.9 %collective-permute-start.10 = (f16[520,1024]{1,0:T(8,128)(2,1)}, f16[520,1024]{1,0:T(8,128)(2,1)}, u32[]{:S(2)}, u32[]{:S(2)}) collective-permute-start(f16[520,1024]{1,0:T(8,128)(2,1)} %convert_element_type.31), channel_id=1, source_target_pairs={{0,1},{1,2},{2,3},{3,0},{4,5},{5,6},{6,7},{7,4},{8,9},{9,10},{10,1... | collective-permute-start | bytes 3194888 | tf_op jit(solution)/shard_map/layer/from3/ppermute | solution.py:35
  77.0 43.7 %collective-permute-start.13 = (bf16[256,2048]{1,0:T(8,128)(2,1)S(1)}, bf16[256,2048]{1,0:T(8,128)(2,1)S(1)}, u32[]{:S(2)}, u32[]{:S(2)}) collective-permute-start(bf16[256,2048]{1,0:T(8,128)(2,1)S(1)} %layer.4), channel_id=1, source_target_pairs={{0,1},{1,2},{2,3},{3,0},{4,5},{5,6},{6,7},{7,4},{8,9},{9,10},{10,1... | collective-permute-start | bytes 3145736 | tf_op jit(solution)/shard_map/layer/from3/ppermute | solution.py:35
  80.2 40.5 %collective-permute-start.11 = (bf16[256,2048]{1,0:T(8,128)(2,1)S(1)}, bf16[256,2048]{1,0:T(8,128)(2,1)S(1)}, u32[]{:S(2)}, u32[]{:S(2)}) collective-permute-start(bf16[256,2048]{1,0:T(8,128)(2,1)S(1)} %layer.5), channel_id=1, source_target_pairs={{0,3},{1,0},{2,1},{3,2},{4,7},{5,4},{6,5},{7,6},{8,11},{9,8},{10,9... | collective-permute-start | bytes 3145736 | tf_op jit(solution)/shard_map/layer/from1/ppermute | solution.py:35
  99.6 25.1 %collective-permute-start.12 = (bf16[256,2048]{1,0:T(8,128)(2,1)S(1)}, bf16[256,2048]{1,0:T(8,128)(2,1)S(1)}, u32[]{:S(2)}, u32[]{:S(2)}) collective-permute-start(bf16[256,2048]{1,0:T(8,128)(2,1)S(1)} %layer.6), channel_id=1, source_target_pairs={{0,2},{1,3},{2,0},{3,1},{4,6},{5,7},{6,4},{7,5},{8,10},{9,11},{10,... | collective-permute-start | bytes 3145736 | tf_op jit(solution)/shard_map/layer/from2/ppermute | solution.py:35

commit v5 on v4

--- a/solution.py
+++ b/solution.py
@@ -130,8 +130,8 @@
 
 
 def weight_kernel(m, coded, *refs):
-    ins, cots_ref, out_ref = refs[:SIDE], refs[SIDE], refs[SIDE + 1]
-    features = out_ref.shape[1]
+    ins, cots_ref, outs = refs[:SIDE], refs[SIDE], refs[SIDE + 1 :]
+    features = cots_ref.shape[1]
     width = (ins[0].shape[1] - features) // SIDE
     part = lax.dot_general(
         jnp.concatenate([i[:, m * width : (m + 1) * width] for i in ins], 0),
@@ -143,10 +143,12 @@
         peak = jnp.max(jnp.abs(part), axis=0, keepdims=True)
         peak = jnp.max(peak, axis=1, keepdims=True)
         exponent = jnp.clip(jnp.floor(14.0 - jnp.log2(peak)), -100.0, 100.0)
-        out_ref[:width, :] = part * jnp.exp2(exponent)
-        out_ref[width:, :] = jnp.broadcast_to(exponent, (TAIL, features))
+        rows = width // len(outs)
+        for n, out_ref in enumerate(outs):
+            out_ref[:rows, :] = part[n * rows : (n + 1) * rows] * jnp.exp2(exponent)
+            out_ref[rows:, :] = jnp.broadcast_to(exponent, (TAIL, features))
     else:
-        out_ref[...] = part
+        outs[0][...] = part
 
 
 def local_call(
@@ -162,7 +164,7 @@
         scratch_shapes=scratch,
         input_output_aliases=aliases,
         compiler_params=pltpu.CompilerParams(vmem_limit_bytes=mib * 1024 * 1024),
-        cost_estimate=pl.CostEstimate(flops=0, bytes_accessed=0, transcendentals=0),
+        cost_estimate=pl.CostEstimate(flops=flops, bytes_accessed=0, transcendentals=0),
     )(*operands)
 
 
@@ -207,7 +209,7 @@
     tokens, features = cots.shape[0] // SIDE, cots.shape[1]
     width = rows[0].shape[0]
     out = jax.ShapeDtypeStruct((tokens, SIDE * width), jnp.bfloat16)
-    flops = 2 * tokens * features * width * SIDE
+    flops = 0
     return local_call(
         functools.partial(layer_kernel, j),
         [out],
@@ -223,11 +225,14 @@
     tokens, features = cots.shape
     width = (ins[0].shape[1] - features) // SIDE
     coded = m != 0
-    part = jax.ShapeDtypeStruct((width + (TAIL if coded else 0), features), jnp.float32)
+    count = 2 if m == 2 else 1
+    rows = width // count + (TAIL if coded else 0)
+    parts = [jax.ShapeDtypeStruct((rows, features), jnp.float32)] * count
     kernel = functools.partial(weight_kernel, m, coded)
-    flops = 2 * tokens * features * width
-    part = local_call(kernel, [part], [*ins, cots], [VMEM] * (SIDE + 1), [VMEM], (), flops)[0]
-    return part.astype(jnp.float16) if coded else part
+    flops = 16 * tokens * features * width
+    return local_call(
+        kernel, parts, [*ins, cots], [VMEM] * (SIDE + 1), [VMEM] * count, (), flops
+    )
 
 
 def exchange(pieces, first):
@@ -243,7 +248,19 @@
 
 
 def decoded(value):
-    return value[:-TAIL].astype(jnp.float32) * jnp.exp2(-value[-1:, :1].astype(jnp.float32))
+    return value[:-TAIL].astype(jnp.float32) * jnp.exp2(-value[-1:].astype(jnp.float32))
+
+
+def combined(own, passed, first):
+    rows = passed.shape[0] - TAIL
+    own_exponent, passed_exponent = own[-1:], passed[-1:].astype(jnp.float32)
+    exponent = jnp.minimum(own_exponent, passed_exponent) - 1.0
+    own_scale = jnp.exp2(exponent - own_exponent)
+    added = passed[:rows].astype(jnp.float32) * jnp.exp2(exponent - passed_exponent)
+    top, bottom = own[:rows] * own_scale, own[rows : 2 * rows] * own_scale
+    top, bottom = (top + added, bottom) if first else (top, bottom + added)
+    tail = jnp.broadcast_to(exponent, (TAIL, own.shape[1]))
+    return jnp.concatenate([top, bottom, tail], 0).astype(jnp.float16)
 
 
 def shards(layer_input, key_cotangent, key_weight, block_mask):
@@ -269,33 +286,50 @@
     with jax.named_scope("cots_below"):
         cots_above = to_layer_below(cots)
     with jax.named_scope("rows"):
-        rows = exchange([rows_above] * SIDE, True)
-
-    parts = [None] * SIDE
+        before = move(rows_above, True, 1)
+        behind = move(rows_above, True, -1)
+
     with jax.named_scope("weight"):
-        parts[2] = weight_term(ins, cots, 2)
-        parts[1] = weight_term(after(ins, parts[2]), cots, 1)
-        parts[3] = weight_term(after(ins, parts[1]), cots, 3)
-
-    parts[1:], rows = lax.optimization_barrier((parts[1:], rows))
+        halves = [part.astype(jnp.float16) for part in weight_term(ins, cots, 2)]
+        (part_on,) = weight_term(after(ins, halves), cots, 1)
+        (part_back,) = weight_term(after(ins, part_on), cots, 3)
+    halves, part_on, part_back, before, behind = lax.optimization_barrier(
+        (halves, part_on, part_back, before, behind)
+    )
+    with jax.named_scope("weight_far"):
+        passed_on = move(halves[0], False, 1)
+        passed_back = move(halves[1], False, -1)
+
+    half = before.shape[0] // 2
+    with jax.named_scope("rows_far"):
+        far = [move(before[:half], True, 1), move(behind[half:], True, -1)]
+    part_on, part_back, far, cots_above = lax.optimization_barrier(
+        (part_on, part_back, far, cots_above)
+    )
+    rows = [rows_above, behind, *far, before]
+    with jax.named_scope("weight_near"):
+        sent = [
+            move(combined(part_on, passed_on, True), False, 1),
+            move(combined(part_back, passed_back, False), False, -1),
+        ]
 
     terms = [None] * SIDE
     with jax.named_scope("layer"):
         terms[1] = layer_term(cots_above, rows, 1)
         terms[3] = layer_term(after(cots_above, terms[1]), rows, 3)
-        sent = exchange(parts, False)
-        terms[2] = layer_term(after(cots_above, sent[1]), rows, 2)
+        terms[2] = layer_term(after(cots_above, terms[3]), rows, 2)
         terms[0] = layer_term(after(cots_above, terms[2]), rows, 0)
         grads = exchange(terms, False)
-    with jax.named_scope("join"):
-        input_grad = join_columns(place, grads, (0, 1, 2, 3))
-
     with jax.named_scope("weight"):
-        total = weight_term(after(ins, terms[3]), cots, 0)
-        for value in after(sent[1:], terms):
+        (total,) = weight_term(after(ins, terms[2]), cots, 0)
+        for value in after(sent, terms):
             total = lax.optimization_barrier(total + decoded(value))
         grad_scale = 1.0 / math.sqrt(cotangent.shape[0] * lax.axis_size("dp"))
         weight_grad = total * (mask.astype(jnp.float32) * grad_scale)
+    with jax.named_scope("join"):
+        grads = after(grads, weight_grad)
+        input_grad = join_columns(place, grads, (0, 2))
+        input_grad = join_columns(place, grads, (1, 3), input_grad)
     return (weight_grad[None], input_grad[None])
 
 

time: 128 us -> 122 us (0.953)
  the two profiles are of different devices: /device:TPU:6 before, /device:TPU:1 now
where the time goes in v5:
time: 122 us; the launch traced here: 121 us
  waiting for transfers between devices  62.8 us (51%)
  starting transfers between devices  22.7 us (19%)
  Pallas kernels  17.2 us (14%)
  other arithmetic  10.6 us (9%)
  local copies, waits for them, and re-layouts  6.13 us (5%)
    ppermute x14, waiting for transfers between devices, move(): return lax.ppermute(value, ('section', 'dp'), pairs)  47.4 us
    pallas_call x12, Pallas kernels, local_call(): pl.pallas_call(kernel, out_shape=out_shape, in_specs=in_specs, out_specs=...  17.2 us
    ppermute x14, starting transfers between devices, move(): return lax.ppermute(value, ('section', 'dp'), pairs)  15.9 us
    ppermute x2, waiting for transfers between devices, to_layer_below(): return lax.ppermute(value, 'section', [(s, s - 1) for s in range(1, count)])  15.4 us
    ppermute x2, starting transfers between devices, to_layer_below(): return lax.ppermute(value, 'section', [(s, s - 1) for s in range(1, count)])  6.73 us
    unnamed x26, local copies, waits for them, and re-layouts  5.91 us
    add x2, other arithmetic, shards(): total = lax.optimization_barrier(total + decoded(value))  3.42 us
    concatenate x2, other arithmetic, combined(): return jnp.concatenate([top, bottom, tail], 0).astype(jnp.float16)  2.65 us
  transfers between devices with their start and end apart: 16, of which 10 were waited for; matrix products, arithmetic and copies ran while one was open for 7% of the time, Pallas kernels for 10%

profile of v5, /device:TPU:1, one launch (start us, length us, event | category | flops | bytes accessed | tf_op | source)
XLA Modules:
  0.0 120.6 jit_solution(12705828690904383057)
XLA Ops:
  0.7 2.2 %copy-done = bf16[1,256,8192]{2,1,0:T(8,128)(2,1)S(1)} copy-done((bf16[1,256,8192]{2,1,0:T(8,128)(2,1)S(1)}, bf16[1,256,8192]{2,1,0:T(8,128)(2,1)}, u32[]{:S(2)}) %copy-start) | copy-done | bytes 4194328
  4.0 1.3 %shard_map.59 = (bf16[256,3072]{1,0:T(8,128)(2,1)S(1)}, bf16[256,3072]{1,0:T(8,128)(2,1)S(1)}, bf16[256,3072]{1,0:T(8,128)(2,1)S(1)}, bf16[256,3072]{1,0:T(8,128)(2,1)S(1)}) custom-call(s32[4]{0:T(128)S(1)} %broadcast_select_fusion.place_ref, bf16[256,1024]{1,0:T(8,128)(2,1)S(1)} %bitcast.19, bf16[256,8192]{1,0:T(8,128)(2,1)S(1)} %bitcast.17), custom_call_target="tpu_custom_call" | custom-call | tf_op jit(solution)/shard_map/pallas_call | solution.py:159
  5.2 3.6 %collective-permute-start = (bf16[256,3072]{1,0:T(8,128)(2,1)S(1)}, bf16[256,3072]{1,0:T(8,128)(2,1)S(1)}, u32[]{:S(2)}, u32[]{:S(2)}) collective-permute-start(bf16[256,3072]{1,0:T(8,128)(2,1)S(1)} %get-tuple-element.44), channel_id=1, source_target_pairs={{0,12},{1,13},{2,14},{3,15},{4,0},{5,1},{6,2},{7,3},{8,4},{9,5},{1... | collective-permute-start | bytes 4718600 | tf_op jit(solution)/shard_map/ins/from1/ppermute | solution.py:35
  11.1 3.3 %collective-permute-start.3 = (bf16[512,1024]{1,0:T(8,128)(2,1)S(1)}, bf16[512,1024]{1,0:T(8,128)(2,1)S(1)}, u32[]{:S(2)}, u32[]{:S(2)}) collective-permute-start(bf16[512,1024]{1,0:T(8,128)(2,1)S(1)} %get-tuple-element.58), channel_id=1, source_target_pairs={{16,0},{32,16},{48,32},{64,48},{80,64},{96,80},{112,96},{128,112},... | collective-permute-start | bytes 3145736 | tf_op jit(solution)/shard_map/rows_below/ppermute | solution.py:40
  14.4 14.2 %collective-permute-done.3.refs_0_ = bf16[512,1024]{1,0:T(8,128)(2,1)S(1)} collective-permute-done((bf16[512,1024]{1,0:T(8,128)(2,1)S(1)}, bf16[512,1024]{1,0:T(8,128)(2,1)S(1)}, u32[]{:S(2)}, u32[]{:S(2)}) %collective-permute-start.3) | collective-permute-done | bytes 1048608 | tf_op jit(solution)/shard_map/rows_below/ppermute | solution.py:40
  28.6 2.7 %collective-permute-start.5 = (bf16[512,1024]{1,0:T(8,128)(2,1)S(1)}, bf16[512,1024]{1,0:T(8,128)(2,1)S(1)}, u32[]{:S(2)}, u32[]{:S(2)}) collective-permute-start(bf16[512,1024]{1,0:T(8,128)(2,1)S(1)} %collective-permute-done.3.refs_0_), channel_id=1, source_target_pairs={{0,12},{1,13},{2,14},{3,15},{4,0},{5,1},{6,2},{7,3},{8,4},{9,5},{1... | collective-permute-start | bytes 3145736 | tf_op jit(solution)/shard_map/rows/ppermute | solution.py:35
  31.4 11.7 %collective-permute-done.refs_1_ = bf16[256,3072]{1,0:T(8,128)(2,1)S(1)} collective-permute-done((bf16[256,3072]{1,0:T(8,128)(2,1)S(1)}, bf16[256,3072]{1,0:T(8,128)(2,1)S(1)}, u32[]{:S(2)}, u32[]{:S(2)}) %collective-permute-start) | collective-permute-done | bytes 1572896 | tf_op jit(solution)/shard_map/ins/from1/ppermute | solution.py:35
  43.2 3.6 %collective-permute-done.2.refs_3_ = bf16[256,3072]{1,0:T(8,128)(2,1)S(1)} collective-permute-done((bf16[256,3072]{1,0:T(8,128)(2,1)S(1)}, bf16[256,3072]{1,0:T(8,128)(2,1)S(1)}, u32[]{:S(2)}, u32[]{:S(2)}) %collective-permute-start.2) | collective-permute-done | bytes 1572896 | tf_op jit(solution)/shard_map/ins/from3/ppermute | solution.py:35
  47.0 3.5 %collective-permute-start.8 = (bf16[1024,1024]{1,0:T(8,128)(2,1)S(1)}, bf16[1024,1024]{1,0:T(8,128)(2,1)S(1)}, u32[]{:S(2)}, u32[]{:S(2)}) collective-permute-start(bf16[1024,1024]{1,0:T(8,128)(2,1)S(1)} %pad_maximum_fusion.refs_4_), channel_id=1, source_target_pairs={{16,0},{32,16},{48,32},{64,48},{80,64},{96,80},{112,96},{128,112},... | collective-permute-start | bytes 6291464 | tf_op jit(solution)/shard_map/cots_below/ppermute | solution.py:40
  50.5 1.5 %weight.4 = (f32[264,1024]{1,0:T(8,128)S(1)}, f32[264,1024]{1,0:T(8,128)S(1)}) custom-call(bf16[256,3072]{1,0:T(8,128)(2,1)S(1)} %get-tuple-element.68.refs_0_, bf16[256,3072]{1,0:T(8,128)(2,1)S(1)} %collective-permute-done.refs_1_, bf16[256,3072]{1,0:T(8,128)(2,1)S(1)} %collective-permute-done.1.refs_2_, ...), custom_call_target="tpu_custom_call" | custom-call | flops 8589934592 | tf_op jit(solution)/shard_map/weight/pallas_call | solution.py:159
  53.5 1.5 %weight.5 = f32[520,1024]{1,0:T(8,128)S(1)} custom-call(bf16[256,3072]{1,0:T(8,128)(2,1)S(1)} %get-tuple-element.68.refs_0_, bf16[256,3072]{1,0:T(8,128)(2,1)S(1)} %collective-permute-done.refs_1_, bf16[256,3072]{1,0:T(8,128)(2,1)S(1)} %copy-done.8, bf16[256,3072]{1,0:T(8,128)(2,1)S(1)} %collective-permute-done.2.refs_3_, ...), custom_call_target="tpu_custom_call" | custom-call | flops 8589934592 | tf_op jit(solution)/shard_map/weight/pallas_call | solution.py:159
  55.0 1.5 %weight.6 = f32[520,1024]{1,0:T(8,128)S(1)} custom-call(bf16[256,3072]{1,0:T(8,128)(2,1)S(1)} %get-tuple-element.68.refs_0_, bf16[256,3072]{1,0:T(8,128)(2,1)S(1)} %collective-permute-done.refs_1_, bf16[256,3072]{1,0:T(8,128)(2,1)S(1)} %copy-done.8, bf16[256,3072]{1,0:T(8,128)(2,1)S(1)} %collective-permute-done.2.refs_3_, ...), custom_call_target="tpu_custom_call" | custom-call | flops 8589934592 | tf_op jit(solution)/shard_map/weight/pallas_call | solution.py:159
  56.5 1.5 %collective-permute-done.4.refs_4_ = bf16[512,1024]{1,0:T(8,128)(2,1)S(1)} collective-permute-done((bf16[512,1024]{1,0:T(8,128)(2,1)S(1)}, bf16[512,1024]{1,0:T(8,128)(2,1)S(1)}, u32[]{:S(2)}, u32[]{:S(2)}) %collective-permute-start.4) | collective-permute-done | bytes 1048608 | tf_op jit(solution)/shard_map/rows/ppermute | solution.py:35
  60.6 1.8 %collective-permute-start.11 = (f16[264,1024]{1,0:T(8,128)(2,1)S(1)}, f16[264,1024]{1,0:T(8,128)(2,1)S(1)}, u32[]{:S(2)}, u32[]{:S(2)}) collective-permute-start(f16[264,1024]{1,0:T(8,128)(2,1)S(1)} %convert_element_type.36), channel_id=1, source_target_pairs={{0,3},{1,0},{2,1},{3,2},{4,7},{5,4},{6,5},{7,6},{8,11},{9,8},{10,9... | collective-permute-start | bytes 1622024 | tf_op jit(solution)/shard_map/weight_far/ppermute | solution.py:35
  62.3 6.0 %collective-permute-done.7.refs_3_ = bf16[256,1024]{1,0:T(8,128)(2,1)S(1)} collective-permute-done((bf16[256,1024]{1,0:T(8,128)(2,1)S(1)}, bf16[256,1024]{1,0:T(8,128)(2,1)S(1)}, u32[]{:S(2)}, u32[]{:S(2)}) %collective-permute-start.7) | collective-permute-done | bytes 524320 | tf_op jit(solution)/shard_map/rows_far/ppermute | solution.py:35
  68.3 6.3 %collective-permute-done.6.refs_2_ = bf16[256,1024]{1,0:T(8,128)(2,1)S(1)} collective-permute-done((bf16[256,1024]{1,0:T(8,128)(2,1)S(1)}, bf16[256,1024]{1,0:T(8,128)(2,1)S(1)}, u32[]{:S(2)}, u32[]{:S(2)}) %collective-permute-start.6) | collective-permute-done | bytes 524320 | tf_op jit(solution)/shard_map/rows_far/ppermute | solution.py:35
  76.6 1.4 %pad_maximum_fusion.1 = f16[520,1024]{1,0:T(8,128)(2,1)} fusion(f16[8,1024]{1,0:T(8,128)(2,1)S(1)} %broadcast_in_dim.21, f16[256,1024]{1,0:T(8,128)(2,1)S(1)} %get-tuple-element.92, f16[256,1024]{1,0:T(8,128)(2,1)S(1)} %get-tuple-element.93), kind=kLoop, calls=%fused_computation.4 | loop fusion | flops 1064960 | bytes 2129920 | tf_op jit(solution)/shard_map/weight_near/concatenate | solution.py:263
  78.0 1.3 %pad_maximum_fusion.2 = f16[520,1024]{1,0:T(8,128)(2,1)} fusion(f16[8,1024]{1,0:T(8,128)(2,1)S(1)} %broadcast_in_dim.23, f16[256,1024]{1,0:T(8,128)(2,1)S(1)} %get-tuple-element.89, f16[256,1024]{1,0:T(8,128)(2,1)S(1)} %get-tuple-element.88), kind=kLoop, calls=%fused_computation.5 | loop fusion | flops 1064960 | bytes 2129920 | tf_op jit(solution)/shard_map/weight_near/concatenate | solution.py:263
  79.3 2.7 %collective-permute-start.12 = (f16[520,1024]{1,0:T(8,128)(2,1)}, f16[520,1024]{1,0:T(8,128)(2,1)}, u32[]{:S(2)}, u32[]{:S(2)}) collective-permute-start(f16[520,1024]{1,0:T(8,128)(2,1)} %pad_maximum_fusion.2), channel_id=1, source_target_pairs={{0,3},{1,0},{2,1},{3,2},{4,7},{5,4},{6,5},{7,6},{8,11},{9,8},{10,9... | collective-permute-start | bytes 3194888 | tf_op jit(solution)/shard_map/weight_near/ppermute | solution.py:35
  82.0 1.3 %layer.4 = bf16[256,2048]{1,0:T(8,128)(2,1)S(1)} custom-call(bf16[1024,1024]{1,0:T(8,128)(2,1)S(1)} %collective-permute-done.8.cots_ref, bf16[512,1024]{1,0:T(8,128)(2,1)S(1)} %collective-permute-done.3.refs_0_, bf16[512,1024]{1,0:T(8,128)(2,1)S(1)} %collective-permute-done.5.refs_1_, bf16[256,1024]{1,0:T(8,128)(2,1)S(1)} %collective-permute-done.6.refs_2_, ...), custom_call_target="tpu_custom_call" | custom-call | tf_op jit(solution)/shard_map/layer/pallas_call | solution.py:159
  83.3 1.3 %layer.5 = bf16[256,2048]{1,0:T(8,128)(2,1)S(1)} custom-call(bf16[1024,1024]{1,0:T(8,128)(2,1)S(1)} %collective-permute-done.8.cots_ref, bf16[512,1024]{1,0:T(8,128)(2,1)S(1)} %collective-permute-done.3.refs_0_, bf16[512,1024]{1,0:T(8,128)(2,1)S(1)} %collective-permute-done.5.refs_1_, bf16[256,1024]{1,0:T(8,128)(2,1)S(1)} %collective-permute-done.6.refs_2_, ...), custom_call_target="tpu_custom_call" | custom-call | tf_op jit(solution)/shard_map/layer/pallas_call | solution.py:159
  84.6 1.3 %layer.6 = bf16[256,2048]{1,0:T(8,128)(2,1)S(1)} custom-call(bf16[1024,1024]{1,0:T(8,128)(2,1)S(1)} %collective-permute-done.8.cots_ref, bf16[512,1024]{1,0:T(8,128)(2,1)S(1)} %collective-permute-done.3.refs_0_, bf16[512,1024]{1,0:T(8,128)(2,1)S(1)} %collective-permute-done.5.refs_1_, bf16[256,1024]{1,0:T(8,128)(2,1)S(1)} %collective-permute-done.6.refs_2_, ...), custom_call_target="tpu_custom_call" | custom-call | tf_op jit(solution)/shard_map/layer/pallas_call | solution.py:159
  87.5 1.3 %layer.7.refs_0_ = bf16[256,2048]{1,0:T(8,128)(2,1)S(1)} custom-call(bf16[1024,1024]{1,0:T(8,128)(2,1)S(1)} %collective-permute-done.8.cots_ref, bf16[512,1024]{1,0:T(8,128)(2,1)S(1)} %collective-permute-done.3.refs_0_, bf16[512,1024]{1,0:T(8,128)(2,1)S(1)} %collective-permute-done.5.refs_1_, bf16[256,1024]{1,0:T(8,128)(2,1)S(1)} %collective-permute-done.6.refs_2_, ...), custom_call_target="tpu_custom_call" | custom-call | tf_op jit(solution)/shard_map/layer/pallas_call | solution.py:159
  88.9 1.4 %copy-done.11 = bf16[256,3072]{1,0:T(8,128)(2,1)S(1)} copy-done((bf16[256,3072]{1,0:T(8,128)(2,1)S(1)}, bf16[256,3072]{1,0:T(8,128)(2,1)}, u32[]{:S(2)}) %copy-start.11) | copy-done | bytes 1572888
  90.3 1.3 %weight.7 = f32[512,1024]{1,0:T(8,128)S(1)} custom-call(bf16[256,3072]{1,0:T(8,128)(2,1)S(1)} %copy-done.4, bf16[256,3072]{1,0:T(8,128)(2,1)S(1)} %copy-done.6, bf16[256,3072]{1,0:T(8,128)(2,1)S(1)} %copy-done.9, bf16[256,3072]{1,0:T(8,128)(2,1)S(1)} %copy-done.11, bf16[1024,1024]{1,0:T(8,128)(2,1)S(1)} %pad_maximum_fusion.refs_4_), custom_call_target="tpu_custom_call" | custom-call | flops 8589934592 | tf_op jit(solution)/shard_map/weight/pallas_call | solution.py:159
  91.5 13.2 %collective-permute-done.10 = f16[520,1024]{1,0:T(8,128)(2,1)} collective-permute-done((f16[520,1024]{1,0:T(8,128)(2,1)}, f16[520,1024]{1,0:T(8,128)(2,1)}, u32[]{:S(2)}, u32[]{:S(2)}) %collective-permute-start.10) | collective-permute-done | bytes 1064992 | tf_op jit(solution)/shard_map/weight_near/ppermute | solution.py:35
  106.2 1.7 %multiply_add_fusion.1 = f32[512,1024]{1,0:T(8,128)S(1)} fusion(f32[512,1024]{1,0:T(8,128)S(1)} %weight.7, f32[1024]{0:T(1024)S(1)} %bitcast.27, f16[520,1024]{1,0:T(8,128)(2,1)} %collective-permute-done.10), kind=kLoop, calls=%fused_computation.3 | loop fusion | flops 1572864 | bytes 5246976 | tf_op jit(solution)/shard_map/weight/add | solution.py:326
  108.6 1.7 %multiply_add_fusion = f32[512,1024]{1,0:T(8,128)S(1)} fusion(f32[512,1024]{1,0:T(8,128)S(1)} %multiply_add_fusion.1, f32[1024]{0:T(1024)S(1)} %bitcast.28, f16[520,1024]{1,0:T(8,128)(2,1)} %collective-permute-done.12), kind=kLoop, calls=%fused_computation.2 | loop fusion | flops 1572864 | bytes 5246976 | tf_op jit(solution)/shard_map/weight/add | solution.py:326
  110.4 1.8 %multiply_multiply_fusion = f32[512,1024]{1,0:T(8,128)} fusion(f32[512,1024]{1,0:T(8,128)S(1)} %multiply_add_fusion, bf16[512,1024]{1,0:T(8,128)(2,1)S(1)} %get-tuple-element.79), kind=kLoop, calls=%fused_computation.1 | loop fusion | flops 1572864 | bytes 5242880 | tf_op jit(solution)/shard_map/weight/mul | solution.py:328
  112.2 4.4 %collective-permute-done.13.refs_0_ = bf16[256,2048]{1,0:T(8,128)(2,1)S(1)} collective-permute-done((bf16[256,2048]{1,0:T(8,128)(2,1)S(1)}, bf16[256,2048]{1,0:T(8,128)(2,1)S(1)}, u32[]{:S(2)}, u32[]{:S(2)}) %collective-permute-start.13) | collective-permute-done | bytes 1048608 | tf_op jit(solution)/shard_map/layer/from1/ppermute | solution.py:35
  116.6 1.9 %join.2.refs_2_ = bf16[256,8192]{1,0:T(8,128)(2,1)} custom-call(s32[4]{0:T(128)S(1)} %broadcast_select_fusion.place_ref, bf16[256,2048]{1,0:T(8,128)(2,1)S(1)} %layer.7.refs_0_, bf16[256,2048]{1,0:T(8,128)(2,1)S(1)} %collective-permute-done.14.refs_1_), custom_call_target="tpu_custom_call" | custom-call | tf_op jit(solution)/shard_map/join/pallas_call | solution.py:159
  118.5 1.9 %join.3 = bf16[256,8192]{1,0:T(8,128)(2,1)} custom-call(s32[4]{0:T(128)S(1)} %broadcast_select_fusion.place_ref, bf16[256,2048]{1,0:T(8,128)(2,1)S(1)} %collective-permute-done.13.refs_0_, bf16[256,2048]{1,0:T(8,128)(2,1)S(1)} %collective-permute-done.15.refs_1_, bf16[256,8192]{1,0:T(8,128)(2,1)} %join.2.refs_2_), custom_call_target="tpu_custom_call", output_to_operand_aliasing={{}: (3, {})} | custom-call | tf_op jit(solution)/shard_map/join/pallas_call | solution.py:159
  (64 shorter events, 13.4 us)
Async XLA Ops:
  0.7 2.2 %copy-start = (bf16[1,256,8192]{2,1,0:T(8,128)(2,1)S(1)}, bf16[1,256,8192]{2,1,0:T(8,128)(2,1)}, u32[]{:S(2)}) copy-start(bf16[1,256,8192]{2,1,0:T(8,128)(2,1)} %param.4) | copy-start | bytes 12582916
  2.9 1.0 copy-start.2
  4.0 6.0 %copy-start.1 = (bf16[1,512,1024]{2,1,0:T(8,128)(2,1)S(1)}, bf16[1,512,1024]{2,1,0:T(8,128)(2,1)}, u32[]{:S(2)}) copy-start(bf16[1,512,1024]{2,1,0:T(8,128)(2,1)} %param.6) | copy-start | bytes 3145732
  4.0 6.0 %copy-start.12 = (s32[1,128,16]{1,2,0:T(8,128)S(1)}, s32[1,128,16]{1,2,0:T(8,128)}, u32[]{:S(2)}) copy-start(s32[1,128,16]{1,2,0:T(8,128)} %param.7) | copy-start | bytes 24580
  5.2 49.7 %copy-start.3 = (bf16[256,3072]{1,0:T(8,128)(2,1)}, bf16[256,3072]{1,0:T(8,128)(2,1)S(1)}, u32[]{:S(2)}) copy-start(bf16[256,3072]{1,0:T(8,128)(2,1)S(1)} %get-tuple-element.68.refs_0_) | copy-start | bytes 4718596
  5.2 37.9 %collective-permute-start = (bf16[256,3072]{1,0:T(8,128)(2,1)S(1)}, bf16[256,3072]{1,0:T(8,128)(2,1)S(1)}, u32[]{:S(2)}, u32[]{:S(2)}) collective-permute-start(bf16[256,3072]{1,0:T(8,128)(2,1)S(1)} %get-tuple-element.44), channel_id=1, source_target_pairs={{0,12},{1,13},{2,14},{3,15},{4,0},{5,1},{6,2},{7,3},{8,4},{9,5},{1... | collective-permute-start | bytes 4718600 | tf_op jit(solution)/shard_map/ins/from1/ppermute | solution.py:35
  8.9 34.3 %collective-permute-start.1 = (bf16[256,3072]{1,0:T(8,128)(2,1)S(1)}, bf16[256,3072]{1,0:T(8,128)(2,1)S(1)}, u32[]{:S(2)}, u32[]{:S(2)}) collective-permute-start(bf16[256,3072]{1,0:T(8,128)(2,1)S(1)} %get-tuple-element.45), channel_id=1, source_target_pairs={{0,8},{1,9},{2,10},{3,11},{4,12},{5,13},{6,14},{7,15},{8,0},{9,1},... | collective-permute-start | bytes 4718600 | tf_op jit(solution)/shard_map/ins/from2/ppermute | solution.py:35
  9.2 37.6 %collective-permute-start.2 = (bf16[256,3072]{1,0:T(8,128)(2,1)S(1)}, bf16[256,3072]{1,0:T(8,128)(2,1)S(1)}, u32[]{:S(2)}, u32[]{:S(2)}) collective-permute-start(bf16[256,3072]{1,0:T(8,128)(2,1)S(1)} %get-tuple-element.46), channel_id=1, source_target_pairs={{0,4},{1,5},{2,6},{3,7},{4,8},{5,9},{6,10},{7,11},{8,12},{9,13},{1... | collective-permute-start | bytes 4718600 | tf_op jit(solution)/shard_map/ins/from3/ppermute | solution.py:35
  11.1 17.5 %collective-permute-start.3 = (bf16[512,1024]{1,0:T(8,128)(2,1)S(1)}, bf16[512,1024]{1,0:T(8,128)(2,1)S(1)}, u32[]{:S(2)}, u32[]{:S(2)}) collective-permute-start(bf16[512,1024]{1,0:T(8,128)(2,1)S(1)} %get-tuple-element.58), channel_id=1, source_target_pairs={{16,0},{32,16},{48,32},{64,48},{80,64},{96,80},{112,96},{128,112},... | collective-permute-start | bytes 3145736 | tf_op jit(solution)/shard_map/rows_below/ppermute | solution.py:40
  28.6 27.9 %collective-permute-start.5 = (bf16[512,1024]{1,0:T(8,128)(2,1)S(1)}, bf16[512,1024]{1,0:T(8,128)(2,1)S(1)}, u32[]{:S(2)}, u32[]{:S(2)}) collective-permute-start(bf16[512,1024]{1,0:T(8,128)(2,1)S(1)} %collective-permute-done.3.refs_0_), channel_id=1, source_target_pairs={{0,12},{1,13},{2,14},{3,15},{4,0},{5,1},{6,2},{7,3},{8,4},{9,5},{1... | collective-permute-start | bytes 3145736 | tf_op jit(solution)/shard_map/rows/ppermute | solution.py:35
  31.4 26.7 %collective-permute-start.4 = (bf16[512,1024]{1,0:T(8,128)(2,1)S(1)}, bf16[512,1024]{1,0:T(8,128)(2,1)S(1)}, u32[]{:S(2)}, u32[]{:S(2)}) collective-permute-start(bf16[512,1024]{1,0:T(8,128)(2,1)S(1)} %collective-permute-done.3.refs_0_), channel_id=1, source_target_pairs={{0,4},{1,5},{2,6},{3,7},{4,8},{5,9},{6,10},{7,11},{8,12},{9,13},{1... | collective-permute-start | bytes 3145736 | tf_op jit(solution)/shard_map/rows/ppermute | solution.py:35
  43.1 11.9 %copy-start.5 = (bf16[256,3072]{1,0:T(8,128)(2,1)}, bf16[256,3072]{1,0:T(8,128)(2,1)S(1)}, u32[]{:S(2)}) copy-start(bf16[256,3072]{1,0:T(8,128)(2,1)S(1)} %collective-permute-done.refs_1_) | copy-start | bytes 4718596
  43.2 7.4 %copy-start.7 = (bf16[256,3072]{1,0:T(8,128)(2,1)}, bf16[256,3072]{1,0:T(8,128)(2,1)S(1)}, u32[]{:S(2)}) copy-start(bf16[256,3072]{1,0:T(8,128)(2,1)S(1)} %collective-permute-done.1.refs_2_) | copy-start | bytes 4718596
  46.8 8.2 %copy-start.10 = (bf16[256,3072]{1,0:T(8,128)(2,1)}, bf16[256,3072]{1,0:T(8,128)(2,1)S(1)}, u32[]{:S(2)}) copy-start(bf16[256,3072]{1,0:T(8,128)(2,1)S(1)} %collective-permute-done.2.refs_3_) | copy-start | bytes 4718596
  47.0 28.7 %collective-permute-start.8 = (bf16[1024,1024]{1,0:T(8,128)(2,1)S(1)}, bf16[1024,1024]{1,0:T(8,128)(2,1)S(1)}, u32[]{:S(2)}, u32[]{:S(2)}) collective-permute-start(bf16[1024,1024]{1,0:T(8,128)(2,1)S(1)} %pad_maximum_fusion.refs_4_), channel_id=1, source_target_pairs={{16,0},{32,16},{48,32},{64,48},{80,64},{96,80},{112,96},{128,112},... | collective-permute-start | bytes 6291464 | tf_op jit(solution)/shard_map/cots_below/ppermute | solution.py:40
  52.0 1.4 %copy-start.8 = (bf16[256,3072]{1,0:T(8,128)(2,1)S(1)}, bf16[256,3072]{1,0:T(8,128)(2,1)}, u32[]{:S(2)}) copy-start(bf16[256,3072]{1,0:T(8,128)(2,1)} %copy-done.7) | copy-start | bytes 4718596
  58.0 17.7 %collective-permute-start.9 = (f16[264,1024]{1,0:T(8,128)(2,1)S(1)}, f16[264,1024]{1,0:T(8,128)(2,1)S(1)}, u32[]{:S(2)}, u32[]{:S(2)}) collective-permute-start(f16[264,1024]{1,0:T(8,128)(2,1)S(1)} %convert_element_type.35), channel_id=1, source_target_pairs={{0,1},{1,2},{2,3},{3,0},{4,5},{5,6},{6,7},{7,4},{8,9},{9,10},{10,1... | collective-permute-start | bytes 1622024 | tf_op jit(solution)/shard_map/weight_far/ppermute | solution.py:35
  59.0 9.3 %collective-permute-start.7 = (bf16[256,1024]{1,0:T(8,128)(2,1)S(1)}, bf16[256,1024]{1,0:T(8,128)(2,1)S(1)}, u32[]{:S(2)}, u32[]{:S(2)}) collective-permute-start(bf16[256,1024]{1,0:T(8,128)(2,1)S(1)} %slice.65), channel_id=1, source_target_pairs={{0,12},{1,13},{2,14},{3,15},{4,0},{5,1},{6,2},{7,3},{8,4},{9,5},{1... | collective-permute-start | bytes 1572872 | tf_op jit(solution)/shard_map/rows_far/ppermute | solution.py:35
  59.7 14.8 %collective-permute-start.6 = (bf16[256,1024]{1,0:T(8,128)(2,1)S(1)}, bf16[256,1024]{1,0:T(8,128)(2,1)S(1)}, u32[]{:S(2)}, u32[]{:S(2)}) collective-permute-start(bf16[256,1024]{1,0:T(8,128)(2,1)S(1)} %slice.64), channel_id=1, source_target_pairs={{0,4},{1,5},{2,6},{3,7},{4,8},{5,9},{6,10},{7,11},{8,12},{9,13},{1... | collective-permute-start | bytes 1572872 | tf_op jit(solution)/shard_map/rows_far/ppermute | solution.py:35
  60.6 15.2 %collective-permute-start.11 = (f16[264,1024]{1,0:T(8,128)(2,1)S(1)}, f16[264,1024]{1,0:T(8,128)(2,1)S(1)}, u32[]{:S(2)}, u32[]{:S(2)}) collective-permute-start(f16[264,1024]{1,0:T(8,128)(2,1)S(1)} %convert_element_type.36), channel_id=1, source_target_pairs={{0,3},{1,0},{2,1},{3,2},{4,7},{5,4},{6,5},{7,6},{8,11},{9,8},{10,9... | collective-permute-start | bytes 1622024 | tf_op jit(solution)/shard_map/weight_far/ppermute | solution.py:35
  78.0 26.8 %collective-permute-start.10 = (f16[520,1024]{1,0:T(8,128)(2,1)}, f16[520,1024]{1,0:T(8,128)(2,1)}, u32[]{:S(2)}, u32[]{:S(2)}) collective-permute-start(f16[520,1024]{1,0:T(8,128)(2,1)} %pad_maximum_fusion.1), channel_id=1, source_target_pairs={{0,1},{1,2},{2,3},{3,0},{4,5},{5,6},{6,7},{7,4},{8,9},{9,10},{10,1... | collective-permute-start | bytes 3194888 | tf_op jit(solution)/shard_map/weight_near/ppermute | solution.py:35
  79.3 26.1 %collective-permute-start.12 = (f16[520,1024]{1,0:T(8,128)(2,1)}, f16[520,1024]{1,0:T(8,128)(2,1)}, u32[]{:S(2)}, u32[]{:S(2)}) collective-permute-start(f16[520,1024]{1,0:T(8,128)(2,1)} %pad_maximum_fusion.2), channel_id=1, source_target_pairs={{0,3},{1,0},{2,1},{3,2},{4,7},{5,4},{6,5},{7,6},{8,11},{9,8},{10,9... | collective-permute-start | bytes 3194888 | tf_op jit(solution)/shard_map/weight_near/ppermute | solution.py:35
  85.9 3.0 %copy-start.4 = (bf16[256,3072]{1,0:T(8,128)(2,1)S(1)}, bf16[256,3072]{1,0:T(8,128)(2,1)}, u32[]{:S(2)}) copy-start(bf16[256,3072]{1,0:T(8,128)(2,1)} %copy-done.3) | copy-start | bytes 4718596
  85.9 3.0 %copy-start.6 = (bf16[256,3072]{1,0:T(8,128)(2,1)S(1)}, bf16[256,3072]{1,0:T(8,128)(2,1)}, u32[]{:S(2)}) copy-start(bf16[256,3072]{1,0:T(8,128)(2,1)} %copy-done.5) | copy-start | bytes 4718596
  85.9 3.0 %copy-start.9 = (bf16[256,3072]{1,0:T(8,128)(2,1)S(1)}, bf16[256,3072]{1,0:T(8,128)(2,1)}, u32[]{:S(2)}) copy-start(bf16[256,3072]{1,0:T(8,128)(2,1)} %copy-done.7) | copy-start | bytes 4718596
  85.9 26.3 %collective-permute-start.14 = (bf16[256,2048]{1,0:T(8,128)(2,1)S(1)}, bf16[256,2048]{1,0:T(8,128)(2,1)S(1)}, u32[]{:S(2)}, u32[]{:S(2)}) collective-permute-start(bf16[256,2048]{1,0:T(8,128)(2,1)S(1)} %layer.6), channel_id=1, source_target_pairs={{0,2},{1,3},{2,0},{3,1},{4,6},{5,7},{6,4},{7,5},{8,10},{9,11},{10,... | collective-permute-start | bytes 3145736 | tf_op jit(solution)/shard_map/layer/from2/ppermute | solution.py:35
  86.0 30.6 %collective-permute-start.13 = (bf16[256,2048]{1,0:T(8,128)(2,1)S(1)}, bf16[256,2048]{1,0:T(8,128)(2,1)S(1)}, u32[]{:S(2)}, u32[]{:S(2)}) collective-permute-start(bf16[256,2048]{1,0:T(8,128)(2,1)S(1)} %layer.5), channel_id=1, source_target_pairs={{0,3},{1,0},{2,1},{3,2},{4,7},{5,4},{6,5},{7,6},{8,11},{9,8},{10,9... | collective-permute-start | bytes 3145736 | tf_op jit(solution)/shard_map/layer/from1/ppermute | solution.py:35
  87.2 29.4 %collective-permute-start.15 = (bf16[256,2048]{1,0:T(8,128)(2,1)S(1)}, bf16[256,2048]{1,0:T(8,128)(2,1)S(1)}, u32[]{:S(2)}, u32[]{:S(2)}) collective-permute-start(bf16[256,2048]{1,0:T(8,128)(2,1)S(1)} %layer.4), channel_id=1, source_target_pairs={{0,1},{1,2},{2,3},{3,0},{4,5},{5,6},{6,7},{7,4},{8,9},{9,10},{10,1... | collective-permute-start | bytes 3145736 | tf_op jit(solution)/shard_map/layer/from3/ppermute | solution.py:35
  88.8 1.4 %copy-start.11 = (bf16[256,3072]{1,0:T(8,128)(2,1)S(1)}, bf16[256,3072]{1,0:T(8,128)(2,1)}, u32[]{:S(2)}) copy-start(bf16[256,3072]{1,0:T(8,128)(2,1)} %copy-done.10) | copy-start | bytes 4718596

commit v6 on v5

--- a/solution.py
+++ b/solution.py
@@ -328,8 +328,7 @@
         weight_grad = total * (mask.astype(jnp.float32) * grad_scale)
     with jax.named_scope("join"):
         grads = after(grads, weight_grad)
-        input_grad = join_columns(place, grads, (0, 2))
-        input_grad = join_columns(place, grads, (1, 3), input_grad)
+        input_grad = join_columns(place, grads, (0, 1, 2, 3))
     return (weight_grad[None], input_grad[None])
 
 

time: 122 us -> 121 us (level)
    pallas_call x12 -> x11, Pallas kernels: 17.2 us -> 16 us  [local_call(): pl.pallas_call(kernel, out_shape=out_shape, in_specs=in_specs, out_specs=...]
where the time goes in v6:
time: 121 us; the launch traced here: 119 us
  waiting for transfers between devices  62.8 us (52%)
  starting transfers between devices  22.7 us (19%)
  Pallas kernels  16 us (13%)
  other arithmetic  10.6 us (9%)
  local copies, waits for them, and re-layouts  6.13 us (5%)
    ppermute x14, waiting for transfers between devices, move(): return lax.ppermute(value, ('section', 'dp'), pairs)  47.4 us
    pallas_call x11, Pallas kernels, local_call(): pl.pallas_call(kernel, out_shape=out_shape, in_specs=in_specs, out_specs=...  16 us
    ppermute x14, starting transfers between devices, move(): return lax.ppermute(value, ('section', 'dp'), pairs)  15.9 us
    ppermute x2, waiting for transfers between devices, to_layer_below(): return lax.ppermute(value, 'section', [(s, s - 1) for s in range(1, count)])  15.4 us
    ppermute x2, starting transfers between devices, to_layer_below(): return lax.ppermute(value, 'section', [(s, s - 1) for s in range(1, count)])  6.73 us
    unnamed x26, local copies, waits for them, and re-layouts  5.91 us
    add x2, other arithmetic, shards(): total = lax.optimization_barrier(total + decoded(value))  3.42 us
    concatenate x2, other arithmetic, combined(): return jnp.concatenate([top, bottom, tail], 0).astype(jnp.float16)  2.65 us
  transfers between devices with their start and end apart: 16, of which 10 were waited for; matrix products, arithmetic and copies ran while one was open for 7% of the time, Pallas kernels for 10%

profile of v6, /device:TPU:1, one launch (start us, length us, event | category | flops | bytes accessed | tf_op | source)
XLA Modules:
  0.0 119.4 jit_solution(2094084335912621108)
XLA Ops:
  0.7 2.2 %copy-done = bf16[1,256,8192]{2,1,0:T(8,128)(2,1)S(1)} copy-done((bf16[1,256,8192]{2,1,0:T(8,128)(2,1)S(1)}, bf16[1,256,8192]{2,1,0:T(8,128)(2,1)}, u32[]{:S(2)}) %copy-start) | copy-done | bytes 4194328
  4.0 1.3 %shard_map.59 = (bf16[256,3072]{1,0:T(8,128)(2,1)S(1)}, bf16[256,3072]{1,0:T(8,128)(2,1)S(1)}, bf16[256,3072]{1,0:T(8,128)(2,1)S(1)}, bf16[256,3072]{1,0:T(8,128)(2,1)S(1)}) custom-call(s32[4]{0:T(128)S(1)} %broadcast_select_fusion.place_ref, bf16[256,1024]{1,0:T(8,128)(2,1)S(1)} %bitcast.19, bf16[256,8192]{1,0:T(8,128)(2,1)S(1)} %bitcast.17), custom_call_target="tpu_custom_call" | custom-call | tf_op jit(solution)/shard_map/pallas_call | solution.py:159
  5.2 3.6 %collective-permute-start = (bf16[256,3072]{1,0:T(8,128)(2,1)S(1)}, bf16[256,3072]{1,0:T(8,128)(2,1)S(1)}, u32[]{:S(2)}, u32[]{:S(2)}) collective-permute-start(bf16[256,3072]{1,0:T(8,128)(2,1)S(1)} %get-tuple-element.44), channel_id=1, source_target_pairs={{0,12},{1,13},{2,14},{3,15},{4,0},{5,1},{6,2},{7,3},{8,4},{9,5},{1... | collective-permute-start | bytes 4718600 | tf_op jit(solution)/shard_map/ins/from1/ppermute | solution.py:35
  11.1 3.3 %collective-permute-start.3 = (bf16[512,1024]{1,0:T(8,128)(2,1)S(1)}, bf16[512,1024]{1,0:T(8,128)(2,1)S(1)}, u32[]{:S(2)}, u32[]{:S(2)}) collective-permute-start(bf16[512,1024]{1,0:T(8,128)(2,1)S(1)} %get-tuple-element.58), channel_id=1, source_target_pairs={{16,0},{32,16},{48,32},{64,48},{80,64},{96,80},{112,96},{128,112},... | collective-permute-start | bytes 3145736 | tf_op jit(solution)/shard_map/rows_below/ppermute | solution.py:40
  14.4 14.2 %collective-permute-done.3.refs_0_ = bf16[512,1024]{1,0:T(8,128)(2,1)S(1)} collective-permute-done((bf16[512,1024]{1,0:T(8,128)(2,1)S(1)}, bf16[512,1024]{1,0:T(8,128)(2,1)S(1)}, u32[]{:S(2)}, u32[]{:S(2)}) %collective-permute-start.3) | collective-permute-done | bytes 1048608 | tf_op jit(solution)/shard_map/rows_below/ppermute | solution.py:40
  28.6 2.7 %collective-permute-start.5 = (bf16[512,1024]{1,0:T(8,128)(2,1)S(1)}, bf16[512,1024]{1,0:T(8,128)(2,1)S(1)}, u32[]{:S(2)}, u32[]{:S(2)}) collective-permute-start(bf16[512,1024]{1,0:T(8,128)(2,1)S(1)} %collective-permute-done.3.refs_0_), channel_id=1, source_target_pairs={{0,12},{1,13},{2,14},{3,15},{4,0},{5,1},{6,2},{7,3},{8,4},{9,5},{1... | collective-permute-start | bytes 3145736 | tf_op jit(solution)/shard_map/rows/ppermute | solution.py:35
  31.4 11.7 %collective-permute-done.refs_1_ = bf16[256,3072]{1,0:T(8,128)(2,1)S(1)} collective-permute-done((bf16[256,3072]{1,0:T(8,128)(2,1)S(1)}, bf16[256,3072]{1,0:T(8,128)(2,1)S(1)}, u32[]{:S(2)}, u32[]{:S(2)}) %collective-permute-start) | collective-permute-done | bytes 1572896 | tf_op jit(solution)/shard_map/ins/from1/ppermute | solution.py:35
  43.2 3.6 %collective-permute-done.2.refs_3_ = bf16[256,3072]{1,0:T(8,128)(2,1)S(1)} collective-permute-done((bf16[256,3072]{1,0:T(8,128)(2,1)S(1)}, bf16[256,3072]{1,0:T(8,128)(2,1)S(1)}, u32[]{:S(2)}, u32[]{:S(2)}) %collective-permute-start.2) | collective-permute-done | bytes 1572896 | tf_op jit(solution)/shard_map/ins/from3/ppermute | solution.py:35
  47.0 3.5 %collective-permute-start.8 = (bf16[1024,1024]{1,0:T(8,128)(2,1)S(1)}, bf16[1024,1024]{1,0:T(8,128)(2,1)S(1)}, u32[]{:S(2)}, u32[]{:S(2)}) collective-permute-start(bf16[1024,1024]{1,0:T(8,128)(2,1)S(1)} %pad_maximum_fusion.refs_4_), channel_id=1, source_target_pairs={{16,0},{32,16},{48,32},{64,48},{80,64},{96,80},{112,96},{128,112},... | collective-permute-start | bytes 6291464 | tf_op jit(solution)/shard_map/cots_below/ppermute | solution.py:40
  50.5 1.5 %weight.4 = (f32[264,1024]{1,0:T(8,128)S(1)}, f32[264,1024]{1,0:T(8,128)S(1)}) custom-call(bf16[256,3072]{1,0:T(8,128)(2,1)S(1)} %get-tuple-element.68.refs_0_, bf16[256,3072]{1,0:T(8,128)(2,1)S(1)} %collective-permute-done.refs_1_, bf16[256,3072]{1,0:T(8,128)(2,1)S(1)} %collective-permute-done.1.refs_2_, ...), custom_call_target="tpu_custom_call" | custom-call | flops 8589934592 | tf_op jit(solution)/shard_map/weight/pallas_call | solution.py:159
  52.2 1.2 %copy-done.8 = bf16[256,3072]{1,0:T(8,128)(2,1)S(1)} copy-done((bf16[256,3072]{1,0:T(8,128)(2,1)S(1)}, bf16[256,3072]{1,0:T(8,128)(2,1)}, u32[]{:S(2)}) %copy-start.8) | copy-done | bytes 1572888
  53.5 1.5 %weight.5 = f32[520,1024]{1,0:T(8,128)S(1)} custom-call(bf16[256,3072]{1,0:T(8,128)(2,1)S(1)} %get-tuple-element.68.refs_0_, bf16[256,3072]{1,0:T(8,128)(2,1)S(1)} %collective-permute-done.refs_1_, bf16[256,3072]{1,0:T(8,128)(2,1)S(1)} %copy-done.8, bf16[256,3072]{1,0:T(8,128)(2,1)S(1)} %collective-permute-done.2.refs_3_, ...), custom_call_target="tpu_custom_call" | custom-call | flops 8589934592 | tf_op jit(solution)/shard_map/weight/pallas_call | solution.py:159
  55.0 1.5 %weight.6 = f32[520,1024]{1,0:T(8,128)S(1)} custom-call(bf16[256,3072]{1,0:T(8,128)(2,1)S(1)} %get-tuple-element.68.refs_0_, bf16[256,3072]{1,0:T(8,128)(2,1)S(1)} %collective-permute-done.refs_1_, bf16[256,3072]{1,0:T(8,128)(2,1)S(1)} %copy-done.8, bf16[256,3072]{1,0:T(8,128)(2,1)S(1)} %collective-permute-done.2.refs_3_, ...), custom_call_target="tpu_custom_call" | custom-call | flops 8589934592 | tf_op jit(solution)/shard_map/weight/pallas_call | solution.py:159
  56.5 1.5 %collective-permute-done.4.refs_4_ = bf16[512,1024]{1,0:T(8,128)(2,1)S(1)} collective-permute-done((bf16[512,1024]{1,0:T(8,128)(2,1)S(1)}, bf16[512,1024]{1,0:T(8,128)(2,1)S(1)}, u32[]{:S(2)}, u32[]{:S(2)}) %collective-permute-start.4) | collective-permute-done | bytes 1048608 | tf_op jit(solution)/shard_map/rows/ppermute | solution.py:35
  60.6 1.8 %collective-permute-start.11 = (f16[264,1024]{1,0:T(8,128)(2,1)S(1)}, f16[264,1024]{1,0:T(8,128)(2,1)S(1)}, u32[]{:S(2)}, u32[]{:S(2)}) collective-permute-start(f16[264,1024]{1,0:T(8,128)(2,1)S(1)} %convert_element_type.36), channel_id=1, source_target_pairs={{0,3},{1,0},{2,1},{3,2},{4,7},{5,4},{6,5},{7,6},{8,11},{9,8},{10,9... | collective-permute-start | bytes 1622024 | tf_op jit(solution)/shard_map/weight_far/ppermute | solution.py:35
  62.3 6.0 %collective-permute-done.7.refs_3_ = bf16[256,1024]{1,0:T(8,128)(2,1)S(1)} collective-permute-done((bf16[256,1024]{1,0:T(8,128)(2,1)S(1)}, bf16[256,1024]{1,0:T(8,128)(2,1)S(1)}, u32[]{:S(2)}, u32[]{:S(2)}) %collective-permute-start.7) | collective-permute-done | bytes 524320 | tf_op jit(solution)/shard_map/rows_far/ppermute | solution.py:35
  68.3 6.3 %collective-permute-done.6.refs_2_ = bf16[256,1024]{1,0:T(8,128)(2,1)S(1)} collective-permute-done((bf16[256,1024]{1,0:T(8,128)(2,1)S(1)}, bf16[256,1024]{1,0:T(8,128)(2,1)S(1)}, u32[]{:S(2)}, u32[]{:S(2)}) %collective-permute-start.6) | collective-permute-done | bytes 524320 | tf_op jit(solution)/shard_map/rows_far/ppermute | solution.py:35
  76.6 1.4 %pad_maximum_fusion.1 = f16[520,1024]{1,0:T(8,128)(2,1)} fusion(f16[8,1024]{1,0:T(8,128)(2,1)S(1)} %broadcast_in_dim.21, f16[256,1024]{1,0:T(8,128)(2,1)S(1)} %get-tuple-element.92, f16[256,1024]{1,0:T(8,128)(2,1)S(1)} %get-tuple-element.93), kind=kLoop, calls=%fused_computation.4 | loop fusion | flops 1064960 | bytes 2129920 | tf_op jit(solution)/shard_map/weight_near/concatenate | solution.py:263
  78.0 1.3 %pad_maximum_fusion.2 = f16[520,1024]{1,0:T(8,128)(2,1)} fusion(f16[8,1024]{1,0:T(8,128)(2,1)S(1)} %broadcast_in_dim.23, f16[256,1024]{1,0:T(8,128)(2,1)S(1)} %get-tuple-element.89, f16[256,1024]{1,0:T(8,128)(2,1)S(1)} %get-tuple-element.88), kind=kLoop, calls=%fused_computation.5 | loop fusion | flops 1064960 | bytes 2129920 | tf_op jit(solution)/shard_map/weight_near/concatenate | solution.py:263
  79.3 2.7 %collective-permute-start.12 = (f16[520,1024]{1,0:T(8,128)(2,1)}, f16[520,1024]{1,0:T(8,128)(2,1)}, u32[]{:S(2)}, u32[]{:S(2)}) collective-permute-start(f16[520,1024]{1,0:T(8,128)(2,1)} %pad_maximum_fusion.2), channel_id=1, source_target_pairs={{0,3},{1,0},{2,1},{3,2},{4,7},{5,4},{6,5},{7,6},{8,11},{9,8},{10,9... | collective-permute-start | bytes 3194888 | tf_op jit(solution)/shard_map/weight_near/ppermute | solution.py:35
  82.0 1.3 %layer.4 = bf16[256,2048]{1,0:T(8,128)(2,1)S(1)} custom-call(bf16[1024,1024]{1,0:T(8,128)(2,1)S(1)} %collective-permute-done.8.cots_ref, bf16[512,1024]{1,0:T(8,128)(2,1)S(1)} %collective-permute-done.3.refs_0_, bf16[512,1024]{1,0:T(8,128)(2,1)S(1)} %collective-permute-done.5.refs_1_, bf16[256,1024]{1,0:T(8,128)(2,1)S(1)} %collective-permute-done.6.refs_2_, ...), custom_call_target="tpu_custom_call" | custom-call | tf_op jit(solution)/shard_map/layer/pallas_call | solution.py:159
  83.3 1.3 %layer.5 = bf16[256,2048]{1,0:T(8,128)(2,1)S(1)} custom-call(bf16[1024,1024]{1,0:T(8,128)(2,1)S(1)} %collective-permute-done.8.cots_ref, bf16[512,1024]{1,0:T(8,128)(2,1)S(1)} %collective-permute-done.3.refs_0_, bf16[512,1024]{1,0:T(8,128)(2,1)S(1)} %collective-permute-done.5.refs_1_, bf16[256,1024]{1,0:T(8,128)(2,1)S(1)} %collective-permute-done.6.refs_2_, ...), custom_call_target="tpu_custom_call" | custom-call | tf_op jit(solution)/shard_map/layer/pallas_call | solution.py:159
  84.6 1.3 %layer.6 = bf16[256,2048]{1,0:T(8,128)(2,1)S(1)} custom-call(bf16[1024,1024]{1,0:T(8,128)(2,1)S(1)} %collective-permute-done.8.cots_ref, bf16[512,1024]{1,0:T(8,128)(2,1)S(1)} %collective-permute-done.3.refs_0_, bf16[512,1024]{1,0:T(8,128)(2,1)S(1)} %collective-permute-done.5.refs_1_, bf16[256,1024]{1,0:T(8,128)(2,1)S(1)} %collective-permute-done.6.refs_2_, ...), custom_call_target="tpu_custom_call" | custom-call | tf_op jit(solution)/shard_map/layer/pallas_call | solution.py:159
  87.5 1.3 %layer.7.refs_0_ = bf16[256,2048]{1,0:T(8,128)(2,1)S(1)} custom-call(bf16[1024,1024]{1,0:T(8,128)(2,1)S(1)} %collective-permute-done.8.cots_ref, bf16[512,1024]{1,0:T(8,128)(2,1)S(1)} %collective-permute-done.3.refs_0_, bf16[512,1024]{1,0:T(8,128)(2,1)S(1)} %collective-permute-done.5.refs_1_, bf16[256,1024]{1,0:T(8,128)(2,1)S(1)} %collective-permute-done.6.refs_2_, ...), custom_call_target="tpu_custom_call" | custom-call | tf_op jit(solution)/shard_map/layer/pallas_call | solution.py:159
  88.9 1.4 %copy-done.11 = bf16[256,3072]{1,0:T(8,128)(2,1)S(1)} copy-done((bf16[256,3072]{1,0:T(8,128)(2,1)S(1)}, bf16[256,3072]{1,0:T(8,128)(2,1)}, u32[]{:S(2)}) %copy-start.11) | copy-done | bytes 1572888
  90.3 1.3 %weight.7 = f32[512,1024]{1,0:T(8,128)S(1)} custom-call(bf16[256,3072]{1,0:T(8,128)(2,1)S(1)} %copy-done.4, bf16[256,3072]{1,0:T(8,128)(2,1)S(1)} %copy-done.6, bf16[256,3072]{1,0:T(8,128)(2,1)S(1)} %copy-done.9, bf16[256,3072]{1,0:T(8,128)(2,1)S(1)} %copy-done.11, bf16[1024,1024]{1,0:T(8,128)(2,1)S(1)} %pad_maximum_fusion.refs_4_), custom_call_target="tpu_custom_call" | custom-call | flops 8589934592 | tf_op jit(solution)/shard_map/weight/pallas_call | solution.py:159
  91.5 13.2 %collective-permute-done.10 = f16[520,1024]{1,0:T(8,128)(2,1)} collective-permute-done((f16[520,1024]{1,0:T(8,128)(2,1)}, f16[520,1024]{1,0:T(8,128)(2,1)}, u32[]{:S(2)}, u32[]{:S(2)}) %collective-permute-start.10) | collective-permute-done | bytes 1064992 | tf_op jit(solution)/shard_map/weight_near/ppermute | solution.py:35
  106.2 1.7 %multiply_add_fusion.1 = f32[512,1024]{1,0:T(8,128)S(1)} fusion(f32[512,1024]{1,0:T(8,128)S(1)} %weight.7, f32[1024]{0:T(1024)S(1)} %bitcast.27, f16[520,1024]{1,0:T(8,128)(2,1)} %collective-permute-done.10), kind=kLoop, calls=%fused_computation.3 | loop fusion | flops 1572864 | bytes 5246976 | tf_op jit(solution)/shard_map/weight/add | solution.py:326
  108.6 1.7 %multiply_add_fusion = f32[512,1024]{1,0:T(8,128)S(1)} fusion(f32[512,1024]{1,0:T(8,128)S(1)} %multiply_add_fusion.1, f32[1024]{0:T(1024)S(1)} %bitcast.28, f16[520,1024]{1,0:T(8,128)(2,1)} %collective-permute-done.12), kind=kLoop, calls=%fused_computation.2 | loop fusion | flops 1572864 | bytes 5246976 | tf_op jit(solution)/shard_map/weight/add | solution.py:326
  110.4 1.8 %multiply_multiply_fusion = f32[512,1024]{1,0:T(8,128)} fusion(f32[512,1024]{1,0:T(8,128)S(1)} %multiply_add_fusion, bf16[512,1024]{1,0:T(8,128)(2,1)S(1)} %get-tuple-element.79), kind=kLoop, calls=%fused_computation.1 | loop fusion | flops 1572864 | bytes 5242880 | tf_op jit(solution)/shard_map/weight/mul | solution.py:328
  112.2 4.4 %collective-permute-done.13.refs_1_ = bf16[256,2048]{1,0:T(8,128)(2,1)S(1)} collective-permute-done((bf16[256,2048]{1,0:T(8,128)(2,1)S(1)}, bf16[256,2048]{1,0:T(8,128)(2,1)S(1)}, u32[]{:S(2)}, u32[]{:S(2)}) %collective-permute-start.13) | collective-permute-done | bytes 1048608 | tf_op jit(solution)/shard_map/layer/from1/ppermute | solution.py:35
  116.6 2.7 %join.1 = bf16[256,8192]{1,0:T(8,128)(2,1)} custom-call(s32[4]{0:T(128)S(1)} %broadcast_select_fusion.place_ref, bf16[256,2048]{1,0:T(8,128)(2,1)S(1)} %layer.7.refs_0_, bf16[256,2048]{1,0:T(8,128)(2,1)S(1)} %collective-permute-done.13.refs_1_, bf16[256,2048]{1,0:T(8,128)(2,1)S(1)} %collective-permute-done.14.refs_2_, ...), custom_call_target="tpu_custom_call" | custom-call | tf_op jit(solution)/shard_map/join/pallas_call | solution.py:159
  (63 shorter events, 12.2 us)
Async XLA Ops:
  0.7 2.2 %copy-start = (bf16[1,256,8192]{2,1,0:T(8,128)(2,1)S(1)}, bf16[1,256,8192]{2,1,0:T(8,128)(2,1)}, u32[]{:S(2)}) copy-start(bf16[1,256,8192]{2,1,0:T(8,128)(2,1)} %param.4) | copy-start | bytes 12582916
  2.9 1.0 copy-start.2
  4.0 6.0 %copy-start.1 = (bf16[1,512,1024]{2,1,0:T(8,128)(2,1)S(1)}, bf16[1,512,1024]{2,1,0:T(8,128)(2,1)}, u32[]{:S(2)}) copy-start(bf16[1,512,1024]{2,1,0:T(8,128)(2,1)} %param.6) | copy-start | bytes 3145732
  4.0 6.0 %copy-start.12 = (s32[1,128,16]{1,2,0:T(8,128)S(1)}, s32[1,128,16]{1,2,0:T(8,128)}, u32[]{:S(2)}) copy-start(s32[1,128,16]{1,2,0:T(8,128)} %param.7) | copy-start | bytes 24580
  5.2 49.7 %copy-start.3 = (bf16[256,3072]{1,0:T(8,128)(2,1)}, bf16[256,3072]{1,0:T(8,128)(2,1)S(1)}, u32[]{:S(2)}) copy-start(bf16[256,3072]{1,0:T(8,128)(2,1)S(1)} %get-tuple-element.68.refs_0_) | copy-start | bytes 4718596
  5.2 37.9 %collective-permute-start = (bf16[256,3072]{1,0:T(8,128)(2,1)S(1)}, bf16[256,3072]{1,0:T(8,128)(2,1)S(1)}, u32[]{:S(2)}, u32[]{:S(2)}) collective-permute-start(bf16[256,3072]{1,0:T(8,128)(2,1)S(1)} %get-tuple-element.44), channel_id=1, source_target_pairs={{0,12},{1,13},{2,14},{3,15},{4,0},{5,1},{6,2},{7,3},{8,4},{9,5},{1... | collective-permute-start | bytes 4718600 | tf_op jit(solution)/shard_map/ins/from1/ppermute | solution.py:35
  8.9 34.3 %collective-permute-start.1 = (bf16[256,3072]{1,0:T(8,128)(2,1)S(1)}, bf16[256,3072]{1,0:T(8,128)(2,1)S(1)}, u32[]{:S(2)}, u32[]{:S(2)}) collective-permute-start(bf16[256,3072]{1,0:T(8,128)(2,1)S(1)} %get-tuple-element.45), channel_id=1, source_target_pairs={{0,8},{1,9},{2,10},{3,11},{4,12},{5,13},{6,14},{7,15},{8,0},{9,1},... | collective-permute-start | bytes 4718600 | tf_op jit(solution)/shard_map/ins/from2/ppermute | solution.py:35
  9.2 37.6 %collective-permute-start.2 = (bf16[256,3072]{1,0:T(8,128)(2,1)S(1)}, bf16[256,3072]{1,0:T(8,128)(2,1)S(1)}, u32[]{:S(2)}, u32[]{:S(2)}) collective-permute-start(bf16[256,3072]{1,0:T(8,128)(2,1)S(1)} %get-tuple-element.46), channel_id=1, source_target_pairs={{0,4},{1,5},{2,6},{3,7},{4,8},{5,9},{6,10},{7,11},{8,12},{9,13},{1... | collective-permute-start | bytes 4718600 | tf_op jit(solution)/shard_map/ins/from3/ppermute | solution.py:35
  11.1 17.5 %collective-permute-start.3 = (bf16[512,1024]{1,0:T(8,128)(2,1)S(1)}, bf16[512,1024]{1,0:T(8,128)(2,1)S(1)}, u32[]{:S(2)}, u32[]{:S(2)}) collective-permute-start(bf16[512,1024]{1,0:T(8,128)(2,1)S(1)} %get-tuple-element.58), channel_id=1, source_target_pairs={{16,0},{32,16},{48,32},{64,48},{80,64},{96,80},{112,96},{128,112},... | collective-permute-start | bytes 3145736 | tf_op jit(solution)/shard_map/rows_below/ppermute | solution.py:40
  28.6 27.9 %collective-permute-start.5 = (bf16[512,1024]{1,0:T(8,128)(2,1)S(1)}, bf16[512,1024]{1,0:T(8,128)(2,1)S(1)}, u32[]{:S(2)}, u32[]{:S(2)}) collective-permute-start(bf16[512,1024]{1,0:T(8,128)(2,1)S(1)} %collective-permute-done.3.refs_0_), channel_id=1, source_target_pairs={{0,12},{1,13},{2,14},{3,15},{4,0},{5,1},{6,2},{7,3},{8,4},{9,5},{1... | collective-permute-start | bytes 3145736 | tf_op jit(solution)/shard_map/rows/ppermute | solution.py:35
  31.4 26.7 %collective-permute-start.4 = (bf16[512,1024]{1,0:T(8,128)(2,1)S(1)}, bf16[512,1024]{1,0:T(8,128)(2,1)S(1)}, u32[]{:S(2)}, u32[]{:S(2)}) collective-permute-start(bf16[512,1024]{1,0:T(8,128)(2,1)S(1)} %collective-permute-done.3.refs_0_), channel_id=1, source_target_pairs={{0,4},{1,5},{2,6},{3,7},{4,8},{5,9},{6,10},{7,11},{8,12},{9,13},{1... | collective-permute-start | bytes 3145736 | tf_op jit(solution)/shard_map/rows/ppermute | solution.py:35
  43.1 11.9 %copy-start.5 = (bf16[256,3072]{1,0:T(8,128)(2,1)}, bf16[256,3072]{1,0:T(8,128)(2,1)S(1)}, u32[]{:S(2)}) copy-start(bf16[256,3072]{1,0:T(8,128)(2,1)S(1)} %collective-permute-done.refs_1_) | copy-start | bytes 4718596
  43.2 7.4 %copy-start.7 = (bf16[256,3072]{1,0:T(8,128)(2,1)}, bf16[256,3072]{1,0:T(8,128)(2,1)S(1)}, u32[]{:S(2)}) copy-start(bf16[256,3072]{1,0:T(8,128)(2,1)S(1)} %collective-permute-done.1.refs_2_) | copy-start | bytes 4718596
  46.8 8.2 %copy-start.10 = (bf16[256,3072]{1,0:T(8,128)(2,1)}, bf16[256,3072]{1,0:T(8,128)(2,1)S(1)}, u32[]{:S(2)}) copy-start(bf16[256,3072]{1,0:T(8,128)(2,1)S(1)} %collective-permute-done.2.refs_3_) | copy-start | bytes 4718596
  47.0 28.7 %collective-permute-start.8 = (bf16[1024,1024]{1,0:T(8,128)(2,1)S(1)}, bf16[1024,1024]{1,0:T(8,128)(2,1)S(1)}, u32[]{:S(2)}, u32[]{:S(2)}) collective-permute-start(bf16[1024,1024]{1,0:T(8,128)(2,1)S(1)} %pad_maximum_fusion.refs_4_), channel_id=1, source_target_pairs={{16,0},{32,16},{48,32},{64,48},{80,64},{96,80},{112,96},{128,112},... | collective-permute-start | bytes 6291464 | tf_op jit(solution)/shard_map/cots_below/ppermute | solution.py:40
  52.0 1.4 %copy-start.8 = (bf16[256,3072]{1,0:T(8,128)(2,1)S(1)}, bf16[256,3072]{1,0:T(8,128)(2,1)}, u32[]{:S(2)}) copy-start(bf16[256,3072]{1,0:T(8,128)(2,1)} %copy-done.7) | copy-start | bytes 4718596
  58.0 17.7 %collective-permute-start.9 = (f16[264,1024]{1,0:T(8,128)(2,1)S(1)}, f16[264,1024]{1,0:T(8,128)(2,1)S(1)}, u32[]{:S(2)}, u32[]{:S(2)}) collective-permute-start(f16[264,1024]{1,0:T(8,128)(2,1)S(1)} %convert_element_type.35), channel_id=1, source_target_pairs={{0,1},{1,2},{2,3},{3,0},{4,5},{5,6},{6,7},{7,4},{8,9},{9,10},{10,1... | collective-permute-start | bytes 1622024 | tf_op jit(solution)/shard_map/weight_far/ppermute | solution.py:35
  59.0 9.3 %collective-permute-start.7 = (bf16[256,1024]{1,0:T(8,128)(2,1)S(1)}, bf16[256,1024]{1,0:T(8,128)(2,1)S(1)}, u32[]{:S(2)}, u32[]{:S(2)}) collective-permute-start(bf16[256,1024]{1,0:T(8,128)(2,1)S(1)} %slice.65), channel_id=1, source_target_pairs={{0,12},{1,13},{2,14},{3,15},{4,0},{5,1},{6,2},{7,3},{8,4},{9,5},{1... | collective-permute-start | bytes 1572872 | tf_op jit(solution)/shard_map/rows_far/ppermute | solution.py:35
  59.7 14.8 %collective-permute-start.6 = (bf16[256,1024]{1,0:T(8,128)(2,1)S(1)}, bf16[256,1024]{1,0:T(8,128)(2,1)S(1)}, u32[]{:S(2)}, u32[]{:S(2)}) collective-permute-start(bf16[256,1024]{1,0:T(8,128)(2,1)S(1)} %slice.64), channel_id=1, source_target_pairs={{0,4},{1,5},{2,6},{3,7},{4,8},{5,9},{6,10},{7,11},{8,12},{9,13},{1... | collective-permute-start | bytes 1572872 | tf_op jit(solution)/shard_map/rows_far/ppermute | solution.py:35
  60.6 15.2 %collective-permute-start.11 = (f16[264,1024]{1,0:T(8,128)(2,1)S(1)}, f16[264,1024]{1,0:T(8,128)(2,1)S(1)}, u32[]{:S(2)}, u32[]{:S(2)}) collective-permute-start(f16[264,1024]{1,0:T(8,128)(2,1)S(1)} %convert_element_type.36), channel_id=1, source_target_pairs={{0,3},{1,0},{2,1},{3,2},{4,7},{5,4},{6,5},{7,6},{8,11},{9,8},{10,9... | collective-permute-start | bytes 1622024 | tf_op jit(solution)/shard_map/weight_far/ppermute | solution.py:35
  78.0 26.8 %collective-permute-start.10 = (f16[520,1024]{1,0:T(8,128)(2,1)}, f16[520,1024]{1,0:T(8,128)(2,1)}, u32[]{:S(2)}, u32[]{:S(2)}) collective-permute-start(f16[520,1024]{1,0:T(8,128)(2,1)} %pad_maximum_fusion.1), channel_id=1, source_target_pairs={{0,1},{1,2},{2,3},{3,0},{4,5},{5,6},{6,7},{7,4},{8,9},{9,10},{10,1... | collective-permute-start | bytes 3194888 | tf_op jit(solution)/shard_map/weight_near/ppermute | solution.py:35
  79.3 26.1 %collective-permute-start.12 = (f16[520,1024]{1,0:T(8,128)(2,1)}, f16[520,1024]{1,0:T(8,128)(2,1)}, u32[]{:S(2)}, u32[]{:S(2)}) collective-permute-start(f16[520,1024]{1,0:T(8,128)(2,1)} %pad_maximum_fusion.2), channel_id=1, source_target_pairs={{0,3},{1,0},{2,1},{3,2},{4,7},{5,4},{6,5},{7,6},{8,11},{9,8},{10,9... | collective-permute-start | bytes 3194888 | tf_op jit(solution)/shard_map/weight_near/ppermute | solution.py:35
  85.9 3.0 %copy-start.4 = (bf16[256,3072]{1,0:T(8,128)(2,1)S(1)}, bf16[256,3072]{1,0:T(8,128)(2,1)}, u32[]{:S(2)}) copy-start(bf16[256,3072]{1,0:T(8,128)(2,1)} %copy-done.3) | copy-start | bytes 4718596
  85.9 3.0 %copy-start.6 = (bf16[256,3072]{1,0:T(8,128)(2,1)S(1)}, bf16[256,3072]{1,0:T(8,128)(2,1)}, u32[]{:S(2)}) copy-start(bf16[256,3072]{1,0:T(8,128)(2,1)} %copy-done.5) | copy-start | bytes 4718596
  85.9 3.0 %copy-start.9 = (bf16[256,3072]{1,0:T(8,128)(2,1)S(1)}, bf16[256,3072]{1,0:T(8,128)(2,1)}, u32[]{:S(2)}) copy-start(bf16[256,3072]{1,0:T(8,128)(2,1)} %copy-done.7) | copy-start | bytes 4718596
  85.9 26.3 %collective-permute-start.14 = (bf16[256,2048]{1,0:T(8,128)(2,1)S(1)}, bf16[256,2048]{1,0:T(8,128)(2,1)S(1)}, u32[]{:S(2)}, u32[]{:S(2)}) collective-permute-start(bf16[256,2048]{1,0:T(8,128)(2,1)S(1)} %layer.6), channel_id=1, source_target_pairs={{0,2},{1,3},{2,0},{3,1},{4,6},{5,7},{6,4},{7,5},{8,10},{9,11},{10,... | collective-permute-start | bytes 3145736 | tf_op jit(solution)/shard_map/layer/from2/ppermute | solution.py:35
  86.0 30.6 %collective-permute-start.13 = (bf16[256,2048]{1,0:T(8,128)(2,1)S(1)}, bf16[256,2048]{1,0:T(8,128)(2,1)S(1)}, u32[]{:S(2)}, u32[]{:S(2)}) collective-permute-start(bf16[256,2048]{1,0:T(8,128)(2,1)S(1)} %layer.5), channel_id=1, source_target_pairs={{0,3},{1,0},{2,1},{3,2},{4,7},{5,4},{6,5},{7,6},{8,11},{9,8},{10,9... | collective-permute-start | bytes 3145736 | tf_op jit(solution)/shard_map/layer/from1/ppermute | solution.py:35
  87.2 29.4 %collective-permute-start.15 = (bf16[256,2048]{1,0:T(8,128)(2,1)S(1)}, bf16[256,2048]{1,0:T(8,128)(2,1)S(1)}, u32[]{:S(2)}, u32[]{:S(2)}) collective-permute-start(bf16[256,2048]{1,0:T(8,128)(2,1)S(1)} %layer.4), channel_id=1, source_target_pairs={{0,1},{1,2},{2,3},{3,0},{4,5},{5,6},{6,7},{7,4},{8,9},{9,10},{10,1... | collective-permute-start | bytes 3145736 | tf_op jit(solution)/shard_map/layer/from3/ppermute | solution.py:35
  88.8 1.4 %copy-start.11 = (bf16[256,3072]{1,0:T(8,128)(2,1)S(1)}, bf16[256,3072]{1,0:T(8,128)(2,1)}, u32[]{:S(2)}) copy-start(bf16[256,3072]{1,0:T(8,128)(2,1)} %copy-done.10) | copy-start | bytes 4718596
